TPU v7x, 32 devices: a whole 2x2x4 slice. The times are simulated.
32 devices in a mesh: dp: 32 (over z, y, x, core).
Axes of the slice: x: 2, y: 2, z: 4, core: 2. Of those that a mesh axis runs over, the one named last changes fastest.
Arguments:
- tokens: bfloat16 [32768, 576], P('dp'), may hold values from -6 to 6
- cotangent: bfloat16 [32768, 576], P('dp'), may hold values from -16 to 16, as said below
- w_query: bfloat16 [331776], P('dp'), may hold values from -0.25 to 0.25
- w_key: bfloat16 [110592], P('dp'), may hold values from -0.25 to 0.25
- w_value: bfloat16 [110592], P('dp'), may hold values from -0.25 to 0.25
- w_out: bfloat16 [331776], P('dp'), may hold values from -2 to 2
- w_gate: bfloat16 [884736], P('dp'), may hold values from -0.25 to 0.25
- w_up: bfloat16 [884736], P('dp'), may hold values from -0.25 to 0.25
- w_down: bfloat16 [884736], P('dp'), may hold values from -0.15625 to 0.15625
- norm_gains: bfloat16 [2, 576], replicated, may hold values from 0.5 to 1.5
Outputs:
- output: bfloat16 [32768, 576], P('dp')
- input_grad: bfloat16 [32768, 576], P('dp')
- query_grad: float32 [331776], P('dp')
- key_grad: float32 [110592], P('dp')
- value_grad: float32 [110592], P('dp')
- out_grad: float32 [331776], P('dp')
- gate_grad: float32 [884736], P('dp')
- up_grad: float32 [884736], P('dp')
- down_grad: float32 [884736], P('dp')
- gain_grad: float32 [2, 576], replicated
Inputs may be any that keep to these rules, and one draw needn't show every extreme that they name: `cotangent`: rows of one sequence share a scale; scales vary over the sequences.
All inputs are finite; a program needn't handle non-finite values.
Results may differ from a plain program's by a relative error of at most 0.013.
Values may be sent and summed in bfloat16 or wider, within the bound.
No kernel may reach another device: no remote copies, remote signals or barrier semaphores. Data moves between devices by JAX's collectives and lax.ppermute only.
A program may use at most 128 MiB of HBM per device.

v0:
```python
import jax
import jax.numpy as jnp
from jax import lax
from jax.sharding import PartitionSpec as P

HEADS = 9
KV_HEADS = 3
HEAD_DIM = 64
LENGTH = 1024


EPS = 1e-05
THETA = 100000.0
NEG_BIG = -1e30


def rotary_tables(length, head_dim):
    half_dim = head_dim // 2
    frequency = THETA ** (-(jnp.arange(half_dim, dtype=jnp.float32) * 2.0 / head_dim))
    angles = jnp.arange(length, dtype=jnp.float32)[:, None] * frequency[None, :]
    return (jnp.cos(angles), jnp.sin(angles))


def rotate_heads(field, cosine, sine):
    half_dim = field.shape[-1] // 2
    first_half = field[..., :half_dim]
    second_half = field[..., half_dim:]
    cosine = cosine[None, :, None, :]
    sine = sine[None, :, None, :]
    return jnp.concatenate(
        [first_half * cosine - second_half * sine, second_half * cosine + first_half * sine], -1
    )


def normalize(hidden, gain):
    inv_rms = lax.rsqrt(jnp.mean(hidden * hidden, -1, keepdims=True) + EPS)
    return (hidden * inv_rms * gain, inv_rms)


def normalize_back(grad, hidden, inv_rms, gain):
    weighted = grad * gain
    cubed = inv_rms * inv_rms * inv_rms
    hidden_grad = inv_rms * weighted - hidden * cubed * jnp.mean(
        weighted * hidden, -1, keepdims=True
    )
    gain_part = jnp.sum(grad * hidden * inv_rms, 0)
    return (hidden_grad, gain_part)


def outer_prod(left, right):
    return lax.dot_general(
        left, right, (((0,), (0,)), ((), ())), preferred_element_type=jnp.float32
    )


def times_transposed(left, matrix):
    return lax.dot_general(
        left, matrix, (((1,), (1,)), ((), ())), preferred_element_type=jnp.float32
    )


def unpack(flat_set, model_width):
    shaped = tuple((piece.reshape(model_width, -1) for piece in flat_set[:6]))
    return shaped + (flat_set[6].reshape(-1, model_width),)


def block_scores(query_blk, keys_part, q_start):
    scores = jnp.einsum(
        "sqkgd,stkd->skgqt", query_blk, keys_part, preferred_element_type=jnp.float32
    )
    scores = scores * HEAD_DIM ** (-0.5)
    row_index = q_start + jnp.arange(query_blk.shape[1])[:, None]
    col_index = jnp.arange(keys_part.shape[1])[None, :]
    return jnp.where(row_index >= col_index, scores, NEG_BIG)


def body(tokens, cotangent, w_query, w_key, w_value, w_out, w_gate, w_up, w_down, norm_gains):
    model_width = tokens.shape[1]
    seq_count = tokens.shape[0] // LENGTH
    group_size = HEADS // KV_HEADS
    block_rows = min(512, LENGTH)
    scale_factor = HEAD_DIM ** (-0.5)
    gain_f = norm_gains.astype(jnp.float32)
    shards = (w_query, w_key, w_value, w_out, w_gate, w_up, w_down)
    wq_mat, wk_mat, wv_mat, wo_mat, wg_mat, wu_mat, wd_mat = unpack(
        (
            lax.all_gather(shards[0], "dp", axis=0, tiled=True),
            lax.all_gather(shards[1], "dp", axis=0, tiled=True),
            lax.all_gather(shards[2], "dp", axis=0, tiled=True),
            lax.all_gather(shards[3], "dp", axis=0, tiled=True),
            lax.all_gather(shards[4], "dp", axis=0, tiled=True),
            lax.all_gather(shards[5], "dp", axis=0, tiled=True),
            lax.all_gather(shards[6], "dp", axis=0, tiled=True),
        ),
        model_width,
    )
    resid_in = tokens.astype(jnp.float32)
    normed_one, rms_one = normalize(resid_in, gain_f[0])
    normed_one = normed_one.astype(jnp.bfloat16)
    query_lin = jnp.dot(normed_one, wq_mat, preferred_element_type=jnp.float32)
    key_lin = jnp.dot(normed_one, wk_mat, preferred_element_type=jnp.float32)
    value_lin = jnp.dot(normed_one, wv_mat, preferred_element_type=jnp.float32)
    cosine, sine = rotary_tables(LENGTH, HEAD_DIM)
    query_rot = rotate_heads(
        query_lin.reshape(seq_count, LENGTH, HEADS, HEAD_DIM), cosine, sine
    ).astype(jnp.bfloat16)
    query_rot = query_rot.reshape(seq_count, LENGTH, KV_HEADS, group_size, HEAD_DIM)
    key_rot = rotate_heads(
        key_lin.reshape(seq_count, LENGTH, KV_HEADS, HEAD_DIM), cosine, sine
    ).astype(jnp.bfloat16)
    values = value_lin.astype(jnp.bfloat16).reshape(seq_count, LENGTH, KV_HEADS, HEAD_DIM)
    mixed_blocks = []
    total_blocks = []
    for index in range(LENGTH // block_rows):
        q_start = index * block_rows
        key_end = q_start + block_rows
        scores = block_scores(query_rot[:, q_start:key_end], key_rot[:, :key_end], q_start)
        maxima = jnp.max(scores, -1, keepdims=True)
        expo = jnp.exp(scores - maxima)
        totals = jnp.sum(expo, -1, keepdims=True)
        probs = (expo / totals).astype(jnp.bfloat16)
        mixed_blocks.append(
            jnp.einsum(
                "skgqt,stkd->sqkgd", probs, values[:, :key_end], preferred_element_type=jnp.float32
            )
        )
        total_blocks.append((maxima + jnp.log(totals))[..., 0])
    mixed = (
        jnp.concatenate(mixed_blocks, 1)
        .reshape(seq_count * LENGTH, model_width)
        .astype(jnp.bfloat16)
    )
    attn_out = jnp.dot(mixed, wo_mat, preferred_element_type=jnp.float32)
    middle = resid_in + attn_out
    normed_two, rms_two = normalize(middle, gain_f[1])
    normed_two = normed_two.astype(jnp.bfloat16)
    gate = jnp.dot(normed_two, wg_mat, preferred_element_type=jnp.float32)
    upward = jnp.dot(normed_two, wu_mat, preferred_element_type=jnp.float32)
    sigmoid_g = jax.nn.sigmoid(gate)
    activated = gate * sigmoid_g
    hidden = (activated * upward).astype(jnp.bfloat16)
    ffn_out = jnp.dot(hidden, wd_mat, preferred_element_type=jnp.float32)
    output = (middle + ffn_out).astype(jnp.bfloat16)
    wq_mat, wk_mat, wv_mat, wo_mat, wg_mat, wu_mat, wd_mat = unpack(
        (
            lax.all_gather(shards[0], "dp", axis=0, tiled=True),
            lax.all_gather(shards[1], "dp", axis=0, tiled=True),
            lax.all_gather(shards[2], "dp", axis=0, tiled=True),
            lax.all_gather(shards[3], "dp", axis=0, tiled=True),
            lax.all_gather(shards[4], "dp", axis=0, tiled=True),
            lax.all_gather(shards[5], "dp", axis=0, tiled=True),
            lax.all_gather(shards[6], "dp", axis=0, tiled=True),
        ),
        model_width,
    )
    grad_down = outer_prod(hidden, cotangent)
    hidden_back = times_transposed(cotangent, wd_mat)
    gate_back = (hidden_back * upward * sigmoid_g * (1.0 + gate * (1.0 - sigmoid_g))).astype(
        jnp.bfloat16
    )
    up_back = (hidden_back * activated).astype(jnp.bfloat16)
    grad_gate = outer_prod(normed_two, gate_back)
    grad_up = outer_prod(normed_two, up_back)
    two_back = times_transposed(gate_back, wg_mat) + times_transposed(up_back, wu_mat)
    norm_two_back, gain_two = normalize_back(two_back, middle, rms_two, gain_f[1])
    mid_back = cotangent.astype(jnp.float32) + norm_two_back
    mid_low = mid_back.astype(jnp.bfloat16)
    grad_out = outer_prod(mixed, mid_low)
    mixed_back = times_transposed(mid_low, wo_mat).astype(jnp.bfloat16)
    mixed_back = mixed_back.reshape(seq_count, LENGTH, KV_HEADS, group_size, HEAD_DIM)
    query_parts = []
    key_acc = jnp.zeros((seq_count, LENGTH, KV_HEADS, HEAD_DIM), jnp.float32)
    value_acc = jnp.zeros((seq_count, LENGTH, KV_HEADS, HEAD_DIM), jnp.float32)
    for index in range(LENGTH // block_rows):
        q_start = index * block_rows
        key_end = q_start + block_rows
        query_blk = query_rot[:, q_start:key_end]
        keys_part = key_rot[:, :key_end]
        values_part = values[:, :key_end]
        back_blk = mixed_back[:, q_start:key_end]
        scores = block_scores(query_blk, keys_part, q_start)
        probs = jnp.exp(scores - total_blocks[index][..., None])
        prob_back = jnp.einsum(
            "sqkgd,stkd->skgqt", back_blk, values_part, preferred_element_type=jnp.float32
        )
        centred = prob_back - jnp.sum(probs * prob_back, -1, keepdims=True)
        score_back = (probs * centred).astype(jnp.bfloat16)
        query_parts.append(
            jnp.einsum(
                "skgqt,stkd->sqkgd", score_back, keys_part, preferred_element_type=jnp.float32
            )
            * scale_factor
        )
        key_part = (
            jnp.einsum(
                "skgqt,sqkgd->stkd", score_back, query_blk, preferred_element_type=jnp.float32
            )
            * scale_factor
        )
        value_part = jnp.einsum(
            "skgqt,sqkgd->stkd",
            probs.astype(jnp.bfloat16),
            back_blk,
            preferred_element_type=jnp.float32,
        )
        padding = ((0, 0), (0, LENGTH - key_end), (0, 0), (0, 0))
        key_acc = key_acc + jnp.pad(key_part, padding)
        value_acc = value_acc + jnp.pad(value_part, padding)
    rot_query_back = jnp.concatenate(query_parts, 1).reshape(seq_count, LENGTH, HEADS, HEAD_DIM)
    query_back = (
        rotate_heads(rot_query_back, cosine, -sine)
        .reshape(seq_count * LENGTH, model_width)
        .astype(jnp.bfloat16)
    )
    key_back = (
        rotate_heads(key_acc, cosine, -sine).reshape(seq_count * LENGTH, -1).astype(jnp.bfloat16)
    )
    value_back = value_acc.reshape(seq_count * LENGTH, -1).astype(jnp.bfloat16)
    grad_query = outer_prod(normed_one, query_back)
    grad_key = outer_prod(normed_one, key_back)
    grad_value = outer_prod(normed_one, value_back)
    one_back = (
        times_transposed(query_back, wq_mat)
        + times_transposed(key_back, wk_mat)
        + times_transposed(value_back, wv_mat)
    )
    norm_one_back, gain_one = normalize_back(one_back, resid_in, rms_one, gain_f[0])
    input_grad = (mid_back + norm_one_back).astype(jnp.bfloat16)
    all_parts = (
        lax.psum_scatter(grad_query.reshape(-1), "dp", scatter_dimension=0, tiled=True),
        lax.psum_scatter(grad_key.reshape(-1), "dp", scatter_dimension=0, tiled=True),
        lax.psum_scatter(grad_value.reshape(-1), "dp", scatter_dimension=0, tiled=True),
        lax.psum_scatter(grad_out.reshape(-1), "dp", scatter_dimension=0, tiled=True),
        lax.psum_scatter(grad_gate.reshape(-1), "dp", scatter_dimension=0, tiled=True),
        lax.psum_scatter(grad_up.reshape(-1), "dp", scatter_dimension=0, tiled=True),
        lax.psum_scatter(grad_down.reshape(-1), "dp", scatter_dimension=0, tiled=True),
    )
    gain_grad = lax.psum(jnp.stack([gain_one, gain_two]), "dp")
    return (output, input_grad) + tuple(all_parts) + (gain_grad,)


def solution(mesh):
    return jax.shard_map(
        body,
        mesh=mesh,
        in_specs=(
            P("dp", None),
            P("dp", None),
            P("dp"),
            P("dp"),
            P("dp"),
            P("dp"),
            P("dp"),
            P("dp"),
            P("dp"),
            P(),
        ),
        out_specs=(
            P("dp", None),
            P("dp", None),
            P("dp"),
            P("dp"),
            P("dp"),
            P("dp"),
            P("dp"),
            P("dp"),
            P("dp"),
            P(),
        ),
        check_vma=False,
    )
```

profile of v0, /device:TPU:0, one launch (start us, length us, event | category | flops | bytes accessed | tf_op | source)
XLA Modules:
  0.0 680.1 jit_solution(12479597163947359396)
XLA Ops:
  10.3 1.5 fusion.25
  14.5 1.4 reshape.532
  15.9 1.4 reshape.534
  18.5 44.7 %all-gather = bf16[32,1,3456]{2,1,0:T(2,128)(2,1)S(1)} all-gather(bf16[1,1,3456]{2,1,0:T(2,128)(2,1)S(1)} %reshape.528), channel_id=1, replica_groups=mesh['dp'=32] {'dp'}, dimensions={0}, use_global_device_ids=true | all-gather | bytes 228096 | tf_op jit(solution)/shard_map/all_gather | solution.py:89
  64.7 38.0 %all-gather.1 = bf16[32,1,3456]{2,1,0:T(2,128)(2,1)S(1)} all-gather(bf16[1,1,3456]{2,1,0:T(2,128)(2,1)S(1)} %reshape.530), channel_id=1, replica_groups=mesh['dp'=32] {'dp'}, dimensions={0}, use_global_device_ids=true | all-gather | bytes 228096 | tf_op jit(solution)/shard_map/all_gather | solution.py:88
  105.5 1.4 convolution_convert_fusion.1
  106.9 1.5 convolution_bitcast_fusion.1
  108.3 43.5 %all-gather.3 = bf16[32,1,10368]{2,1,0:T(2,128)(2,1)S(1)} all-gather(bf16[1,1,10368]{2,1,0:T(2,128)(2,1)S(1)} %copy-done.51), channel_id=1, replica_groups=mesh['dp'=32] {'dp'}, dimensions={0}, use_global_device_ids=true | all-gather | bytes 684288 | tf_op jit(solution)/shard_map/all_gather | solution.py:90
  151.8 4.0 reduce.10
  155.8 1.7 reshape.507
  157.5 42.2 %all-gather.2 = bf16[32,1,10368]{2,1,0:T(2,128)(2,1)S(1)} all-gather(bf16[1,1,10368]{2,1,0:T(2,128)(2,1)S(1)} %copy-done.50), channel_id=1, replica_groups=mesh['dp'=32] {'dp'}, dimensions={0}, use_global_device_ids=true | all-gather | bytes 684288 | tf_op jit(solution)/shard_map/all_gather | solution.py:87
  199.7 4.8 reduce.9
  204.6 2.2 reshape.501
  209.3 1.7 fusion.99
  212.4 2.3 copy-done
  214.7 8.1 %fusion.98 = (f32[3,3,512]{2,1,0:T(4,128)S(1)}, f32[1,3,3,512,1024]{3,4,2,1,0:T(8,128)}) fusion(bf16[1,1024,3,3,32]{1,4,3,2,0:T(8,128)(2,1)S(1)} %bitcast.250, bf16[1,1024,3,3,32]{1,4,3,2,0:T(8,128)(2,1)S(1)} %bitcast.246, bf16[1024,3,32]{0,2,1:T(8,128)(2,1)S(1)} %bitcast.262, bf16[1024,3,32]{0,2,1:T(8,128)(2,1)S(1)} %bitcast.260, ...), kind=kOutput, calls=%fused_computation.146 | convolution fusion | flops 620097024 | bytes 20989952 | tf_op jit(solution)/shard_map/sqkgd,stkd->skgqt/dot_general | solution.py:68
  222.8 9.0 %fusion.3 = f32[3,3,512]{2,1,0:T(4,128)S(1)} fusion(f32[1,3,3,512,1024]{3,4,2,1,0:T(8,128)} %get-tuple-element.42, f32[3,3,512]{2,1,0:T(4,128)S(1)} %get-tuple-element.41), kind=kLoop, calls=%fused_computation.9 | loop fusion | flops 9432576 | bytes 18911232 | tf_op jit(solution)/shard_map/reduce_sum | solution.py:120
  231.8 8.7 %fusion.37 = bf16[3,64,3,512]{3,1,2,0:T(8,128)(2,1)S(1)} fusion(bf16[1024,3,64,1]{0,2,3,1:T(8,128)(2,1)S(1)} %bitcast.271, f32[3,3,512]{2,1,0:T(4,128)S(1)} %fusion.3, f32[1,3,3,512,1024]{3,4,2,1,0:T(8,128)} %get-tuple-element.42, f32[3,3,512]{2,1,0:T(4,128)S(1)} %get-tuple-element.41), kind=kOutput, calls=%fused_computation.72 | convolution fusion | flops 618430464 | bytes 19894272 | tf_op jit(solution)/shard_map/skgqt,stkd->sqkgd/dot_general | solution.py:123
  240.6 1.7 fusion.40
  248.1 4.4 reshape.508
  252.5 4.4 reshape.509
  256.9 7.2 %fusion.101 = f32[1024,1536]{1,0:T(8,128)} fusion(bf16[1024,576]{0,1:T(8,128)(2,1)} %multiply_convert_fusion.3, bf16[576,1536]{1,0:T(8,128)(2,1)} %reshape.509), kind=kOutput, calls=%fused_computation.149 | convolution fusion | flops 1811939328 | bytes 9240576 | tf_op jit(solution)/shard_map/dot_general | solution.py:138
  264.1 4.6 fusion.100
  268.7 4.3 reshape.510
  273.0 10.9 %multiply_convert_fusion = (bf16[1024,1536]{1,0:T(8,128)(2,1)S(1)}, bf16[1024,1536]{1,0:T(8,128)(2,1)S(1)}, bf16[1024,1536]{1,0:T(8,128)(2,1)}) fusion(f32[1024,1536]{1,0:T(8,128)} %fusion.100, f32[1024,1536]{1,0:T(8,128)} %fusion.101, bf16[1024,576]{0,1:T(8,128)(2,1)} %param.11, bf16[1536,576]{1,0:T(8,128)(2,1)} %reshape.510), kind=kOutput, calls=%fused_computation.28 | convolution fusion | flops 1835532288 | bytes 24969216 | tf_op jit(solution)/shard_map/dot_general | solution.py:57
  283.9 2.0 fusion.102
  286.0 3.8 fusion.103
  289.7 3.7 fusion.104
  293.5 2.9 multiply_reduce_fusion
  296.5 2.4 subtract_add_fusion
  300.1 2.3 fusion.55
  302.4 5.6 fusion.9
  308.0 11.1 %fusion.21 = bf16[3,3,512,512]{2,3,1,0:T(8,128)(2,1)} fusion(f32[3,512,512,3]{2,1,3,0:T(8,128)} %get-tuple-element.51, f32[1,3,3,512,512]{3,4,2,1,0:T(8,128)} %copy-done, f32[3,3,512]{2,1,0:T(4,128)} %get-tuple-element.50, f32[3,3,512]{2,1,0:T(4,128)} %log_add_fusion.1), kind=kLoop, calls=%fused_computation.41 | loop fusion | flops 9437184 | bytes 23629824 | tf_op jit(solution)/shard_map/reshape.30
  319.1 5.0 fusion.59
  324.1 1.9 fusion.35
  326.1 2.3 fusion.68
  328.3 2.8 reshape.522
  331.1 4.6 reshape.523
  335.7 4.6 reshape.524
  340.2 13.0 %fusion = (f32[3,3,512]{2,1,0:T(4,128)}, f32[3,1024,512,3]{2,1,3,0:T(8,128)}) fusion(f32[1,3,3,512,1024]{3,4,2,1,0:T(8,128)} %get-tuple-element.42, f32[3,3,512]{2,1,0:T(4,128)} %log_add_fusion, bf16[1024,3,64,1]{0,2,3,1:T(8,128)(2,1)} %bitcast.270, bf16[1,1024,3,3,64]{1,4,3,2,0:T(8,128)(2,1)} %bitcast.256), kind=kOutput, calls=%fused_computation.3 | convolution fusion | flops 618130944 | bytes 38774784 | tf_op jit(solution)/shard_map/sqkgd,stkd->skgqt/dot_general | solution.py:183
  353.2 8.3 %fusion.52 = bf16[1,1024,3,64]{1,3,2,0:T(8,128)(2,1)S(1)} fusion(f32[1,3,3,512,1024]{3,4,2,1,0:T(8,128)} %get-tuple-element.42, f32[3,3,512]{2,1,0:T(4,128)S(1)} %copy-done.48, f32[1,512,3,64]{1,3,2,0:T(8,128)S(1)} %copy-done.31, bf16[1,1024,3,3,64]{1,4,3,2,0:T(8,128)(2,1)S(1)} %bitcast.257), kind=kOutput, calls=%fused_computation.82 | convolution fusion | flops 613810176 | bytes 20275200 | tf_op jit(solution)/shard_map/skgqt,sqkgd->stkd/dot_general | solution.py:200
  363.6 2.1 reshape.521
  365.8 6.8 %fusion.105 = f32[1536,576]{1,0:T(8,128)} fusion(bf16[1024,1536]{1,0:T(8,128)(2,1)} %get-tuple-element.25, bf16[1024,576]{0,1:T(8,128)(2,1)} %param.11), kind=kOutput, calls=%fused_computation.153 | convolution fusion | flops 1811939328 | bytes 7864320 | tf_op jit(solution)/shard_map/dot_general | solution.py:51
  372.6 5.3 reshape.525
  377.9 13.5 %fusion.8 = bf16[3,3,512,1024]{2,3,1,0:T(8,128)(2,1)S(1)} fusion(f32[3,1024,512,3]{2,1,3,0:T(8,128)} %get-tuple-element.49, f32[1,3,3,512,1024]{3,4,2,1,0:T(8,128)} %get-tuple-element.42, f32[3,3,512]{2,1,0:T(4,128)} %get-tuple-element.48, f32[3,3,512]{2,1,0:T(4,128)} %log_add_fusion), kind=kLoop, calls=%fused_computation.13 | loop fusion | flops 18874368 | bytes 47222784 | tf_op jit(solution)/shard_map/reshape.69
  391.4 1.7 fusion.36
  393.2 2.9 fusion.48
  396.5 1.4 multiply_subtract_fusion
  400.0 2.1 reshape.520
  404.5 2.3 fusion.92
  406.8 3.0 reshape.519
  410.6 1.5 fusion.107
  413.4 3.1 fusion.34
  416.4 38.8 %psum.7 = f32[2,576]{1,0:T(2,128)} all-reduce(f32[2,576]{1,0:T(2,128)S(1)} %pad_maximum_fusion.4), channel_id=1, replica_groups=mesh['dp'=32] {'dp'}, use_global_device_ids=true, to_apply=%region_19.20 | all-reduce | flops 1152 | bytes 9216 | tf_op jit(solution)/shard_map/psum | solution.py:238
  455.9 3.5 fusion.31
  459.4 5.1 add_convert_fusion
  464.5 198.1 %all-reduce.12.cloned.1.call-done = (f32[331776]{0:T(1024)}, f32[110592]{0:T(1024)}, f32[110592]{0:T(1024)}, f32[331776]{0:T(1024)}, f32[884736]{0:T(1024)}, /*index=5*/f32[884736]{0:T(1024)}, f32[884736]{0:T(1024)}) async-done(((f32[331776]{0:T(1024)}, f32[110592]{0:T(1024)}, f32[110592]{0:T(1024)}, f32[331776]{0:T(1024)}, f32[884736]{0:T(1024)}, /*index=5*/f32[884736]{0:T(1024)}, f32[884736]{0:T(1024)}), ...) | async-done | bytes 14155792
  662.6 1.5 dynamic-slice
  664.1 1.5 dynamic-slice.3
  665.6 1.4 dynamic-slice.1
  667.0 1.4 dynamic-slice.2
  668.4 1.5 dynamic-slice.4
  669.9 1.5 dynamic-slice.5
  671.5 1.5 dynamic-slice.6
  (187 shorter events, 31.6 us)
Async XLA Ops:
  7.2 240.9 %all-gather.8.cloned.1.call-start = ((), (), s32[]{:S(2)}) async-start(), calls=%async_computation | async-start | bytes 1824768 | tf_op jit(solution)/shard_map/all_gather | solution.py:91
  7.9 244.6 %all-gather.10.cloned.1.call-start = ((), (), s32[]{:S(2)}) async-start(), calls=%async_computation.1 | async-start | bytes 1824768 | tf_op jit(solution)/shard_map/all_gather | solution.py:92
  8.7 260.0 %all-gather.12.cloned.1.call-start = ((), (), s32[]{:S(2)}) async-start(), calls=%async_computation.2 | async-start | bytes 1824768 | tf_op jit(solution)/shard_map/all_gather | solution.py:93
  9.4 653.2 %all-reduce.12.cloned.1.call-start = ((), (), s32[]{:S(2)}) async-start(), calls=%async_computation.3 | async-start | bytes 28311552
  17.3 88.2 %copy-start.2 = (bf16[1024,576]{0,1:T(8,128)(2,1)S(1)}, bf16[1024,576]{0,1:T(8,128)(2,1)}, u32[]{:S(2)}) copy-start(bf16[1024,576]{0,1:T(8,128)(2,1)} %param.10) | copy-start | bytes 3538948
  18.5 190.0 %copy-start.13 = (f32[1024,32]{0,1:T(8,128)}, f32[1024,32]{0,1:T(8,128)S(1)}, u32[]{:S(2)}) copy-start(f32[1024,32]{0,1:T(8,128)S(1)} %get-tuple-element.40) | copy-start | bytes 393220
  64.7 42.2 %copy-start.33 = (bf16[576,192]{1,0:T(8,128)(2,1)}, bf16[576,192]{1,0:T(8,128)(2,1)S(1)}, u32[]{:S(2)}) copy-start(bf16[576,192]{1,0:T(8,128)(2,1)S(1)} %reshape.496) | copy-start | bytes 663556
  104.1 4.2 copy-start.17
  105.5 2.8 copy-start.51
  108.3 49.2 %copy-start.50 = (bf16[1,1,10368]{2,1,0:T(2,128)(2,1)S(1)}, bf16[1,1,10368]{2,1,0:T(2,128)(2,1)}, u32[]{:S(2)}) copy-start(bf16[1,1,10368]{2,1,0:T(2,128)(2,1)} %reshape.532) | copy-start | bytes 62212
  206.8 1.5 copy-start.15
  208.5 6.2 copy-start.22
  208.5 6.2 copy-start.25
  208.9 5.8 copy-start.5
  208.9 5.8 copy-start.7
  211.0 3.7 copy-start
  211.0 29.6 %copy-start.52 = (f32[3,3,512]{2,1,0:T(4,128)}, f32[3,3,512]{2,1,0:T(4,128)S(1)}, u32[]{:S(2)}) copy-start(f32[3,3,512]{2,1,0:T(4,128)S(1)} %get-tuple-element.43) | copy-start | bytes 55300
  211.0 3.7 copy-start.46
  214.6 25.9 %copy-start.54 = (f32[3,3,512]{2,1,0:T(4,128)}, f32[3,3,512]{2,1,0:T(4,128)S(1)}, u32[]{:S(2)}) copy-start(f32[3,3,512]{2,1,0:T(4,128)S(1)} %fusion.15) | copy-start | bytes 55300
  222.7 9.0 %copy-start.56 = (f32[3,3,512]{2,1,0:T(4,128)}, f32[3,3,512]{2,1,0:T(4,128)S(1)}, u32[]{:S(2)}) copy-start(f32[3,3,512]{2,1,0:T(4,128)S(1)} %get-tuple-element.41) | copy-start | bytes 55300
  222.7 9.0 %copy-start.41 = (bf16[1024,192]{0,1:T(8,128)(2,1)S(1)}, bf16[1024,192]{0,1:T(8,128)(2,1)}, u32[]{:S(2)}) copy-start(bf16[1024,192]{0,1:T(8,128)(2,1)} %convolution_convert_fusion.1) | copy-start | bytes 1179652
  222.7 17.8 %slice-start = ((s8[9437184]{0:T(1024)(128)(4,1)}), s8[1048576]{0:T(1024)(128)(4,1)S(1)}, s32[]{:S(2)}) async-start(s8[9437184]{0:T(1024)(128)(4,1)} %bitcast.240), calls=%async_computation.4 | async-start | bytes 2097152
  231.7 8.8 %copy-start.58 = (f32[3,3,512]{2,1,0:T(4,128)}, f32[3,3,512]{2,1,0:T(4,128)S(1)}, u32[]{:S(2)}) copy-start(f32[3,3,512]{2,1,0:T(4,128)S(1)} %fusion.3) | copy-start | bytes 55300
  231.8 8.8 %slice-start.1 = ((s8[9437184]{0:T(1024)(128)(4,1)}), s8[4194304]{0:T(1024)(128)(4,1)S(1)}, s32[]{:S(2)}) async-start(s8[9437184]{0:T(1024)(128)(4,1)} %bitcast.240), calls=%async_computation.5 | async-start | bytes 8388608
  231.8 8.8 %slice-start.2 = ((s8[9437184]{0:T(1024)(128)(4,1)}), s8[4194304]{0:T(1024)(128)(4,1)S(1)}, s32[]{:S(2)}) async-start(s8[9437184]{0:T(1024)(128)(4,1)} %bitcast.240), calls=%async_computation.6 | async-start | bytes 8388608
  242.3 1.2 copy-start.44
  243.6 1.9 copy-start.53
  243.6 1.9 copy-start.55
  243.6 2.6 copy-start.57
  243.6 2.6 copy-start.59
  244.8 48.7 %copy-start.3 = (f32[1024,576]{0,1:T(8,128)}, f32[1024,576]{0,1:T(8,128)S(1)}, u32[]{:S(2)}) copy-start(f32[1024,576]{0,1:T(8,128)S(1)} %get-tuple-element.46) | copy-start | bytes 7077892
  256.9 7.2 %copy-start.20 = (bf16[576,1536]{1,0:T(8,128)(2,1)S(1)}, bf16[576,1536]{1,0:T(8,128)(2,1)}, u32[]{:S(2)}) copy-start(bf16[576,1536]{1,0:T(8,128)(2,1)} %reshape.508) | copy-start | bytes 5308420
  256.9 7.2 %copy-start.35 = (bf16[1024,576]{0,1:T(8,128)(2,1)S(1)}, bf16[1024,576]{0,1:T(8,128)(2,1)}, u32[]{:S(2)}) copy-start(bf16[1024,576]{0,1:T(8,128)(2,1)} %multiply_convert_fusion.3) | copy-start | bytes 3538948
  273.0 10.9 %copy-start.21 = (bf16[576,1536]{1,0:T(8,128)(2,1)S(1)}, bf16[576,1536]{1,0:T(8,128)(2,1)}, u32[]{:S(2)}) copy-start(bf16[576,1536]{1,0:T(8,128)(2,1)} %reshape.508) | copy-start | bytes 5308420
  283.9 2.0 copy-start.36
  289.7 3.7 copy-start.19
  293.5 3.0 copy-start.39
  293.5 3.0 copy-start.60
  293.5 6.5 slice-start.3
  293.5 6.5 slice-start.4
  296.4 2.5 copy-start.45
  296.5 3.6 slice-start.5
  300.0 2.4 copy-start.11
  300.1 2.3 copy-start.42
  319.1 5.0 copy-start.1
  319.1 5.0 copy-start.23
  319.1 5.0 copy-start.26
  324.1 2.0 copy-start.9
  340.2 13.0 %copy-start.12 = (bf16[1024,576]{0,1:T(8,128)(2,1)S(1)}, bf16[1024,576]{0,1:T(8,128)(2,1)}, u32[]{:S(2)}) copy-start(bf16[1024,576]{0,1:T(8,128)(2,1)} %copy-done.11) | copy-start | bytes 3538948
  340.2 13.0 %copy-start.31 = (f32[1,512,3,64]{1,3,2,0:T(8,128)S(1)}, f32[1,512,3,64]{1,3,2,0:T(8,128)}, u32[]{:S(2)}) copy-start(f32[1,512,3,64]{1,3,2,0:T(8,128)} %fusion.55) | copy-start | bytes 1179652
  340.2 13.0 %copy-start.48 = (f32[3,3,512]{2,1,0:T(4,128)S(1)}, f32[3,3,512]{2,1,0:T(4,128)}, u32[]{:S(2)}) copy-start(f32[3,3,512]{2,1,0:T(4,128)} %log_add_fusion) | copy-start | bytes 55300
  377.8 13.5 %copy-start.24 = (bf16[1,1024,3,32]{1,3,2,0:T(8,128)(2,1)S(1)}, bf16[1,1024,3,32]{1,3,2,0:T(8,128)(2,1)}, u32[]{:S(2)}) copy-start(bf16[1,1024,3,32]{1,3,2,0:T(8,128)(2,1)} %copy-done.22) | copy-start | bytes 589828
  377.9 13.5 %copy-start.27 = (bf16[1,1024,3,32]{1,3,2,0:T(8,128)(2,1)S(1)}, bf16[1,1024,3,32]{1,3,2,0:T(8,128)(2,1)}, u32[]{:S(2)}) copy-start(bf16[1,1024,3,32]{1,3,2,0:T(8,128)(2,1)} %copy-done.25) | copy-start | bytes 589828
  391.4 1.8 copy-start.6
  391.4 1.8 copy-start.8
  391.4 1.8 copy-start.28
  393.2 3.0 copy-start.14
  393.2 3.0 copy-start.40
  393.2 3.1 copy-start.10
  409.9 2.2 copy-start.16
  409.9 2.2 copy-start.38
  412.1 1.2 copy-start.34
  455.9 3.5 copy-start.4
  455.9 3.5 copy-start.18
  (8 other events, 7.6 us)
Sparse Core Ops, SparseCore 0:
  10.8 58.4 all-gather.7
  72.2 55.5 all-gather.9
  130.6 56.8 all-gather.11
  410.0 252.5 all-reduce.11
where the time goes:
time: 687 us; the launch traced here: 680 us
  blocking collectives  207 us (30%)
  waiting for transfers between devices  200 us (29%)
  matrix products  127 us (18%)
  other arithmetic  67 us (10%)
  local copies, waits for them, and re-layouts  63.5 us (9%)
  between operations  15.1 us (2%)
    unnamed x5, waiting for transfers between devices  200 us
    all_gather x1, blocking collectives, body(): lax.all_gather(shards[2], 'dp', axis=0, tiled=True)  44.7 us
    all_gather x1, blocking collectives, body(): lax.all_gather(shards[3], 'dp', axis=0, tiled=True)  43.5 us
    all_gather x1, blocking collectives, body(): lax.all_gather(shards[0], 'dp', axis=0, tiled=True)  42.2 us
    psum x1, blocking collectives, body(): gain_grad = lax.psum(jnp.stack([gain_one, gain_two]), 'dp')  38.8 us
    all_gather x1, blocking collectives, body(): lax.all_gather(shards[1], 'dp', axis=0, tiled=True)  38 us
    another operation x4, other arithmetic  25.1 us
    dot_general x7, matrix products, times_transposed(): lax.dot_general(left, matrix, (((1,), (1,)), ((), ())), preferred_element...  22.6 us
  transfers between devices with their start and end apart: 4, of which 1 were waited for; matrix products, arithmetic and copies ran while one was open for 15% of the time, Pallas kernels for 0%

commit v1 on v0

--- a/solution.py
+++ b/solution.py
@@ -1,6 +1,10 @@
+import functools
+
 import jax
 import jax.numpy as jnp
 from jax import lax
+from jax.experimental import pallas as pl
+from jax.experimental.pallas import tpu as pltpu
 from jax.sharding import PartitionSpec as P
 
 HEADS = 9
@@ -12,6 +16,217 @@
 EPS = 1e-05
 THETA = 100000.0
 NEG_BIG = -1e30
+LANES = 128
+VMEM_LIMIT = 56 * 1024 * 1024
+CORE_MASK = 1
+
+
+def masks_of(devices):
+    plane = tuple(2 * step for step in range(4))
+    line = tuple(8 * step for step in range(devices // 8))
+    return (plane, line)
+
+
+def swap(field, mask, devices):
+    return lax.ppermute(field, "dp", [(place, place ^ mask) for place in range(devices)])
+
+
+def gather_pieces(piece, devices):
+    plane, line = masks_of(devices)
+    held = jnp.stack([piece] + [swap(piece, mask, devices) for mask in line[1:]])
+    held = jnp.concatenate([held] + [swap(held, mask, devices) for mask in plane[1:]])
+    return (held, swap(held, CORE_MASK, devices))
+
+
+def tree_sum(terms):
+    while len(terms) > 1:
+        terms = [terms[at] + terms[at + 1] for at in range(0, len(terms), 2)]
+    return terms[0]
+
+
+def widen(field):
+    return field.astype(jnp.float32)
+
+
+def scatter_pieces(kept, sent, devices):
+    plane, line = masks_of(devices)
+    got = swap(sent, CORE_MASK, devices)
+    block = kept.shape[0] // len(plane)
+    parts = [
+        (widen(kept[at * block : (at + 1) * block]) + widen(got[at * block : (at + 1) * block])).astype(jnp.bfloat16)
+        for at in range(len(plane))
+    ]
+    arrived = [swap(part, mask, devices) for part, mask in zip(parts[1:], plane[1:])]
+    parts = [
+        tree_sum([widen(term[at]) for term in [parts[0]] + arrived]).astype(jnp.bfloat16)
+        for at in range(len(line))
+    ]
+    arrived = [swap(part, mask, devices) for part, mask in zip(parts[1:], line[1:])]
+    return tree_sum([widen(term) for term in [parts[0]] + arrived])
+
+
+def slot_mask(core, slot, devices):
+    line = devices // 8
+    return core * CORE_MASK + 2 * (slot // line) + 8 * (slot % line)
+
+
+def each_group(devices, step, body):
+    group = 4
+
+    def run(at, carry):
+        for inner in range(group):
+            body(at * group + inner, pl.multiple_of(at * group * step, 8) + inner * step)
+        return carry
+
+    lax.fori_loop(0, devices // group, run, 0)
+
+
+def half_tiles(tiles):
+    lane = lax.broadcasted_iota(jnp.int32, tiles[0].shape, 1)
+    rolled = [pltpu.roll(tile, LANES // 2, 1) for tile in tiles]
+    shifted = [
+        jnp.where(lane < LANES // 2, rolled[at], rolled[at + 1]) for at in range(len(tiles) - 1)
+    ]
+    return shifted + [rolled[-1]]
+
+
+def unpack_rows(stage, owner, start, rows, wide, target, row):
+    whole = wide // LANES
+    if wide % LANES == 0:
+        for at in range(whole):
+            target[at, pl.ds(row, rows), :] = stage[
+                owner, pl.ds(start + at, rows, stride=whole), :
+            ]
+        return
+    pairs, tiles_in = rows // 2, 2 * wide // LANES
+    tiles = [stage[owner, pl.ds(start + at, pairs, stride=tiles_in), :] for at in range(tiles_in)]
+    for at in range(whole):
+        target[at, pl.ds(row, pairs, stride=2), :] = tiles[at]
+    target[whole, pl.ds(row, pairs, stride=2), :] = tiles[whole]
+    for at, tile in enumerate(half_tiles(tiles[whole:])):
+        target[at, pl.ds(row + 1, pairs, stride=2), :] = tile
+
+
+def pack_rows(source, row, rows, wide, stage, owner, start):
+    whole = wide // LANES
+    if wide % LANES == 0:
+        for at in range(whole):
+            stage[owner, pl.ds(start + at, rows, stride=whole), :] = source[
+                at, pl.ds(row, rows), :
+            ]
+        return
+    pairs, tiles_in = rows // 2, 2 * wide // LANES
+    even = [
+        source[at, pl.ds(row, pairs, stride=2), :] for at in range(whole + 1)
+    ]
+    odd = [
+        source[at, pl.ds(row + 1, pairs, stride=2), :]
+        for at in range(whole + 1)
+    ]
+    lane = lax.broadcasted_iota(jnp.int32, even[0].shape, 1)
+    rolled = [pltpu.roll(tile, LANES // 2, 1) for tile in odd]
+    tiles = even[:whole]
+    tiles.append(jnp.where(lane < LANES // 2, even[whole], rolled[0]))
+    for at in range(whole):
+        tiles.append(jnp.where(lane < LANES // 2, rolled[at], rolled[at + 1]))
+    for at in range(tiles_in):
+        stage[owner, pl.ds(start + at, pairs, stride=tiles_in), :] = tiles[at]
+
+
+def tile_widths(wide):
+    return [min(LANES, wide - at) for at in range(0, wide, LANES)]
+
+
+def load_stage(place_ref, own_ref, got_ref, stage, devices):
+    place = place_ref[0]
+    for core, pieces in enumerate((own_ref, got_ref)):
+
+        def load(slot, carry, core=core, pieces=pieces):
+            owner = place ^ slot_mask(core, slot, devices)
+            stage[owner] = pieces[slot].astype(jnp.float32)
+            return carry
+
+        lax.fori_loop(0, devices // 2, load, 0)
+
+
+def store_stage(kept_ref, sent_ref, stage, devices):
+    for core, pieces in enumerate((kept_ref, sent_ref)):
+
+        def store(slot, carry, core=core, pieces=pieces):
+            pieces[slot] = stage[slot_mask(core, slot, devices)].astype(jnp.bfloat16)
+            return carry
+
+        lax.fori_loop(0, devices // 2, store, 0)
+
+
+def unpack_kernel(place_ref, own_ref, got_ref, *refs, devices, shapes):
+    count = len(shapes)
+    outs, stage, wides = refs[:count], refs[count], refs[count + 1 :]
+    load_stage(place_ref, own_ref, got_ref, stage, devices)
+    start = 0
+    for (rows, wide), out, target in zip(shapes, outs, wides):
+        each = rows // devices
+        each_group(
+            devices,
+            each,
+            lambda owner, row, start=start, each=each, wide=wide, target=target: unpack_rows(
+                stage, owner, start, each, wide, target, row
+            ),
+        )
+        start += each * wide // LANES
+        for at, width in enumerate(tile_widths(wide)):
+            out[:, at * LANES : at * LANES + width] = target[at][:, :width].astype(jnp.bfloat16)
+
+
+def unpack_pieces(place, pieces, shapes, devices):
+    rows_in = pieces[0].shape[1]
+    return pl.pallas_call(
+        functools.partial(unpack_kernel, devices=devices, shapes=shapes),
+        out_shape=[jax.ShapeDtypeStruct(shape, jnp.bfloat16) for shape in shapes],
+        in_specs=[pl.BlockSpec(memory_space=pltpu.SMEM)] + [pl.BlockSpec(memory_space=pltpu.VMEM)] * 2,
+        out_specs=[pl.BlockSpec(memory_space=pltpu.VMEM)] * len(shapes),
+        scratch_shapes=[pltpu.VMEM((devices, rows_in, LANES), jnp.float32)]
+        + [pltpu.VMEM((-(-wide // LANES), rows, LANES), jnp.float32) for rows, wide in shapes],
+        compiler_params=pltpu.CompilerParams(vmem_limit_bytes=VMEM_LIMIT),
+        name="unpack",
+    )(place, *pieces)
+
+
+def pack_kernel(place_ref, *refs, devices, shapes):
+    count = len(shapes)
+    sources, kept_ref, sent_ref, stage = refs[:count], refs[count], refs[count + 1], refs[count + 2]
+    wides = refs[count + 3 :]
+    place = place_ref[0]
+    start = 0
+    for (rows, wide), source, tiled in zip(shapes, sources, wides):
+        each = rows // devices
+        for at, width in enumerate(tile_widths(wide)):
+            tiled[at, :, :width] = source[:, at * LANES : at * LANES + width]
+        each_group(
+            devices,
+            each,
+            lambda owner, row, start=start, each=each, wide=wide, tiled=tiled: pack_rows(
+                tiled, row, each, wide, stage, place ^ owner, start
+            ),
+        )
+        start += each * wide // LANES
+    store_stage(kept_ref, sent_ref, stage, devices)
+
+
+def pack_grads(place, grads, shapes, devices):
+    rows_out = sum(rows * wide for rows, wide in shapes) // (devices * LANES)
+    half = jax.ShapeDtypeStruct((devices // 2, rows_out, LANES), jnp.bfloat16)
+    return pl.pallas_call(
+        functools.partial(pack_kernel, devices=devices, shapes=shapes),
+        out_shape=[half, half],
+        in_specs=[pl.BlockSpec(memory_space=pltpu.SMEM)]
+        + [pl.BlockSpec(memory_space=pltpu.VMEM)] * len(shapes),
+        out_specs=[pl.BlockSpec(memory_space=pltpu.VMEM)] * 2,
+        scratch_shapes=[pltpu.VMEM((devices, rows_out, LANES), jnp.float32)]
+        + [pltpu.VMEM((-(-wide // LANES), rows, LANES), jnp.float32) for rows, wide in shapes],
+        compiler_params=pltpu.CompilerParams(vmem_limit_bytes=VMEM_LIMIT),
+        name="pack",
+    )(place, *grads)
 
 
 def rotary_tables(length, head_dim):
@@ -59,11 +274,6 @@
     )
 
 
-def unpack(flat_set, model_width):
-    shaped = tuple((piece.reshape(model_width, -1) for piece in flat_set[:6]))
-    return shaped + (flat_set[6].reshape(-1, model_width),)
-
-
 def block_scores(query_blk, keys_part, q_start):
     scores = jnp.einsum(
         "sqkgd,stkd->skgqt", query_blk, keys_part, preferred_element_type=jnp.float32
@@ -72,6 +282,51 @@
     row_index = q_start + jnp.arange(query_blk.shape[1])[:, None]
     col_index = jnp.arange(keys_part.shape[1])[None, :]
     return jnp.where(row_index >= col_index, scores, NEG_BIG)
+
+
+def whole_rows(shapes, devices):
+    return devices % 8 == 0 and all(
+        rows % (2 * devices) == 0 and wide % (LANES // 2) == 0 for rows, wide in shapes
+    ) and (devices & (devices - 1)) == 0
+
+
+def gather_weights(shards, shapes, devices):
+    if not whole_rows(shapes, devices):
+        return [
+            lax.all_gather(shard, "dp", axis=0, tiled=True).reshape(shape)
+            for shard, shape in zip(shards, shapes)
+        ]
+    place = lax.axis_index("dp").astype(jnp.int32).reshape(1)
+    mats = []
+    for part in (slice(0, 3), slice(3, 7)):
+        piece = jnp.concatenate([shard.reshape(-1, LANES) for shard in shards[part]])
+        mats += unpack_pieces(place, gather_pieces(piece, devices), shapes[part], devices)
+    return mats
+
+
+def scatter_grads(grads, shapes, devices):
+    if not whole_rows(shapes, devices):
+        return [
+            lax.psum_scatter(grad.reshape(-1), "dp", scatter_dimension=0, tiled=True)
+            for grad in grads
+        ]
+    place = lax.axis_index("dp").astype(jnp.int32).reshape(1)
+    sums = []
+    for part in (slice(0, 4), slice(4, 7)):
+        pieces = scatter_pieces(*pack_grads(place, grads[part], shapes[part], devices), devices)
+        start = 0
+        for rows, wide in shapes[part]:
+            count = rows * wide // (devices * LANES)
+            sums.append(pieces[start : start + count].reshape(-1))
+            start += count
+    return sums
+
+
+def sum_all(field, devices):
+    plane, line = masks_of(devices)
+    for masks in ((0, CORE_MASK), plane, line):
+        field = tree_sum([field] + [swap(field, mask, devices) for mask in masks[1:]])
+    return field
 
 
 def body(tokens, cotangent, w_query, w_key, w_value, w_out, w_gate, w_up, w_down, norm_gains):
@@ -82,18 +337,12 @@
     scale_factor = HEAD_DIM ** (-0.5)
     gain_f = norm_gains.astype(jnp.float32)
     shards = (w_query, w_key, w_value, w_out, w_gate, w_up, w_down)
-    wq_mat, wk_mat, wv_mat, wo_mat, wg_mat, wu_mat, wd_mat = unpack(
-        (
-            lax.all_gather(shards[0], "dp", axis=0, tiled=True),
-            lax.all_gather(shards[1], "dp", axis=0, tiled=True),
-            lax.all_gather(shards[2], "dp", axis=0, tiled=True),
-            lax.all_gather(shards[3], "dp", axis=0, tiled=True),
-            lax.all_gather(shards[4], "dp", axis=0, tiled=True),
-            lax.all_gather(shards[5], "dp", axis=0, tiled=True),
-            lax.all_gather(shards[6], "dp", axis=0, tiled=True),
-        ),
-        model_width,
-    )
+    devices = lax.axis_size("dp")
+    widths = [shards[at].shape[0] * devices // model_width for at in range(6)]
+    shapes = [(model_width, wide) for wide in widths] + [
+        (shards[6].shape[0] * devices // model_width, model_width)
+    ]
+    wq_mat, wk_mat, wv_mat, wo_mat, wg_mat, wu_mat, wd_mat = gather_weights(shards, shapes, devices)
     resid_in = tokens.astype(jnp.float32)
     normed_one, rms_one = normalize(resid_in, gain_f[0])
     normed_one = normed_one.astype(jnp.bfloat16)
@@ -141,18 +390,6 @@
     hidden = (activated * upward).astype(jnp.bfloat16)
     ffn_out = jnp.dot(hidden, wd_mat, preferred_element_type=jnp.float32)
     output = (middle + ffn_out).astype(jnp.bfloat16)
-    wq_mat, wk_mat, wv_mat, wo_mat, wg_mat, wu_mat, wd_mat = unpack(
-        (
-            lax.all_gather(shards[0], "dp", axis=0, tiled=True),
-            lax.all_gather(shards[1], "dp", axis=0, tiled=True),
-            lax.all_gather(shards[2], "dp", axis=0, tiled=True),
-            lax.all_gather(shards[3], "dp", axis=0, tiled=True),
-            lax.all_gather(shards[4], "dp", axis=0, tiled=True),
-            lax.all_gather(shards[5], "dp", axis=0, tiled=True),
-            lax.all_gather(shards[6], "dp", axis=0, tiled=True),
-        ),
-        model_width,
-    )
     grad_down = outer_prod(hidden, cotangent)
     hidden_back = times_transposed(cotangent, wd_mat)
     gate_back = (hidden_back * upward * sigmoid_g * (1.0 + gate * (1.0 - sigmoid_g))).astype(
@@ -226,16 +463,9 @@
     )
     norm_one_back, gain_one = normalize_back(one_back, resid_in, rms_one, gain_f[0])
     input_grad = (mid_back + norm_one_back).astype(jnp.bfloat16)
-    all_parts = (
-        lax.psum_scatter(grad_query.reshape(-1), "dp", scatter_dimension=0, tiled=True),
-        lax.psum_scatter(grad_key.reshape(-1), "dp", scatter_dimension=0, tiled=True),
-        lax.psum_scatter(grad_value.reshape(-1), "dp", scatter_dimension=0, tiled=True),
-        lax.psum_scatter(grad_out.reshape(-1), "dp", scatter_dimension=0, tiled=True),
-        lax.psum_scatter(grad_gate.reshape(-1), "dp", scatter_dimension=0, tiled=True),
-        lax.psum_scatter(grad_up.reshape(-1), "dp", scatter_dimension=0, tiled=True),
-        lax.psum_scatter(grad_down.reshape(-1), "dp", scatter_dimension=0, tiled=True),
-    )
-    gain_grad = lax.psum(jnp.stack([gain_one, gain_two]), "dp")
+    grads = (grad_query, grad_key, grad_value, grad_out, grad_gate, grad_up, grad_down)
+    all_parts = scatter_grads(grads, shapes, devices)
+    gain_grad = sum_all(jnp.stack([gain_one, gain_two]), devices)
     return (output, input_grad) + tuple(all_parts) + (gain_grad,)
 
 

time: 687 us -> 327 us (0.48)
  blocking collectives: 207 us -> 0 us
  waiting for transfers between devices: 200 us -> 53.2 us
  starting transfers between devices: 0.15 us -> 41 us
  local copies, waits for them, and re-layouts: 63.5 us -> 25.1 us
  Pallas kernels: 0 us -> 32.8 us
  between operations: 15.1 us -> 1.73 us
  matrix products: 127 us -> 114 us
  other arithmetic: 67 us -> 54.7 us
    unnamed x5 -> x0, waiting for transfers between devices: 200 us -> none
    all_gather x4 -> x0, blocking collectives: 168 us -> none  [the longest x1 44.7 us: body(): lax.all_gather(shards[2], 'dp', axis=0, tiled=True)]
    ppermute x0 -> x35, waiting for transfers between devices: none -> 53.2 us  [swap(): lax.ppermute(field, 'dp', [(place, place ^ mask) for place in range(devic...]
    ppermute x0 -> x35, starting transfers between devices: none -> 41 us  [swap(): lax.ppermute(field, 'dp', [(place, place ^ mask) for place in range(devic...]
    reshape x14 -> x3, local copies, waits for them, and re-layouts: 42 us -> 1.99 us  [scatter_grads(): sums.append(pieces[start:start + count].reshape(-1))]
    psum x1 -> x0, blocking collectives: 38.8 us -> none  [body(): gain_grad = lax.psum(jnp.stack([gain_one, gain_two]), 'dp')]
    pallas_call x0 -> x4, Pallas kernels: none -> 32.8 us  [the longest x2 17.6 us: pack_grads(): pl.pallas_call(functools.partial(pack_kernel, devices=devices, shapes=sha...]
    all_gather x4 -> x0, other arithmetic: 11.4 us -> none  [the longest x1 4.85 us: body(): lax.all_gather(shards[0], 'dp', axis=0, tiled=True)]
  transfers between devices with their start and end apart: 4 -> 35, of which waited for: 1 -> 11; matrix products, arithmetic and copies ran while one was open for 15% -> 21% of each run, Pallas kernels for 0% -> 4%
where the time goes in v1:
time: 327 us; the launch traced here: 323 us
  matrix products  114 us (35%)
  other arithmetic  54.7 us (17%)
  waiting for transfers between devices  53.2 us (16%)
  starting transfers between devices  41 us (13%)
  Pallas kernels  32.8 us (10%)
  local copies, waits for them, and re-layouts  25.1 us (8%)
    ppermute x35, waiting for transfers between devices, swap(): lax.ppermute(field, 'dp', [(place, place ^ mask) for place in range(devic...  53.2 us
    ppermute x35, starting transfers between devices, swap(): lax.ppermute(field, 'dp', [(place, place ^ mask) for place in range(devic...  41 us
    another operation x6, other arithmetic  25.9 us
    dot_general x7, matrix products, outer_prod(): lax.dot_general(left, right, (((0,), (0,)), ((), ())), preferred_element_...  19.6 us
    dot_general x2, matrix products, body(): jnp.einsum('sqkgd,stkd->skgqt', back_blk, values_part, preferred_element_...  17.7 us
    pallas_call x2, Pallas kernels, pack_grads(): pl.pallas_call(functools.partial(pack_kernel, devices=devices, shapes=sha...  17.6 us
    dot_general x7, matrix products, times_transposed(): lax.dot_general(left, matrix, (((1,), (1,)), ((), ())), preferred_element...  15.5 us
    pallas_call x2, Pallas kernels, unpack_pieces(): pl.pallas_call(functools.partial(unpack_kernel, devices=devices, shapes=s...  15.2 us
  transfers between devices with their start and end apart: 35, of which 11 were waited for; matrix products, arithmetic and copies ran while one was open for 21% of the time, Pallas kernels for 4%

profile of v1, /device:TPU:0, one launch (start us, length us, event | category | flops | bytes accessed | tf_op | source)
XLA Modules:
  0.0 323.0 jit_solution(10387740475650778211)
XLA Ops:
  0.7 1.7 fusion.104
  2.3 4.0 %collective-permute-start.8 = (bf16[729,128]{1,0:T(8,128)(2,1)}, bf16[729,128]{1,0:T(8,128)(2,1)S(1)}, u32[]{:S(2)}, u32[]{:S(2)}) collective-permute-start(bf16[729,128]{1,0:T(8,128)(2,1)} %get-tuple-element.70), channel_id=1, source_target_pairs={{0,16},{1,17},{2,18},{3,19},{4,20},{5,21},{6,22},{7,23},{8,24},{9,... | collective-permute-start | bytes 559880 | tf_op jit(solution)/shard_map/ppermute | solution.py:31
  6.4 1.6 collective-permute-start.7
  7.9 1.4 constant_dynamic-update-slice_fusion.6
  9.3 1.9 collective-permute-start.1
  11.2 2.5 collective-permute-start
  15.5 1.5 fusion.29
  21.3 1.6 collective-permute-start.4
  22.9 1.5 collective-permute-start.3
  24.4 1.4 constant_dynamic-update-slice_fusion.5
  27.0 1.8 collective-permute-done.3
  30.7 4.0 %collective-permute-done.5 = bf16[4,135,128]{2,1,0:T(8,128)(2,1)S(1)} collective-permute-done((bf16[4,135,128]{2,1,0:T(8,128)(2,1)S(1)}, bf16[4,135,128]{2,1,0:T(8,128)(2,1)S(1)}, u32[]{:S(2)}, u32[]{:S(2)}) %collective-permute-start.5) | collective-permute-done | bytes 138272 | tf_op jit(solution)/shard_map/ppermute | solution.py:31
  39.5 2.3 collective-permute-start.11
  44.4 5.3 %unpack.2 = (bf16[576,576]{1,0:T(8,128)(2,1)}, bf16[576,192]{1,0:T(8,128)(2,1)}, bf16[576,192]{1,0:T(8,128)(2,1)}) custom-call(s32[1]{0:T(128)} %bitcast.place_ref, bf16[16,135,128]{2,1,0:T(8,128)(2,1)} %constant_dynamic-update-slice_fusion.own_ref, bf16[16,135,128]{2,1,0:T(8,128)(2,1)} %copy.33.got_ref), custom_call_target="tpu_custom_call" | custom-call | tf_op jit(solution)/shard_map/unpack/pallas_call | solution.py:183
  49.8 1.6 convolution_convert_fusion.1
  54.2 1.7 fusion.117
  57.3 2.3 copy-done
  59.5 2.6 fusion.53
  62.1 8.6 %fusion.116 = (f32[3,3,512]{2,1,0:T(4,128)S(1)}, f32[1,3,3,512,1024]{3,4,2,1,0:T(8,128)}) fusion(bf16[1,1024,3,3,32]{1,4,3,2,0:T(8,128)(2,1)S(1)} %bitcast.312, bf16[1,1024,3,3,32]{1,4,3,2,0:T(8,128)(2,1)S(1)} %bitcast.308, bf16[1024,3,32]{0,2,1:T(8,128)(2,1)S(1)} %bitcast.324, bf16[1024,3,32]{0,2,1:T(8,128)(2,1)S(1)} %bitcast.322, ...), kind=kOutput, calls=%fused_computation.203 | convolution fusion | flops 620097024 | bytes 20989952 | tf_op jit(solution)/shard_map/sqkgd,stkd->skgqt/dot_general | solution.py:278
  70.7 8.9 %fusion.3 = f32[3,3,512]{2,1,0:T(4,128)S(1)} fusion(f32[1,3,3,512,1024]{3,4,2,1,0:T(8,128)} %get-tuple-element.83, f32[3,3,512]{2,1,0:T(4,128)S(1)} %get-tuple-element.82), kind=kLoop, calls=%fused_computation.9 | loop fusion | flops 9432576 | bytes 18911232 | tf_op jit(solution)/shard_map/reduce_sum | solution.py:369
  85.2 8.2 %fusion.56 = bf16[1,512,3,3,64]{1,4,3,2,0:T(8,128)(2,1)S(1)} fusion(bf16[1024,3,64,1]{0,2,3,1:T(8,128)(2,1)S(1)} %bitcast.333, f32[3,3,512]{2,1,0:T(4,128)S(1)} %fusion.3, f32[1,3,3,512,1024]{3,4,2,1,0:T(8,128)} %get-tuple-element.83, f32[3,3,512]{2,1,0:T(4,128)S(1)} %get-tuple-element.82), kind=kOutput, calls=%fused_computation.87 | convolution fusion | flops 618430464 | bytes 19894272 | tf_op jit(solution)/shard_map/skgqt,stkd->sqkgd/dot_general | solution.py:372
  94.2 2.4 copy.43.got_ref
  96.6 9.9 %unpack.3 = (bf16[576,576]{1,0:T(8,128)(2,1)}, bf16[576,1536]{1,0:T(8,128)(2,1)}, bf16[576,1536]{1,0:T(8,128)(2,1)}, bf16[1536,576]{1,0:T(8,128)(2,1)}) custom-call(s32[1]{0:T(128)} %bitcast.place_ref, bf16[16,729,128]{2,1,0:T(8,128)(2,1)} %copy-done.2, bf16[16,729,128]{2,1,0:T(8,128)(2,1)} %copy.43.got_ref), custom_call_target="tpu_custom_call" | custom-call | tf_op jit(solution)/shard_map/unpack/pallas_call | solution.py:183
  106.5 2.5 multiply_reduce_fusion.2
  109.0 4.7 %fusion.119 = f32[1536,1024]{0,1:T(8,128)} fusion(bf16[1536,576]{1,0:T(8,128)(2,1)S(1)} %copy-done.45, bf16[1024,576]{0,1:T(8,128)(2,1)S(1)} %copy-done.23), kind=kOutput, calls=%fused_computation.206 | convolution fusion | flops 1811939328 | bytes 9240576 | tf_op jit(solution)/shard_map/dot_general | solution.py:272
  115.2 2.7 fusion.118
  117.9 8.6 %fusion.19 = (bf16[1024,1536]{1,0:T(8,128)(2,1)S(1)}, bf16[1024,1536]{1,0:T(8,128)(2,1)S(1)}, bf16[1024,1536]{1,0:T(8,128)(2,1)}) fusion(f32[1536,1024]{0,1:T(8,128)} %fusion.119, f32[1024,1536]{1,0:T(8,128)S(1)} %fusion.118, bf16[1024,576]{0,1:T(8,128)(2,1)S(1)} %multiply_convert_fusion.1, bf16[576,1536]{1,0:T(8,128)(2,1)S(1)} %copy-done.48), kind=kOutput, calls=%fused_computation.32 | convolution fusion | flops 1835532288 | bytes 24969216 | tf_op jit(solution)/shard_map/dot_general | solution.py:387
  126.5 2.0 fusion.120
  128.5 3.8 %fusion.122.refs_1_ = f32[576,1536]{1,0:T(8,128)} fusion(bf16[1024,576]{0,1:T(8,128)(2,1)S(1)} %multiply_convert_fusion.1, bf16[1024,1536]{1,0:T(8,128)(2,1)S(1)} %get-tuple-element.42), kind=kOutput, calls=%fused_computation.209 | convolution fusion | flops 1811939328 | bytes 7864320 | tf_op jit(solution)/shard_map/dot_general | solution.py:266
  132.3 3.9 %fusion.121.refs_0_ = f32[576,1536]{1,0:T(8,128)} fusion(bf16[1024,576]{0,1:T(8,128)(2,1)S(1)} %multiply_convert_fusion.1, bf16[1024,1536]{1,0:T(8,128)(2,1)S(1)} %get-tuple-element.41), kind=kOutput, calls=%fused_computation.208 | convolution fusion | flops 1811939328 | bytes 7864320 | tf_op jit(solution)/shard_map/dot_general | solution.py:266
  136.2 2.5 multiply_reduce_fusion
  139.4 2.3 fusion.73.refs_3_
  143.2 2.3 fusion.65
  145.6 5.7 %fusion.9 = (f32[3,3,512]{2,1,0:T(4,128)}, f32[3,512,512,3]{2,1,3,0:T(8,128)}) fusion(f32[1,3,3,512,512]{3,4,2,1,0:T(8,128)S(1)} %bitcast.305, f32[3,3,512]{2,1,0:T(4,128)S(1)} %log_add_fusion.1, bf16[1,1024,3,3,64]{1,4,3,2,0:T(8,128)(2,1)S(1)} %bitcast.318, bf16[1,1024,3,64]{1,3,2,0:T(8,128)(2,1)S(1)} %bitcast.334), kind=kOutput, calls=%fused_computation.17 | convolution fusion | flops 309063168 | bytes 19703808 | tf_op jit(solution)/shard_map/sqkgd,stkd->skgqt/dot_general | solution.py:420
  151.2 11.2 %fusion.25 = bf16[3,3,512,512]{2,3,1,0:T(8,128)(2,1)} fusion(f32[3,512,512,3]{2,1,3,0:T(8,128)} %get-tuple-element.92, f32[1,3,3,512,512]{3,4,2,1,0:T(8,128)} %copy-done, f32[3,3,512]{2,1,0:T(4,128)} %get-tuple-element.91, f32[3,3,512]{2,1,0:T(4,128)} %copy-done.34), kind=kLoop, calls=%fused_computation.45 | loop fusion | flops 9437184 | bytes 23629824 | tf_op jit(solution)/shard_map/reshape.56
  162.4 4.2 %fusion.69 = f32[1,512,3,64]{1,3,2,0:T(8,128)S(1)} fusion(bf16[3,3,512,512]{2,3,1,0:T(8,128)(2,1)} %fusion.25, bf16[1,1024,3,3,32]{1,4,3,2,0:T(8,128)(2,1)} %bitcast.309, bf16[1,1024,3,3,32]{1,4,3,2,0:T(8,128)(2,1)} %bitcast.313), kind=kOutput, calls=%fused_computation.93 | convolution fusion | flops 303267840 | bytes 6291456 | tf_op jit(solution)/shard_map/skgqt,sqkgd->stkd/dot_general | solution.py:432
  168.0 12.1 %fusion = (f32[3,3,512]{2,1,0:T(4,128)S(1)}, f32[3,1024,512,3]{2,1,3,0:T(8,128)}) fusion(f32[1,3,3,512,1024]{3,4,2,1,0:T(8,128)} %get-tuple-element.83, f32[3,3,512]{2,1,0:T(4,128)S(1)} %copy-done.35, bf16[1024,3,64,1]{0,2,3,1:T(8,128)(2,1)S(1)} %bitcast.335, bf16[1,1024,3,3,64]{1,4,3,2,0:T(8,128)(2,1)S(1)} %bitcast.319), kind=kOutput, calls=%fused_computation.3 | convolution fusion | flops 618130944 | bytes 38774784 | tf_op jit(solution)/shard_map/sqkgd,stkd->skgqt/dot_general | solution.py:420
  180.1 13.7 %fusion.8 = bf16[3,3,512,1024]{2,3,1,0:T(8,128)(2,1)S(1)} fusion(f32[3,1024,512,3]{2,1,3,0:T(8,128)} %get-tuple-element.90, f32[1,3,3,512,1024]{3,4,2,1,0:T(8,128)} %get-tuple-element.83, f32[3,3,512]{2,1,0:T(4,128)S(1)} %get-tuple-element.89, f32[3,3,512]{2,1,0:T(4,128)S(1)} %copy-done.35), kind=kLoop, calls=%fused_computation.13 | loop fusion | flops 18874368 | bytes 47222784 | tf_op jit(solution)/shard_map/reshape.74
  193.8 1.7 fusion.40
  197.2 2.3 fusion.109.refs_0_
  199.6 2.5 fusion.124
  202.1 2.9 fusion.52
  207.1 8.2 %fusion.62 = bf16[1,1024,3,64]{1,3,2,0:T(8,128)(2,1)S(1)} fusion(f32[1,3,3,512,1024]{3,4,2,1,0:T(8,128)} %get-tuple-element.83, f32[3,3,512]{2,1,0:T(4,128)S(1)} %copy-done.35, f32[1,512,3,64]{1,3,2,0:T(8,128)S(1)} %copy-done.21, bf16[1,1024,3,3,64]{1,4,3,2,0:T(8,128)(2,1)S(1)} %bitcast.320), kind=kOutput, calls=%fused_computation.89 | convolution fusion | flops 613810176 | bytes 20275200 | tf_op jit(solution)/shard_map/skgqt,sqkgd->stkd/dot_general | solution.py:437
  216.7 4.6 %fusion.123.refs_2_ = f32[1536,576]{1,0:T(8,128)} fusion(bf16[1024,1536]{1,0:T(8,128)(2,1)S(1)} %copy-done.52, bf16[1024,576]{0,1:T(8,128)(2,1)S(1)} %copy-done.24), kind=kOutput, calls=%fused_computation.210 | convolution fusion | flops 1811939328 | bytes 7864320 | tf_op jit(solution)/shard_map/dot_general | solution.py:266
  221.3 10.0 %pack.3 = (bf16[16,648,128]{2,1,0:T(8,128)(2,1)}, bf16[16,648,128]{2,1,0:T(8,128)(2,1)}) custom-call(s32[1]{0:T(128)} %bitcast.place_ref, f32[576,1536]{1,0:T(8,128)} %fusion.121.refs_0_, f32[576,1536]{1,0:T(8,128)} %fusion.122.refs_1_, f32[1536,576]{1,0:T(8,128)} %fusion.123.refs_2_), custom_call_target="tpu_custom_call" | custom-call | tf_op jit(solution)/shard_map/pack/pallas_call | solution.py:219
  231.8 7.6 %pack.2 = (bf16[16,216,128]{2,1,0:T(8,128)(2,1)}, bf16[16,216,128]{2,1,0:T(8,128)(2,1)}) custom-call(s32[1]{0:T(128)} %bitcast.place_ref, f32[576,576]{1,0:T(8,128)} %fusion.109.refs_0_, f32[576,192]{1,0:T(8,128)} %fusion.107.refs_1_, f32[576,192]{1,0:T(8,128)} %fusion.105.refs_2_, f32[576,576]{1,0:T(8,128)} %fusion.73.refs_3_), custom_call_target="tpu_custom_call" | custom-call | tf_op jit(solution)/shard_map/pack/pallas_call | solution.py:219
  239.5 2.2 fusion.38
  242.8 3.1 add_convert_fusion
  246.0 2.9 collective-permute-start.31
  249.5 1.6 fusion.35
  251.1 1.4 collective-permute-done.29
  252.6 3.1 collective-permute-start.34
  261.5 4.1 %collective-permute-done.17 = bf16[4,216,128]{2,1,0:T(8,128)(2,1)S(1)} collective-permute-done((bf16[4,216,128]{2,1,0:T(8,128)(2,1)S(1)}, bf16[4,216,128]{2,1,0:T(8,128)(2,1)S(1)}, u32[]{:S(2)}, u32[]{:S(2)}) %collective-permute-start.17) | collective-permute-done | bytes 221216 | tf_op jit(solution)/shard_map/ppermute | solution.py:31
  265.5 2.2 collective-permute-done.16
  268.9 2.4 collective-permute-start.20
  271.5 2.4 add_convert_fusion.4
  276.1 1.4 collective-permute-start.22
  278.2 14.5 %collective-permute-done.24 = bf16[4,648,128]{2,1,0:T(8,128)(2,1)S(1)} collective-permute-done((bf16[4,648,128]{2,1,0:T(8,128)(2,1)S(1)}, bf16[4,648,128]{2,1,0:T(8,128)(2,1)S(1)}, u32[]{:S(2)}, u32[]{:S(2)}) %collective-permute-start.24) | collective-permute-done | bytes 663584 | tf_op jit(solution)/shard_map/ppermute | solution.py:31
  292.7 11.2 %collective-permute-done.23 = bf16[4,648,128]{2,1,0:T(8,128)(2,1)S(1)} collective-permute-done((bf16[4,648,128]{2,1,0:T(8,128)(2,1)S(1)}, bf16[4,648,128]{2,1,0:T(8,128)(2,1)S(1)}, u32[]{:S(2)}, u32[]{:S(2)}) %collective-permute-start.23) | collective-permute-done | bytes 663584 | tf_op jit(solution)/shard_map/ppermute | solution.py:31
  304.2 1.8 collective-permute-start.25
  306.0 2.4 collective-permute-start.27
  309.0 1.7 collective-permute-done.25
  310.7 6.5 %collective-permute-done.27 = bf16[648,128]{1,0:T(8,128)(2,1)S(1)} collective-permute-done((bf16[648,128]{1,0:T(8,128)(2,1)S(1)}, bf16[648,128]{1,0:T(8,128)(2,1)S(1)}, u32[]{:S(2)}, u32[]{:S(2)}) %collective-permute-start.27) | collective-permute-done | bytes 165920 | tf_op jit(solution)/shard_map/ppermute | solution.py:31
  317.1 4.8 %collective-permute-done.26 = bf16[648,128]{1,0:T(8,128)(2,1)S(1)} collective-permute-done((bf16[648,128]{1,0:T(8,128)(2,1)S(1)}, bf16[648,128]{1,0:T(8,128)(2,1)S(1)}, u32[]{:S(2)}, u32[]{:S(2)}) %collective-permute-start.26) | collective-permute-done | bytes 165920 | tf_op jit(solution)/shard_map/ppermute | solution.py:31
  (224 shorter events, 51.0 us)
Async XLA Ops:
  0.6 17.0 %copy-start.44 = (bf16[2,576]{1,0:T(2,128)(2,1)S(1)}, bf16[2,576]{1,0:T(2,128)(2,1)}, u32[]{:S(2)}) copy-start(bf16[2,576]{1,0:T(2,128)(2,1)} %param.19) | copy-start | bytes 6916
  2.3 34.3 %collective-permute-start.8 = (bf16[729,128]{1,0:T(8,128)(2,1)}, bf16[729,128]{1,0:T(8,128)(2,1)S(1)}, u32[]{:S(2)}, u32[]{:S(2)}) collective-permute-start(bf16[729,128]{1,0:T(8,128)(2,1)} %get-tuple-element.70), channel_id=1, source_target_pairs={{0,16},{1,17},{2,18},{3,19},{4,20},{5,21},{6,22},{7,23},{8,24},{9,... | collective-permute-start | bytes 559880 | tf_op jit(solution)/shard_map/ppermute | solution.py:31
  6.4 30.3 %collective-permute-start.7 = (bf16[729,128]{1,0:T(8,128)(2,1)}, bf16[729,128]{1,0:T(8,128)(2,1)}, u32[]{:S(2)}, u32[]{:S(2)}) collective-permute-start(bf16[729,128]{1,0:T(8,128)(2,1)} %get-tuple-element.70), channel_id=1, source_target_pairs={{0,8},{1,9},{2,10},{3,11},{4,12},{5,13},{6,14},{7,15},{8,0},{9,1},... | collective-permute-start | bytes 559880 | tf_op jit(solution)/shard_map/ppermute | solution.py:31
  9.3 10.7 %collective-permute-start.2 = (bf16[135,128]{1,0:T(8,128)(2,1)}, bf16[135,128]{1,0:T(8,128)(2,1)S(1)}, u32[]{:S(2)}, u32[]{:S(2)}) collective-permute-start(bf16[135,128]{1,0:T(8,128)(2,1)} %get-tuple-element.40), channel_id=1, source_target_pairs={{0,24},{1,25},{2,26},{3,27},{4,28},{5,29},{6,30},{7,31},{8,16},{9,... | collective-permute-start | bytes 103688 | tf_op jit(solution)/shard_map/ppermute | solution.py:31
  9.3 11.2 %collective-permute-start.1 = (bf16[135,128]{1,0:T(8,128)(2,1)}, bf16[135,128]{1,0:T(8,128)(2,1)S(1)}, u32[]{:S(2)}, u32[]{:S(2)}) collective-permute-start(bf16[135,128]{1,0:T(8,128)(2,1)} %get-tuple-element.40), channel_id=1, source_target_pairs={{0,16},{1,17},{2,18},{3,19},{4,20},{5,21},{6,22},{7,23},{8,24},{9,... | collective-permute-start | bytes 103688 | tf_op jit(solution)/shard_map/ppermute | solution.py:31
  11.2 9.3 %collective-permute-start = (bf16[135,128]{1,0:T(8,128)(2,1)}, bf16[135,128]{1,0:T(8,128)(2,1)}, u32[]{:S(2)}, u32[]{:S(2)}) collective-permute-start(bf16[135,128]{1,0:T(8,128)(2,1)} %get-tuple-element.40), channel_id=1, source_target_pairs={{0,8},{1,9},{2,10},{3,11},{4,12},{5,13},{6,14},{7,15},{8,0},{9,1},... | collective-permute-start | bytes 103688 | tf_op jit(solution)/shard_map/ppermute | solution.py:31
  17.6 34.4 %copy-start.39 = (f32[1024]{0:T(1024)}, f32[1024]{0:T(1024)S(1)}, u32[]{:S(2)}) copy-start(f32[1024]{0:T(1024)S(1)} %get-tuple-element.76) | copy-start | bytes 12292
  18.8 34.6 %copy-start.13 = (f32[1024,32]{0,1:T(8,128)}, f32[1024,32]{0,1:T(8,128)S(1)}, u32[]{:S(2)}) copy-start(f32[1024,32]{0,1:T(8,128)S(1)} %get-tuple-element.81) | copy-start | bytes 393220
  20.0 32.0 %copy-start.41 = (f32[576]{0:T(1024)}, f32[576]{0:T(1024)S(1)}, u32[]{:S(2)}) copy-start(f32[576]{0:T(1024)S(1)} %get-tuple-element.37) | copy-start | bytes 6916
  20.1 16.6 %copy-start.31 = (bf16[1,729,128]{2,1,0:T(8,128)(2,1)S(1)}, bf16[1,729,128]{2,1,0:T(8,128)(2,1)}, u32[]{:S(2)}) copy-start(bf16[1,729,128]{2,1,0:T(8,128)(2,1)} %get-tuple-element.69) | copy-start | bytes 559876
  20.1 16.6 %collective-permute-start.9 = (bf16[729,128]{1,0:T(8,128)(2,1)}, bf16[729,128]{1,0:T(8,128)(2,1)S(1)}, u32[]{:S(2)}, u32[]{:S(2)}) collective-permute-start(bf16[729,128]{1,0:T(8,128)(2,1)} %get-tuple-element.70), channel_id=1, source_target_pairs={{0,24},{1,25},{2,26},{3,27},{4,28},{5,29},{6,30},{7,31},{8,16},{9,... | collective-permute-start | bytes 559880 | tf_op jit(solution)/shard_map/ppermute | solution.py:31
  21.3 8.7 %collective-permute-start.4 = (bf16[4,135,128]{2,1,0:T(8,128)(2,1)S(1)}, bf16[4,135,128]{2,1,0:T(8,128)(2,1)S(1)}, u32[]{:S(2)}, u32[]{:S(2)}) collective-permute-start(bf16[4,135,128]{2,1,0:T(8,128)(2,1)S(1)} %pad_maximum_fusion.8), channel_id=1, source_target_pairs={{0,4},{1,5},{2,6},{3,7},{4,0},{5,1},{6,2},{7,3},{8,12},{9,13},{10,... | collective-permute-start | bytes 414728 | tf_op jit(solution)/shard_map/ppermute | solution.py:31
  22.9 5.9 %collective-permute-start.3 = (bf16[4,135,128]{2,1,0:T(8,128)(2,1)S(1)}, bf16[4,135,128]{2,1,0:T(8,128)(2,1)S(1)}, u32[]{:S(2)}, u32[]{:S(2)}) collective-permute-start(bf16[4,135,128]{2,1,0:T(8,128)(2,1)S(1)} %pad_maximum_fusion.8), channel_id=1, source_target_pairs={{0,2},{1,3},{2,0},{3,1},{4,6},{5,7},{6,4},{7,5},{8,10},{9,11},{10,... | collective-permute-start | bytes 414728 | tf_op jit(solution)/shard_map/ppermute | solution.py:31
  28.8 6.0 %collective-permute-start.5 = (bf16[4,135,128]{2,1,0:T(8,128)(2,1)S(1)}, bf16[4,135,128]{2,1,0:T(8,128)(2,1)S(1)}, u32[]{:S(2)}, u32[]{:S(2)}) collective-permute-start(bf16[4,135,128]{2,1,0:T(8,128)(2,1)S(1)} %pad_maximum_fusion.8), channel_id=1, source_target_pairs={{0,6},{1,7},{2,4},{3,5},{4,2},{5,3},{6,0},{7,1},{8,14},{9,15},{10,... | collective-permute-start | bytes 414728 | tf_op jit(solution)/shard_map/ppermute | solution.py:31
  36.5 6.9 %collective-permute-start.6 = (bf16[16,135,128]{2,0,1:T(8,128)(2,1)S(1)}, bf16[16,135,128]{2,0,1:T(8,128)(2,1)S(1)}, u32[]{:S(2)}, u32[]{:S(2)}) collective-permute-start(bf16[16,135,128]{2,0,1:T(8,128)(2,1)S(1)} %copy.32), channel_id=1, source_target_pairs={{0,1},{1,0},{2,3},{3,2},{4,5},{5,4},{6,7},{7,6},{8,9},{9,8},{10,11... | collective-permute-start | bytes 1658888 | tf_op jit(solution)/shard_map/ppermute | solution.py:31
  37.7 12.1 %copy-start.3 = (bf16[1024,576]{0,1:T(8,128)(2,1)S(1)}, bf16[1024,576]{0,1:T(8,128)(2,1)}, u32[]{:S(2)}) copy-start(bf16[1024,576]{0,1:T(8,128)(2,1)} %param.10) | copy-start | bytes 3538948
  38.9 43.3 %collective-permute-start.12 = (bf16[4,729,128]{2,0,1:T(4,128)(2,1)}, bf16[4,729,128]{2,0,1:T(4,128)(2,1)}, u32[]{:S(2)}, u32[]{:S(2)}) collective-permute-start(bf16[4,729,128]{2,0,1:T(4,128)(2,1)} %copy.36), channel_id=1, source_target_pairs={{0,6},{1,7},{2,4},{3,5},{4,2},{5,3},{6,0},{7,1},{8,14},{9,15},{10,... | collective-permute-start | bytes 2239496 | tf_op jit(solution)/shard_map/ppermute | solution.py:31
  39.5 41.4 %collective-permute-start.11 = (bf16[4,729,128]{2,0,1:T(4,128)(2,1)}, bf16[4,729,128]{2,0,1:T(4,128)(2,1)}, u32[]{:S(2)}, u32[]{:S(2)}) collective-permute-start(bf16[4,729,128]{2,0,1:T(4,128)(2,1)} %copy.36), channel_id=1, source_target_pairs={{0,4},{1,5},{2,6},{3,7},{4,0},{5,1},{6,2},{7,3},{8,12},{9,13},{10,... | collective-permute-start | bytes 2239496 | tf_op jit(solution)/shard_map/ppermute | solution.py:31
  41.9 37.7 %collective-permute-start.10 = (bf16[4,729,128]{2,0,1:T(4,128)(2,1)}, bf16[4,729,128]{2,0,1:T(4,128)(2,1)}, u32[]{:S(2)}, u32[]{:S(2)}) collective-permute-start(bf16[4,729,128]{2,0,1:T(4,128)(2,1)} %copy.36), channel_id=1, source_target_pairs={{0,2},{1,3},{2,0},{3,1},{4,6},{5,7},{6,4},{7,5},{8,10},{9,11},{10,... | collective-permute-start | bytes 2239496 | tf_op jit(solution)/shard_map/ppermute | solution.py:31
  51.4 5.8 %copy-start.26 = (bf16[1024,192]{0,1:T(8,128)(2,1)}, bf16[1024,192]{0,1:T(8,128)(2,1)S(1)}, u32[]{:S(2)}) copy-start(bf16[1024,192]{0,1:T(8,128)(2,1)S(1)} %convolution_convert_fusion.1) | copy-start | bytes 1179652
  53.4 8.7 %copy-start.17 = (bf16[1,1024,3,32]{1,3,2,0:T(8,128)(2,1)}, bf16[1,1024,3,32]{1,3,2,0:T(8,128)(2,1)S(1)}, u32[]{:S(2)}) copy-start(bf16[1,1024,3,32]{1,3,2,0:T(8,128)(2,1)S(1)} %get-tuple-element.61) | copy-start | bytes 589828
  53.4 8.7 %copy-start.19 = (bf16[1,1024,3,32]{1,3,2,0:T(8,128)(2,1)}, bf16[1,1024,3,32]{1,3,2,0:T(8,128)(2,1)S(1)}, u32[]{:S(2)}) copy-start(bf16[1,1024,3,32]{1,3,2,0:T(8,128)(2,1)S(1)} %get-tuple-element.62) | copy-start | bytes 589828
  53.8 8.3 %copy-start.7 = (bf16[1,1024,9,32]{1,3,2,0:T(8,128)(2,1)}, bf16[1,1024,9,32]{1,3,2,0:T(8,128)(2,1)S(1)}, u32[]{:S(2)}) copy-start(bf16[1,1024,9,32]{1,3,2,0:T(8,128)(2,1)S(1)} %get-tuple-element.53) | copy-start | bytes 1769476
  53.8 8.3 %copy-start.9 = (bf16[1,1024,9,32]{1,3,2,0:T(8,128)(2,1)}, bf16[1,1024,9,32]{1,3,2,0:T(8,128)(2,1)S(1)}, u32[]{:S(2)}) copy-start(bf16[1,1024,9,32]{1,3,2,0:T(8,128)(2,1)S(1)} %get-tuple-element.54) | copy-start | bytes 1769476
  55.9 3.6 %copy-start = (f32[1,3,3,512,512]{3,4,2,1,0:T(8,128)}, f32[1,3,3,512,512]{3,4,2,1,0:T(8,128)S(1)}, u32[]{:S(2)}) copy-start(f32[1,3,3,512,512]{3,4,2,1,0:T(8,128)S(1)} %get-tuple-element.85) | copy-start | bytes 28311556
  85.1 9.1 %collective-permute-start.13 = (bf16[16,729,128]{2,0,1:T(8,128)(2,1)S(1)}, bf16[16,729,128]{2,0,1:T(8,128)(2,1)S(1)}, u32[]{:S(2)}, u32[]{:S(2)}) collective-permute-start(bf16[16,729,128]{2,0,1:T(8,128)(2,1)S(1)} %copy.42), channel_id=1, source_target_pairs={{0,1},{1,0},{2,3},{3,2},{4,5},{5,4},{6,7},{7,6},{8,9},{9,8},{10,11... | collective-permute-start | bytes 8957960 | tf_op jit(solution)/shard_map/ppermute | solution.py:31
  85.2 8.2 %copy-start.32 = (bf16[1,512,3,3,64]{1,4,3,2,0:T(8,128)(2,1)S(1)}, bf16[1,512,3,3,64]{1,4,3,2,0:T(8,128)(2,1)}, u32[]{:S(2)}) copy-start(bf16[1,512,3,3,64]{1,4,3,2,0:T(8,128)(2,1)} %fusion.53) | copy-start | bytes 1769476
  93.6 52.0 %copy-start.34 = (f32[3,3,512]{2,1,0:T(4,128)}, f32[3,3,512]{2,1,0:T(4,128)S(1)}, u32[]{:S(2)}) copy-start(f32[3,3,512]{2,1,0:T(4,128)S(1)} %log_add_fusion.1) | copy-start | bytes 55300
  96.6 9.9 %copy-start.4 = (bf16[1024,576]{0,1:T(8,128)(2,1)S(1)}, bf16[1024,576]{0,1:T(8,128)(2,1)}, u32[]{:S(2)}) copy-start(bf16[1024,576]{0,1:T(8,128)(2,1)} %param.10) | copy-start | bytes 3538948
  109.0 29.7 %copy-start.5 = (f32[1024,576]{0,1:T(8,128)}, f32[1024,576]{0,1:T(8,128)S(1)}, u32[]{:S(2)}) copy-start(f32[1024,576]{0,1:T(8,128)S(1)} %get-tuple-element.87) | copy-start | bytes 7077892
  138.7 4.1 %slice-start = ((s8[9437184]{0:T(1024)(128)(4,1)}), s8[4194304]{0:T(1024)(128)(4,1)S(1)}, s32[]{:S(2)}) async-start(s8[9437184]{0:T(1024)(128)(4,1)} %bitcast.304), calls=%async_computation | async-start | bytes 8388608
  138.7 4.2 %slice-start.1 = ((s8[9437184]{0:T(1024)(128)(4,1)}), s8[4194304]{0:T(1024)(128)(4,1)S(1)}, s32[]{:S(2)}) async-start(s8[9437184]{0:T(1024)(128)(4,1)} %bitcast.304), calls=%async_computation.1 | async-start | bytes 8388608
  139.4 3.9 %slice-start.2 = ((s8[9437184]{0:T(1024)(128)(4,1)}), s8[1048576]{0:T(1024)(128)(4,1)S(1)}, s32[]{:S(2)}) async-start(s8[9437184]{0:T(1024)(128)(4,1)} %bitcast.304), calls=%async_computation.2 | async-start | bytes 2097152
  162.4 4.2 %copy-start.1 = (bf16[3,3,512,512]{2,3,1,0:T(8,128)(2,1)S(1)}, bf16[3,3,512,512]{2,3,1,0:T(8,128)(2,1)}, u32[]{:S(2)}) copy-start(bf16[3,3,512,512]{2,3,1,0:T(8,128)(2,1)} %fusion.25) | copy-start | bytes 14155780
  162.4 4.2 %copy-start.18 = (bf16[1,1024,3,32]{1,3,2,0:T(8,128)(2,1)S(1)}, bf16[1,1024,3,32]{1,3,2,0:T(8,128)(2,1)}, u32[]{:S(2)}) copy-start(bf16[1,1024,3,32]{1,3,2,0:T(8,128)(2,1)} %copy-done.17) | copy-start | bytes 589828
  162.4 4.2 %copy-start.20 = (bf16[1,1024,3,32]{1,3,2,0:T(8,128)(2,1)S(1)}, bf16[1,1024,3,32]{1,3,2,0:T(8,128)(2,1)}, u32[]{:S(2)}) copy-start(bf16[1,1024,3,32]{1,3,2,0:T(8,128)(2,1)} %copy-done.19) | copy-start | bytes 589828
  207.1 9.6 %copy-start.52 = (bf16[1024,1536]{1,0:T(8,128)(2,1)S(1)}, bf16[1024,1536]{1,0:T(8,128)(2,1)}, u32[]{:S(2)}) copy-start(bf16[1024,1536]{1,0:T(8,128)(2,1)} %get-tuple-element.43) | copy-start | bytes 9437188
  215.2 6.0 %copy-start.22 = (bf16[1,1024,3,64]{1,3,2,0:T(8,128)(2,1)}, bf16[1,1024,3,64]{1,3,2,0:T(8,128)(2,1)S(1)}, u32[]{:S(2)}) copy-start(bf16[1,1024,3,64]{1,3,2,0:T(8,128)(2,1)S(1)} %fusion.62) | copy-start | bytes 1179652
  231.3 8.2 %copy-start.16 = (f32[1024,576]{0,1:T(8,128)S(1)}, f32[1024,576]{0,1:T(8,128)}, u32[]{:S(2)}) copy-start(f32[1024,576]{0,1:T(8,128)} %fusion.124) | copy-start | bytes 7077892
  231.3 40.2 %collective-permute-start.21 = (bf16[16,648,128]{2,1,0:T(8,128)(2,1)}, bf16[16,648,128]{2,1,0:T(8,128)(2,1)}, u32[]{:S(2)}, u32[]{:S(2)}) collective-permute-start(bf16[16,648,128]{2,1,0:T(8,128)(2,1)} %get-tuple-element.31), channel_id=1, source_target_pairs={{0,1},{1,0},{2,3},{3,2},{4,5},{5,4},{6,7},{7,6},{8,9},{9,8},{10,11... | collective-permute-start | bytes 7962632 | tf_op jit(solution)/shard_map/ppermute | solution.py:31
  239.4 3.4 %copy-start.53 = (bf16[1024,1536]{1,0:T(8,128)(2,1)S(1)}, bf16[1024,1536]{1,0:T(8,128)(2,1)}, u32[]{:S(2)}) copy-start(bf16[1024,1536]{1,0:T(8,128)(2,1)} %get-tuple-element.43) | copy-start | bytes 9437188
  239.4 17.6 %collective-permute-start.14 = (bf16[16,216,128]{2,1,0:T(8,128)(2,1)}, bf16[16,216,128]{2,1,0:T(8,128)(2,1)S(1)}, u32[]{:S(2)}, u32[]{:S(2)}) collective-permute-start(bf16[16,216,128]{2,1,0:T(8,128)(2,1)} %get-tuple-element.29), channel_id=1, source_target_pairs={{0,1},{1,0},{2,3},{3,2},{4,5},{5,4},{6,7},{7,6},{8,9},{9,8},{10,11... | collective-permute-start | bytes 2654216 | tf_op jit(solution)/shard_map/ppermute | solution.py:31
  241.7 7.8 %copy-start.43 = (f32[1024]{0:T(1024)S(1)}, f32[1024]{0:T(1024)}, u32[]{:S(2)}) copy-start(f32[1024]{0:T(1024)} %get-tuple-element.75) | copy-start | bytes 12292
  241.7 4.2 %collective-permute-start.28 = (f32[2,576]{1,0:T(2,128)S(1)}, f32[2,576]{1,0:T(2,128)S(1)}, u32[]{:S(2)}, u32[]{:S(2)}) collective-permute-start(f32[2,576]{1,0:T(2,128)S(1)} %pad_maximum_fusion.10), channel_id=1, source_target_pairs={{0,1},{1,0},{2,3},{3,2},{4,5},{5,4},{6,7},{7,6},{8,9},{9,8},{10,11... | collective-permute-start | bytes 13832 | tf_op jit(solution)/shard_map/ppermute | solution.py:31
  245.9 5.2 %collective-permute-start.30 = (f32[2,576]{1,0:T(2,128)S(1)}, f32[2,576]{1,0:T(2,128)S(1)}, u32[]{:S(2)}, u32[]{:S(2)}) collective-permute-start(f32[2,576]{1,0:T(2,128)S(1)} %fusion.101), channel_id=1, source_target_pairs={{0,4},{1,5},{2,6},{3,7},{4,0},{5,1},{6,2},{7,3},{8,12},{9,13},{10,... | collective-permute-start | bytes 13832 | tf_op jit(solution)/shard_map/ppermute | solution.py:31
  246.0 5.1 %collective-permute-start.31 = (f32[2,576]{1,0:T(2,128)S(1)}, f32[2,576]{1,0:T(2,128)S(1)}, u32[]{:S(2)}, u32[]{:S(2)}) collective-permute-start(f32[2,576]{1,0:T(2,128)S(1)} %fusion.101), channel_id=1, source_target_pairs={{0,6},{1,7},{2,4},{3,5},{4,2},{5,3},{6,0},{7,1},{8,14},{9,15},{10,... | collective-permute-start | bytes 13832 | tf_op jit(solution)/shard_map/ppermute | solution.py:31
  249.0 3.6 %collective-permute-start.29 = (f32[2,576]{1,0:T(2,128)S(1)}, f32[2,576]{1,0:T(2,128)S(1)}, u32[]{:S(2)}, u32[]{:S(2)}) collective-permute-start(f32[2,576]{1,0:T(2,128)S(1)} %fusion.101), channel_id=1, source_target_pairs={{0,2},{1,3},{2,0},{3,1},{4,6},{5,7},{6,4},{7,5},{8,10},{9,11},{10,... | collective-permute-start | bytes 13832 | tf_op jit(solution)/shard_map/ppermute | solution.py:31
  249.5 7.6 %copy-start.30 = (bf16[16,216,128]{2,1,0:T(8,128)(2,1)S(1)}, bf16[16,216,128]{2,1,0:T(8,128)(2,1)}, u32[]{:S(2)}) copy-start(bf16[16,216,128]{2,1,0:T(8,128)(2,1)} %get-tuple-element.28) | copy-start | bytes 2654212
  251.1 20.4 %copy-start.15 = (bf16[16,648,128]{2,1,0:T(8,128)(2,1)S(1)}, bf16[16,648,128]{2,1,0:T(8,128)(2,1)}, u32[]{:S(2)}) copy-start(bf16[16,648,128]{2,1,0:T(8,128)(2,1)} %get-tuple-element.30) | copy-start | bytes 7962628
  252.6 5.7 %collective-permute-start.34 = (f32[2,576]{1,0:T(2,128)S(1)}, f32[2,576]{1,0:T(2,128)S(1)}, u32[]{:S(2)}, u32[]{:S(2)}) collective-permute-start(f32[2,576]{1,0:T(2,128)S(1)} %add_add_fusion.2), channel_id=1, source_target_pairs={{0,24},{1,25},{2,26},{3,27},{4,28},{5,29},{6,30},{7,31},{8,16},{9,... | collective-permute-start | bytes 13832 | tf_op jit(solution)/shard_map/ppermute | solution.py:31
  255.7 4.5 %collective-permute-start.33 = (f32[2,576]{1,0:T(2,128)S(1)}, f32[2,576]{1,0:T(2,128)S(1)}, u32[]{:S(2)}, u32[]{:S(2)}) collective-permute-start(f32[2,576]{1,0:T(2,128)S(1)} %add_add_fusion.2), channel_id=1, source_target_pairs={{0,16},{1,17},{2,18},{3,19},{4,20},{5,21},{6,22},{7,23},{8,24},{9,... | collective-permute-start | bytes 13832 | tf_op jit(solution)/shard_map/ppermute | solution.py:31
  255.7 5.1 %collective-permute-start.32 = (f32[2,576]{1,0:T(2,128)S(1)}, f32[2,576]{1,0:T(2,128)S(1)}, u32[]{:S(2)}, u32[]{:S(2)}) collective-permute-start(f32[2,576]{1,0:T(2,128)S(1)} %add_add_fusion.2), channel_id=1, source_target_pairs={{0,8},{1,9},{2,10},{3,11},{4,12},{5,13},{6,14},{7,15},{8,0},{9,1},... | collective-permute-start | bytes 13832 | tf_op jit(solution)/shard_map/ppermute | solution.py:31
  257.3 8.2 %collective-permute-start.17 = (bf16[4,216,128]{2,1,0:T(8,128)(2,1)S(1)}, bf16[4,216,128]{2,1,0:T(8,128)(2,1)S(1)}, u32[]{:S(2)}, u32[]{:S(2)}) collective-permute-start(bf16[4,216,128]{2,1,0:T(8,128)(2,1)S(1)} %get-tuple-element.56), channel_id=1, source_target_pairs={{0,6},{1,7},{2,4},{3,5},{4,2},{5,3},{6,0},{7,1},{8,14},{9,15},{10,... | collective-permute-start | bytes 663560 | tf_op jit(solution)/shard_map/ppermute | solution.py:31
  258.3 9.5 %collective-permute-start.16 = (bf16[4,216,128]{2,1,0:T(8,128)(2,1)S(1)}, bf16[4,216,128]{2,1,0:T(8,128)(2,1)S(1)}, u32[]{:S(2)}, u32[]{:S(2)}) collective-permute-start(bf16[4,216,128]{2,1,0:T(8,128)(2,1)S(1)} %get-tuple-element.57), channel_id=1, source_target_pairs={{0,4},{1,5},{2,6},{3,7},{4,0},{5,1},{6,2},{7,3},{8,12},{9,13},{10,... | collective-permute-start | bytes 663560 | tf_op jit(solution)/shard_map/ppermute | solution.py:31
  260.2 7.5 %collective-permute-start.15 = (bf16[4,216,128]{2,1,0:T(8,128)(2,1)S(1)}, bf16[4,216,128]{2,1,0:T(8,128)(2,1)S(1)}, u32[]{:S(2)}, u32[]{:S(2)}) collective-permute-start(bf16[4,216,128]{2,1,0:T(8,128)(2,1)S(1)} %get-tuple-element.58), channel_id=1, source_target_pairs={{0,2},{1,3},{2,0},{3,1},{4,6},{5,7},{6,4},{7,5},{8,10},{9,11},{10,... | collective-permute-start | bytes 663560 | tf_op jit(solution)/shard_map/ppermute | solution.py:31
  267.8 8.3 %collective-permute-start.18 = (bf16[216,128]{1,0:T(8,128)(2,1)S(1)}, bf16[216,128]{1,0:T(8,128)(2,1)S(1)}, u32[]{:S(2)}, u32[]{:S(2)}) collective-permute-start(bf16[216,128]{1,0:T(8,128)(2,1)S(1)} %get-tuple-element.63), channel_id=1, source_target_pairs={{0,8},{1,9},{2,10},{3,11},{4,12},{5,13},{6,14},{7,15},{8,0},{9,1},... | collective-permute-start | bytes 165896 | tf_op jit(solution)/shard_map/ppermute | solution.py:31
  268.9 8.6 %collective-permute-start.20 = (bf16[216,128]{1,0:T(8,128)(2,1)S(1)}, bf16[216,128]{1,0:T(8,128)(2,1)S(1)}, u32[]{:S(2)}, u32[]{:S(2)}) collective-permute-start(bf16[216,128]{1,0:T(8,128)(2,1)S(1)} %get-tuple-element.64), channel_id=1, source_target_pairs={{0,24},{1,25},{2,26},{3,27},{4,28},{5,29},{6,30},{7,31},{8,16},{9,... | collective-permute-start | bytes 165896 | tf_op jit(solution)/shard_map/ppermute | solution.py:31
  271.3 6.2 %collective-permute-start.19 = (bf16[216,128]{1,0:T(8,128)(2,1)S(1)}, bf16[216,128]{1,0:T(8,128)(2,1)S(1)}, u32[]{:S(2)}, u32[]{:S(2)}) collective-permute-start(bf16[216,128]{1,0:T(8,128)(2,1)S(1)} %get-tuple-element.65), channel_id=1, source_target_pairs={{0,16},{1,17},{2,18},{3,19},{4,20},{5,21},{6,22},{7,23},{8,24},{9,... | collective-permute-start | bytes 165896 | tf_op jit(solution)/shard_map/ppermute | solution.py:31
  273.9 18.8 %collective-permute-start.24 = (bf16[4,648,128]{2,1,0:T(8,128)(2,1)S(1)}, bf16[4,648,128]{2,1,0:T(8,128)(2,1)S(1)}, u32[]{:S(2)}, u32[]{:S(2)}) collective-permute-start(bf16[4,648,128]{2,1,0:T(8,128)(2,1)S(1)} %get-tuple-element.45), channel_id=1, source_target_pairs={{0,6},{1,7},{2,4},{3,5},{4,2},{5,3},{6,0},{7,1},{8,14},{9,15},{10,... | collective-permute-start | bytes 1990664 | tf_op jit(solution)/shard_map/ppermute | solution.py:31
  275.2 28.7 %collective-permute-start.23 = (bf16[4,648,128]{2,1,0:T(8,128)(2,1)S(1)}, bf16[4,648,128]{2,1,0:T(8,128)(2,1)S(1)}, u32[]{:S(2)}, u32[]{:S(2)}) collective-permute-start(bf16[4,648,128]{2,1,0:T(8,128)(2,1)S(1)} %get-tuple-element.46), channel_id=1, source_target_pairs={{0,4},{1,5},{2,6},{3,7},{4,0},{5,1},{6,2},{7,3},{8,12},{9,13},{10,... | collective-permute-start | bytes 1990664 | tf_op jit(solution)/shard_map/ppermute | solution.py:31
  276.1 27.8 %collective-permute-start.22 = (bf16[4,648,128]{2,1,0:T(8,128)(2,1)S(1)}, bf16[4,648,128]{2,1,0:T(8,128)(2,1)S(1)}, u32[]{:S(2)}, u32[]{:S(2)}) collective-permute-start(bf16[4,648,128]{2,1,0:T(8,128)(2,1)S(1)} %get-tuple-element.47), channel_id=1, source_target_pairs={{0,2},{1,3},{2,0},{3,1},{4,6},{5,7},{6,4},{7,5},{8,10},{9,11},{10,... | collective-permute-start | bytes 1990664 | tf_op jit(solution)/shard_map/ppermute | solution.py:31
  304.2 6.5 %collective-permute-start.25 = (bf16[648,128]{1,0:T(8,128)(2,1)S(1)}, bf16[648,128]{1,0:T(8,128)(2,1)S(1)}, u32[]{:S(2)}, u32[]{:S(2)}) collective-permute-start(bf16[648,128]{1,0:T(8,128)(2,1)S(1)} %get-tuple-element.48), channel_id=1, source_target_pairs={{0,8},{1,9},{2,10},{3,11},{4,12},{5,13},{6,14},{7,15},{8,0},{9,1},... | collective-permute-start | bytes 497672 | tf_op jit(solution)/shard_map/ppermute | solution.py:31
  306.0 11.2 %collective-permute-start.27 = (bf16[648,128]{1,0:T(8,128)(2,1)S(1)}, bf16[648,128]{1,0:T(8,128)(2,1)S(1)}, u32[]{:S(2)}, u32[]{:S(2)}) collective-permute-start(bf16[648,128]{1,0:T(8,128)(2,1)S(1)} %get-tuple-element.49), channel_id=1, source_target_pairs={{0,24},{1,25},{2,26},{3,27},{4,28},{5,29},{6,30},{7,31},{8,16},{9,... | collective-permute-start | bytes 497672 | tf_op jit(solution)/shard_map/ppermute | solution.py:31
  308.3 13.6 %collective-permute-start.26 = (bf16[648,128]{1,0:T(8,128)(2,1)S(1)}, bf16[648,128]{1,0:T(8,128)(2,1)S(1)}, u32[]{:S(2)}, u32[]{:S(2)}) collective-permute-start(bf16[648,128]{1,0:T(8,128)(2,1)S(1)} %get-tuple-element.50), channel_id=1, source_target_pairs={{0,16},{1,17},{2,18},{3,19},{4,20},{5,21},{6,22},{7,23},{8,24},{9,... | collective-permute-start | bytes 497672 | tf_op jit(solution)/shard_map/ppermute | solution.py:31
  (28 other events, 52.8 us)

commit v2 on v1

--- a/solution.py
+++ b/solution.py
@@ -31,13 +31,6 @@
     return lax.ppermute(field, "dp", [(place, place ^ mask) for place in range(devices)])
 
 
-def gather_pieces(piece, devices):
-    plane, line = masks_of(devices)
-    held = jnp.stack([piece] + [swap(piece, mask, devices) for mask in line[1:]])
-    held = jnp.concatenate([held] + [swap(held, mask, devices) for mask in plane[1:]])
-    return (held, swap(held, CORE_MASK, devices))
-
-
 def tree_sum(terms):
     while len(terms) > 1:
         terms = [terms[at] + terms[at + 1] for at in range(0, len(terms), 2)]
@@ -46,23 +39,6 @@
 
 def widen(field):
     return field.astype(jnp.float32)
-
-
-def scatter_pieces(kept, sent, devices):
-    plane, line = masks_of(devices)
-    got = swap(sent, CORE_MASK, devices)
-    block = kept.shape[0] // len(plane)
-    parts = [
-        (widen(kept[at * block : (at + 1) * block]) + widen(got[at * block : (at + 1) * block])).astype(jnp.bfloat16)
-        for at in range(len(plane))
-    ]
-    arrived = [swap(part, mask, devices) for part, mask in zip(parts[1:], plane[1:])]
-    parts = [
-        tree_sum([widen(term[at]) for term in [parts[0]] + arrived]).astype(jnp.bfloat16)
-        for at in range(len(line))
-    ]
-    arrived = [swap(part, mask, devices) for part, mask in zip(parts[1:], line[1:])]
-    return tree_sum([widen(term) for term in [parts[0]] + arrived])
 
 
 def slot_mask(core, slot, devices):
@@ -229,6 +205,161 @@
     )(place, *grads)
 
 
+BLOCK = 256
+
+
+def dot_nt(left, right):
+    return lax.dot_general(
+        left, right, (((1,), (1,)), ((), ())), preferred_element_type=jnp.float32
+    )
+
+
+def dot_tn(left, right):
+    return lax.dot_general(
+        left, right, (((0,), (0,)), ((), ())), preferred_element_type=jnp.float32
+    )
+
+
+def dot_nn(left, right):
+    return jnp.dot(left, right, preferred_element_type=jnp.float32)
+
+
+def attend_kernel(query_ref, keys_ref, values_ref, mixed_ref, total_ref, *, head, group):
+    length = query_ref.shape[0]
+    keys = keys_ref[:, head * HEAD_DIM : (head + 1) * HEAD_DIM]
+    values = values_ref[:, head * HEAD_DIM : (head + 1) * HEAD_DIM]
+    lower = lax.broadcasted_iota(jnp.int32, (BLOCK, BLOCK), 0) >= lax.broadcasted_iota(
+        jnp.int32, (BLOCK, BLOCK), 1
+    )
+    lane = lax.broadcasted_iota(jnp.int32, (BLOCK, LANES), 1)
+    for start in range(0, length, BLOCK):
+        mixed, totals_row = [], jnp.zeros((BLOCK, LANES), jnp.float32)
+        for member in range(group):
+            at = (head * group + member) * HEAD_DIM
+            query = query_ref[start : start + BLOCK, at : at + HEAD_DIM]
+            diagonal = jnp.where(lower, dot_nt(query, keys[start : start + BLOCK]), NEG_BIG)
+            maxima = jnp.max(diagonal, 1, keepdims=True)
+            if start:
+                before = dot_nt(query, keys[:start])
+                maxima = jnp.maximum(maxima, jnp.max(before, 1, keepdims=True))
+            expo = jnp.exp(diagonal - maxima)
+            totals = jnp.sum(expo, 1, keepdims=True)
+            result = dot_nn(expo.astype(jnp.bfloat16), values[start : start + BLOCK])
+            if start:
+                expo = jnp.exp(before - maxima)
+                totals = totals + jnp.sum(expo, 1, keepdims=True)
+                result = result + dot_nn(expo.astype(jnp.bfloat16), values[:start])
+            mixed.append(result / totals)
+            totals_row = jnp.where(lane == member, maxima + jnp.log(totals), totals_row)
+        mixed_ref[start : start + BLOCK, :] = jnp.concatenate(mixed, 1).astype(jnp.bfloat16)
+        total_ref[start : start + BLOCK, :] = totals_row
+
+
+def attend(query, keys, values, head, group):
+    length = query.shape[0]
+    return pl.pallas_call(
+        functools.partial(attend_kernel, head=head, group=group),
+        out_shape=[
+            jax.ShapeDtypeStruct((length, group * HEAD_DIM), jnp.bfloat16),
+            jax.ShapeDtypeStruct((length, LANES), jnp.float32),
+        ],
+        in_specs=[pl.BlockSpec(memory_space=pltpu.VMEM)] * 3,
+        out_specs=[pl.BlockSpec(memory_space=pltpu.VMEM)] * 2,
+        compiler_params=pltpu.CompilerParams(vmem_limit_bytes=VMEM_LIMIT),
+        cost_estimate=pl.CostEstimate(
+            flops=12 * 10**9, bytes_accessed=4 * 10**6, transcendentals=2 * 10**6
+        ),
+        name="attend",
+    )(query, keys, values)
+
+
+def attend_back_kernel(
+    query_ref, keys_ref, values_ref, back_ref, mixed_ref, total_ref,
+    query_back_ref, key_back_ref, queries, backs, totals, deltas, query_sum, key_sum, value_sum,
+    *, head, group,
+):
+    length = query_ref.shape[0]
+    ones = jnp.ones((8, HEAD_DIM), jnp.float32)
+    totals[...] = total_ref[...].T[:8]
+    for member in range(group):
+        at = (head * group + member) * HEAD_DIM
+        queries[member] = query_ref[:, at : at + HEAD_DIM]
+        back = back_ref[:, at : at + HEAD_DIM]
+        backs[member] = back
+        product = back.astype(jnp.float32) * mixed_ref[
+            :, member * HEAD_DIM : (member + 1) * HEAD_DIM
+        ].astype(jnp.float32)
+        deltas[member] = lax.dot_general(
+            ones, product, (((1,), (1,)), ((), ())),
+            precision=lax.Precision.HIGHEST, preferred_element_type=jnp.float32,
+        )
+    keys_all = keys_ref[:, head * HEAD_DIM : (head + 1) * HEAD_DIM]
+    values_all = values_ref[:, head * HEAD_DIM : (head + 1) * HEAD_DIM]
+    upper = lax.broadcasted_iota(jnp.int32, (BLOCK, BLOCK), 0) <= lax.broadcasted_iota(
+        jnp.int32, (BLOCK, BLOCK), 1
+    )
+    for member in range(group):
+        total_row = totals[member : member + 1, :]
+        delta_row = deltas[member][0:1]
+        for start in range(0, length, BLOCK):
+            keys = keys_all[start : start + BLOCK]
+            values = values_all[start : start + BLOCK]
+            query = queries[member, start:, :]
+            back = backs[member, start:, :]
+            scores = dot_nt(keys, query)
+            probs = jnp.exp(scores - total_row[:, start:])
+            first = jnp.where(upper, probs[:, :BLOCK], 0.0)
+            probs = first if start + BLOCK == length else jnp.concatenate(
+                [first, probs[:, BLOCK:]], 1
+            )
+            prob_back = dot_nt(values, back)
+            score_back = (probs * (prob_back - delta_row[:, start:])).astype(jnp.bfloat16)
+            value_part = dot_nn(probs.astype(jnp.bfloat16), back)
+            key_part = dot_nn(score_back, query)
+            query_part = dot_tn(score_back, keys)
+            if member:
+                key_sum[start : start + BLOCK, :] += key_part
+                value_sum[start : start + BLOCK, :] += value_part
+            else:
+                key_sum[start : start + BLOCK, :] = key_part
+                value_sum[start : start + BLOCK, :] = value_part
+            if start:
+                query_sum[member, start:, :] += query_part
+            else:
+                query_sum[member] = query_part
+    query_back_ref[...] = (
+        jnp.concatenate([query_sum[member] for member in range(group)], 1) * HEAD_DIM ** (-0.5)
+    )
+    key_back_ref[...] = jnp.concatenate([key_sum[...], value_sum[...]], 1)
+
+
+def attend_back(query, keys, values, back, mixed, total, head, group):
+    length = query.shape[0]
+    return pl.pallas_call(
+        functools.partial(attend_back_kernel, head=head, group=group),
+        out_shape=[
+            jax.ShapeDtypeStruct((length, group * HEAD_DIM), jnp.float32),
+            jax.ShapeDtypeStruct((length, 2 * HEAD_DIM), jnp.float32),
+        ],
+        in_specs=[pl.BlockSpec(memory_space=pltpu.VMEM)] * 6,
+        out_specs=[pl.BlockSpec(memory_space=pltpu.VMEM)] * 2,
+        scratch_shapes=[
+            pltpu.VMEM((group, length, HEAD_DIM), jnp.bfloat16),
+            pltpu.VMEM((group, length, HEAD_DIM), jnp.bfloat16),
+            pltpu.VMEM((8, length), jnp.float32),
+            pltpu.VMEM((group, 8, length), jnp.float32),
+            pltpu.VMEM((group, length, HEAD_DIM), jnp.float32),
+            pltpu.VMEM((length, HEAD_DIM), jnp.float32),
+            pltpu.VMEM((length, HEAD_DIM), jnp.float32),
+        ],
+        compiler_params=pltpu.CompilerParams(vmem_limit_bytes=VMEM_LIMIT),
+        cost_estimate=pl.CostEstimate(
+            flops=24 * 10**9, bytes_accessed=8 * 10**6, transcendentals=2 * 10**6
+        ),
+        name="attend_back",
+    )(query, keys, values, back, mixed, total)
+
+
 def rotary_tables(length, head_dim):
     half_dim = head_dim // 2
     frequency = THETA ** (-(jnp.arange(half_dim, dtype=jnp.float32) * 2.0 / head_dim))
@@ -274,66 +405,130 @@
     )
 
 
-def block_scores(query_blk, keys_part, q_start):
-    scores = jnp.einsum(
-        "sqkgd,stkd->skgqt", query_blk, keys_part, preferred_element_type=jnp.float32
-    )
-    scores = scores * HEAD_DIM ** (-0.5)
-    row_index = q_start + jnp.arange(query_blk.shape[1])[:, None]
-    col_index = jnp.arange(keys_part.shape[1])[None, :]
-    return jnp.where(row_index >= col_index, scores, NEG_BIG)
-
-
 def whole_rows(shapes, devices):
-    return devices % 8 == 0 and all(
-        rows % (2 * devices) == 0 and wide % (LANES // 2) == 0 for rows, wide in shapes
-    ) and (devices & (devices - 1)) == 0
-
-
-def gather_weights(shards, shapes, devices):
-    if not whole_rows(shapes, devices):
-        return [
-            lax.all_gather(shard, "dp", axis=0, tiled=True).reshape(shape)
-            for shard, shape in zip(shards, shapes)
+    return (devices & (devices - 1)) == 0 and all(
+        rows % (8 * devices // 4) == 0 and rows * wide % (devices * LANES) == 0
+        for rows, wide in shapes
+    )
+
+
+def place_of():
+    return lax.axis_index("dp").astype(jnp.int32).reshape(1)
+
+
+class WeightGather:
+    def __init__(self, shards, shapes, devices):
+        self.shards, self.shapes, self.devices = shards, shapes, devices
+        self.stages = whole_rows(shapes, devices)
+        if self.stages:
+            self.held = jnp.concatenate([shard.reshape(-1, LANES) for shard in shards])
+
+    def line_stage(self, other):
+        if not self.stages:
+            return other
+        _, line = masks_of(self.devices)
+        self.held, other = tied(self.held, other)
+        self.arrived = [self.held] + [swap(self.held, mask, self.devices) for mask in line[1:]]
+        return other
+
+    def plane_stage(self, other):
+        if not self.stages:
+            return other
+        plane, _ = masks_of(self.devices)
+        self.held, other = tied(jnp.stack(self.arrived), other)
+        self.arrived = [self.held] + [swap(self.held, mask, self.devices) for mask in plane[1:]]
+        return other
+
+    def core_stage(self, other):
+        if not self.stages:
+            return other
+        self.arrived, other = tied(self.arrived, other)
+        self.held = jnp.concatenate(self.arrived)
+        self.got = swap(self.held, CORE_MASK, self.devices)
+        return other
+
+    def result(self):
+        if not self.stages:
+            return [
+                lax.all_gather(shard, "dp", axis=0, tiled=True).reshape(shape)
+                for shard, shape in zip(self.shards, self.shapes)
+            ]
+        return unpack_pieces(place_of(), (self.held, self.got), self.shapes, self.devices)
+
+
+def sum_all(field, devices):
+    step = 1
+    while step < devices:
+        field = field + swap(field, step, devices)
+        step *= 2
+    return field
+
+
+def tied(first, second):
+    return lax.optimization_barrier((first, second))
+
+
+class GradSum:
+    def __init__(self, grads, shapes, devices):
+        self.grads, self.shapes, self.devices = grads, shapes, devices
+        self.stages = whole_rows(shapes, devices)
+        if self.stages:
+            self.kept, self.sent = pack_grads(place_of(), grads, shapes, devices)
+
+    def core_stage(self, other):
+        if not self.stages:
+            return other
+        (self.kept, self.sent), other = tied((self.kept, self.sent), other)
+        self.got = swap(self.sent, CORE_MASK, self.devices)
+        return other
+
+    def plane_stage(self, other):
+        if not self.stages:
+            return other
+        plane, _ = masks_of(self.devices)
+        block = self.kept.shape[0] // len(plane)
+        cuts = [slice(at * block, (at + 1) * block) for at in range(len(plane))]
+        parts = [(widen(self.kept[cut]) + widen(self.got[cut])).astype(jnp.bfloat16) for cut in cuts]
+        self.parts, other = tied(parts, other)
+        self.arrived = [
+            swap(part, mask, self.devices) for part, mask in zip(self.parts[1:], plane[1:])
         ]
-    place = lax.axis_index("dp").astype(jnp.int32).reshape(1)
-    mats = []
-    for part in (slice(0, 3), slice(3, 7)):
-        piece = jnp.concatenate([shard.reshape(-1, LANES) for shard in shards[part]])
-        mats += unpack_pieces(place, gather_pieces(piece, devices), shapes[part], devices)
-    return mats
-
-
-def scatter_grads(grads, shapes, devices):
-    if not whole_rows(shapes, devices):
-        return [
-            lax.psum_scatter(grad.reshape(-1), "dp", scatter_dimension=0, tiled=True)
-            for grad in grads
+        return other
+
+    def line_stage(self, other):
+        if not self.stages:
+            return other
+        _, line = masks_of(self.devices)
+        terms = [self.parts[0]] + self.arrived
+        parts = [
+            tree_sum([widen(term[at]) for term in terms]).astype(jnp.bfloat16)
+            for at in range(len(line))
         ]
-    place = lax.axis_index("dp").astype(jnp.int32).reshape(1)
-    sums = []
-    for part in (slice(0, 4), slice(4, 7)):
-        pieces = scatter_pieces(*pack_grads(place, grads[part], shapes[part], devices), devices)
-        start = 0
-        for rows, wide in shapes[part]:
-            count = rows * wide // (devices * LANES)
+        self.parts, other = tied(parts, other)
+        self.arrived = [
+            swap(part, mask, self.devices) for part, mask in zip(self.parts[1:], line[1:])
+        ]
+        return other
+
+    def result(self):
+        if not self.stages:
+            return [
+                lax.psum_scatter(grad.reshape(-1), "dp", scatter_dimension=0, tiled=True)
+                for grad in self.grads
+            ]
+        pieces = tree_sum([widen(term) for term in [self.parts[0]] + self.arrived])
+        sums, start = [], 0
+        for rows, wide in self.shapes:
+            count = rows * wide // (self.devices * LANES)
             sums.append(pieces[start : start + count].reshape(-1))
             start += count
-    return sums
-
-
-def sum_all(field, devices):
-    plane, line = masks_of(devices)
-    for masks in ((0, CORE_MASK), plane, line):
-        field = tree_sum([field] + [swap(field, mask, devices) for mask in masks[1:]])
-    return field
+        return sums
 
 
 def body(tokens, cotangent, w_query, w_key, w_value, w_out, w_gate, w_up, w_down, norm_gains):
     model_width = tokens.shape[1]
     seq_count = tokens.shape[0] // LENGTH
     group_size = HEADS // KV_HEADS
-    block_rows = min(512, LENGTH)
     scale_factor = HEAD_DIM ** (-0.5)
     gain_f = norm_gains.astype(jnp.float32)
     shards = (w_query, w_key, w_value, w_out, w_gate, w_up, w_down)
@@ -342,7 +537,13 @@
     shapes = [(model_width, wide) for wide in widths] + [
         (shards[6].shape[0] * devices // model_width, model_width)
     ]
-    wq_mat, wk_mat, wv_mat, wo_mat, wg_mat, wu_mat, wd_mat = gather_weights(shards, shapes, devices)
+    first = WeightGather(shards[:3], shapes[:3], devices)
+    second = WeightGather(shards[3:], shapes[3:], devices)
+    tokens = first.line_stage(tokens)
+    tokens = first.plane_stage(tokens)
+    tokens = second.line_stage(tokens)
+    tokens = first.core_stage(tokens)
+    wq_mat, wk_mat, wv_mat = first.result()
     resid_in = tokens.astype(jnp.float32)
     normed_one, rms_one = normalize(resid_in, gain_f[0])
     normed_one = normed_one.astype(jnp.bfloat16)
@@ -350,35 +551,25 @@
     key_lin = jnp.dot(normed_one, wk_mat, preferred_element_type=jnp.float32)
     value_lin = jnp.dot(normed_one, wv_mat, preferred_element_type=jnp.float32)
     cosine, sine = rotary_tables(LENGTH, HEAD_DIM)
+    tokens_here = seq_count * LENGTH
     query_rot = rotate_heads(
         query_lin.reshape(seq_count, LENGTH, HEADS, HEAD_DIM), cosine, sine
-    ).astype(jnp.bfloat16)
-    query_rot = query_rot.reshape(seq_count, LENGTH, KV_HEADS, group_size, HEAD_DIM)
-    key_rot = rotate_heads(
-        key_lin.reshape(seq_count, LENGTH, KV_HEADS, HEAD_DIM), cosine, sine
-    ).astype(jnp.bfloat16)
-    values = value_lin.astype(jnp.bfloat16).reshape(seq_count, LENGTH, KV_HEADS, HEAD_DIM)
-    mixed_blocks = []
-    total_blocks = []
-    for index in range(LENGTH // block_rows):
-        q_start = index * block_rows
-        key_end = q_start + block_rows
-        scores = block_scores(query_rot[:, q_start:key_end], key_rot[:, :key_end], q_start)
-        maxima = jnp.max(scores, -1, keepdims=True)
-        expo = jnp.exp(scores - maxima)
-        totals = jnp.sum(expo, -1, keepdims=True)
-        probs = (expo / totals).astype(jnp.bfloat16)
-        mixed_blocks.append(
-            jnp.einsum(
-                "skgqt,stkd->sqkgd", probs, values[:, :key_end], preferred_element_type=jnp.float32
-            )
-        )
-        total_blocks.append((maxima + jnp.log(totals))[..., 0])
-    mixed = (
-        jnp.concatenate(mixed_blocks, 1)
-        .reshape(seq_count * LENGTH, model_width)
+    ).reshape(tokens_here, -1)
+    query_rot = (query_rot.astype(jnp.bfloat16).astype(jnp.float32) * scale_factor).astype(
+        jnp.bfloat16
+    )
+    key_rot = (
+        rotate_heads(key_lin.reshape(seq_count, LENGTH, KV_HEADS, HEAD_DIM), cosine, sine)
+        .reshape(tokens_here, -1)
         .astype(jnp.bfloat16)
     )
+    values = value_lin.astype(jnp.bfloat16)
+    values = second.plane_stage(values)
+    attended = [attend(query_rot, key_rot, values, head, group_size) for head in range(2)]
+    values, attended = second.core_stage((values, attended))
+    attended.append(attend(query_rot, key_rot, values, 2, group_size))
+    wo_mat, wg_mat, wu_mat, wd_mat = second.result()
+    mixed = jnp.concatenate([part for part, _ in attended], 1)
     attn_out = jnp.dot(mixed, wo_mat, preferred_element_type=jnp.float32)
     middle = resid_in + attn_out
     normed_two, rms_two = normalize(middle, gain_f[1])
@@ -404,46 +595,25 @@
     mid_low = mid_back.astype(jnp.bfloat16)
     grad_out = outer_prod(mixed, mid_low)
     mixed_back = times_transposed(mid_low, wo_mat).astype(jnp.bfloat16)
-    mixed_back = mixed_back.reshape(seq_count, LENGTH, KV_HEADS, group_size, HEAD_DIM)
-    query_parts = []
-    key_acc = jnp.zeros((seq_count, LENGTH, KV_HEADS, HEAD_DIM), jnp.float32)
-    value_acc = jnp.zeros((seq_count, LENGTH, KV_HEADS, HEAD_DIM), jnp.float32)
-    for index in range(LENGTH // block_rows):
-        q_start = index * block_rows
-        key_end = q_start + block_rows
-        query_blk = query_rot[:, q_start:key_end]
-        keys_part = key_rot[:, :key_end]
-        values_part = values[:, :key_end]
-        back_blk = mixed_back[:, q_start:key_end]
-        scores = block_scores(query_blk, keys_part, q_start)
-        probs = jnp.exp(scores - total_blocks[index][..., None])
-        prob_back = jnp.einsum(
-            "sqkgd,stkd->skgqt", back_blk, values_part, preferred_element_type=jnp.float32
-        )
-        centred = prob_back - jnp.sum(probs * prob_back, -1, keepdims=True)
-        score_back = (probs * centred).astype(jnp.bfloat16)
-        query_parts.append(
-            jnp.einsum(
-                "skgqt,stkd->sqkgd", score_back, keys_part, preferred_element_type=jnp.float32
-            )
-            * scale_factor
-        )
-        key_part = (
-            jnp.einsum(
-                "skgqt,sqkgd->stkd", score_back, query_blk, preferred_element_type=jnp.float32
-            )
-            * scale_factor
-        )
-        value_part = jnp.einsum(
-            "skgqt,sqkgd->stkd",
-            probs.astype(jnp.bfloat16),
-            back_blk,
-            preferred_element_type=jnp.float32,
-        )
-        padding = ((0, 0), (0, LENGTH - key_end), (0, 0), (0, 0))
-        key_acc = key_acc + jnp.pad(key_part, padding)
-        value_acc = value_acc + jnp.pad(value_part, padding)
-    rot_query_back = jnp.concatenate(query_parts, 1).reshape(seq_count, LENGTH, HEADS, HEAD_DIM)
+    feed_sum = GradSum((grad_gate, grad_up, grad_down), shapes[4:], devices)
+
+    def back_of(head, field):
+        part, total = attended[head]
+        return attend_back(query_rot, key_rot, values, field, part, total, head, group_size)
+
+    mixed_back = feed_sum.core_stage(mixed_back)
+    backs = [back_of(0, mixed_back)]
+    mixed_back, _ = tied(mixed_back, backs[0])
+    mixed_back = feed_sum.plane_stage(mixed_back)
+    backs += [back_of(head, mixed_back) for head in range(1, KV_HEADS)]
+    backs = feed_sum.line_stage(backs)
+    rot_query_back = jnp.concatenate([back for back, _ in backs], 1).reshape(
+        seq_count, LENGTH, HEADS, HEAD_DIM
+    )
+    key_acc = jnp.concatenate([back[:, :HEAD_DIM] for _, back in backs], 1).reshape(
+        seq_count, LENGTH, KV_HEADS, HEAD_DIM
+    )
+    value_acc = jnp.concatenate([back[:, HEAD_DIM:] for _, back in backs], 1)
     query_back = (
         rotate_heads(rot_query_back, cosine, -sine)
         .reshape(seq_count * LENGTH, model_width)
@@ -463,8 +633,11 @@
     )
     norm_one_back, gain_one = normalize_back(one_back, resid_in, rms_one, gain_f[0])
     input_grad = (mid_back + norm_one_back).astype(jnp.bfloat16)
-    grads = (grad_query, grad_key, grad_value, grad_out, grad_gate, grad_up, grad_down)
-    all_parts = scatter_grads(grads, shapes, devices)
+    mix_sum = GradSum((grad_query, grad_key, grad_value, grad_out), shapes[:4], devices)
+    input_grad = mix_sum.core_stage(input_grad)
+    input_grad = mix_sum.plane_stage(input_grad)
+    input_grad = mix_sum.line_stage(input_grad)
+    all_parts = mix_sum.result() + feed_sum.result()
     gain_grad = sum_all(jnp.stack([gain_one, gain_two]), devices)
     return (output, input_grad) + tuple(all_parts) + (gain_grad,)
 

time: 327 us -> 297 us (0.908)
  Pallas kernels: 32.8 us -> 86.7 us
  matrix products: 114 us -> 61.9 us
  other arithmetic: 54.7 us -> 19 us
  waiting for transfers between devices: 53.2 us -> 58.2 us
  starting transfers between devices: 41 us -> 36.9 us
    dot_general x12 -> x0, matrix products: 59.1 us -> none  [the longest x2 17.7 us: body(): jnp.einsum('sqkgd,stkd->skgqt', back_blk, values_part, preferred_element_...]
    pallas_call x0 -> x6, Pallas kernels: none -> 54.2 us  [the longest x3 32.4 us: attend_back(): pl.pallas_call(functools.partial(attend_back_kernel, head=head, group=gro...]
    another operation x9 -> x6, other arithmetic: 29.4 us -> 3.99 us
    reduce_sum x2 -> x0, other arithmetic: 10.2 us -> none  [body(): totals = jnp.sum(expo, -1, keepdims=True)]
    unnamed x124 -> x98, local copies, waits for them, and re-layouts: 14.3 us -> 6.09 us
    dot_general x7, matrix products: 15.5 us -> 22.7 us  [times_transposed(): lax.dot_general(left, matrix, (((1,), (1,)), ((), ())), preferred_element...]
    dot_general x1, matrix products: 8.56 us -> 2.66 us  [body(): upward = jnp.dot(normed_two, wu_mat, preferred_element_type=jnp.float32)]
    ppermute x35 -> x33, waiting for transfers between devices: 53.2 us -> 58.2 us  [swap(): lax.ppermute(field, 'dp', [(place, place ^ mask) for place in range(devic...]
  transfers between devices with their start and end apart: 35 -> 33, of which waited for: 11 -> 16; matrix products, arithmetic and copies ran while one was open for 21% -> 7% of each run, Pallas kernels for 4% -> 21%
where the time goes in v2:
time: 297 us; the launch traced here: 291 us
  Pallas kernels  86.7 us (29%)
  matrix products  61.9 us (21%)
  waiting for transfers between devices  58.2 us (20%)
  starting transfers between devices  36.9 us (12%)
  local copies, waits for them, and re-layouts  26.9 us (9%)
  other arithmetic  19 us (6%)
    ppermute x33, waiting for transfers between devices, swap(): lax.ppermute(field, 'dp', [(place, place ^ mask) for place in range(devic...  58.2 us
    ppermute x33, starting transfers between devices, swap(): lax.ppermute(field, 'dp', [(place, place ^ mask) for place in range(devic...  36.9 us
    pallas_call x3, Pallas kernels, attend_back(): pl.pallas_call(functools.partial(attend_back_kernel, head=head, group=gro...  32.4 us
    dot_general x7, matrix products, times_transposed(): lax.dot_general(left, matrix, (((1,), (1,)), ((), ())), preferred_element...  22.7 us
    pallas_call x3, Pallas kernels, attend(): pl.pallas_call(functools.partial(attend_kernel, head=head, group=group),...  21.8 us
    dot_general x7, matrix products, outer_prod(): lax.dot_general(left, right, (((0,), (0,)), ((), ())), preferred_element_...  20 us
    pallas_call x2, Pallas kernels, pack_grads(): pl.pallas_call(functools.partial(pack_kernel, devices=devices, shapes=sha...  17.5 us
    pallas_call x2, Pallas kernels, unpack_pieces(): pl.pallas_call(functools.partial(unpack_kernel, devices=devices, shapes=s...  15 us
  transfers between devices with their start and end apart: 33, of which 16 were waited for; matrix products, arithmetic and copies ran while one was open for 7% of the time, Pallas kernels for 21%

profile of v2, /device:TPU:0, one launch (start us, length us, event | category | flops | bytes accessed | tf_op | source)
XLA Modules:
  0.0 291.3 jit_solution(4487413169419100054)
XLA Ops:
  1.5 5.1 %collective-permute-start.2 = (bf16[135,128]{1,0:T(8,128)(2,1)S(1)}, bf16[135,128]{1,0:T(8,128)(2,1)S(1)}, u32[]{:S(2)}, u32[]{:S(2)}) collective-permute-start(bf16[135,128]{1,0:T(8,128)(2,1)S(1)} %pad_maximum_fusion.16), channel_id=1, source_target_pairs={{0,24},{1,25},{2,26},{3,27},{4,28},{5,29},{6,30},{7,31},{8,16},{9,... | collective-permute-start | bytes 103688 | tf_op jit(solution)/shard_map/ppermute | solution.py:31
  8.6 2.9 %collective-permute-done.1 = bf16[135,128]{1,0:T(8,128)(2,1)S(1)} collective-permute-done((bf16[135,128]{1,0:T(8,128)(2,1)S(1)}, bf16[135,128]{1,0:T(8,128)(2,1)S(1)}, u32[]{:S(2)}, u32[]{:S(2)}) %collective-permute-start.1) | collective-permute-done | bytes 34592 | tf_op jit(solution)/shard_map/ppermute | solution.py:31
  11.5 2.5 collective-permute-start.5
  20.9 1.6 collective-permute-start.8
  23.1 2.3 collective-permute-start.6
  26.3 4.2 %collective-permute-done.8 = bf16[729,128]{1,0:T(8,128)(2,1)S(1)} collective-permute-done((bf16[729,128]{1,0:T(8,128)(2,1)S(1)}, bf16[729,128]{1,0:T(8,128)(2,1)S(1)}, u32[]{:S(2)}, u32[]{:S(2)}) %collective-permute-start.8) | collective-permute-done | bytes 186656 | tf_op jit(solution)/shard_map/ppermute | solution.py:31
  30.5 10.1 %collective-permute-done.7 = bf16[729,128]{1,0:T(8,128)(2,1)S(1)} collective-permute-done((bf16[729,128]{1,0:T(8,128)(2,1)S(1)}, bf16[729,128]{1,0:T(8,128)(2,1)S(1)}, u32[]{:S(2)}, u32[]{:S(2)}) %collective-permute-start.7) | collective-permute-done | bytes 186656 | tf_op jit(solution)/shard_map/ppermute | solution.py:31
  41.6 5.1 %unpack.2 = (bf16[576,576]{1,0:T(8,128)(2,1)}, bf16[576,192]{1,0:T(8,128)(2,1)}, bf16[576,192]{1,0:T(8,128)(2,1)}) custom-call(s32[1]{0:T(128)} %bitcast.15.place_ref, bf16[16,135,128]{2,1,0:T(8,128)(2,1)} %copy-done.5, bf16[16,135,128]{2,1,0:T(8,128)(2,1)} %copy.51.got_ref), custom_call_target="tpu_custom_call" | custom-call | tf_op jit(solution)/shard_map/unpack/pallas_call | solution.py:159
  46.7 2.6 convolution_convert_fusion.1.values_ref
  50.5 1.4 collective-permute-start.12
  51.9 1.3 collective-permute-start.11
  57.7 1.6 copy.56.query_ref
  59.3 7.3 %attend.4 = (bf16[1024,192]{1,0:T(8,128)(2,1)}, f32[1024,128]{1,0:T(8,128)}) custom-call(bf16[1024,576]{1,0:T(8,128)(2,1)} %copy.56.query_ref, bf16[1024,192]{1,0:T(8,128)(2,1)} %copy.57.keys_ref, bf16[1024,192]{1,0:T(8,128)(2,1)} %convolution_convert_fusion.1.values_ref), custom_call_target="tpu_custom_call" | custom-call | flops 12000000000 | bytes 4000000 | tf_op jit(solution)/shard_map/attend/pallas_call | solution.py:260
  66.7 7.1 %attend.3 = (bf16[1024,192]{1,0:T(8,128)(2,1)}, f32[1024,128]{1,0:T(8,128)}) custom-call(bf16[1024,576]{1,0:T(8,128)(2,1)} %copy.56.query_ref, bf16[1024,192]{1,0:T(8,128)(2,1)} %copy.57.keys_ref, bf16[1024,192]{1,0:T(8,128)(2,1)} %convolution_convert_fusion.1.values_ref), custom_call_target="tpu_custom_call" | custom-call | flops 12000000000 | bytes 4000000 | tf_op jit(solution)/shard_map/attend/pallas_call | solution.py:260
  73.8 12.5 %collective-permute-done.11 = bf16[4,729,128]{2,0,1:T(4,128)(2,1)} collective-permute-done((bf16[4,729,128]{2,0,1:T(4,128)(2,1)}, bf16[4,729,128]{2,0,1:T(4,128)(2,1)}, u32[]{:S(2)}, u32[]{:S(2)}) %collective-permute-start.11) | collective-permute-done | bytes 746528 | tf_op jit(solution)/shard_map/ppermute | solution.py:31
  86.3 1.3 copy_dynamic-update-slice_fusion.2
  87.6 1.3 copy_dynamic-update-slice_fusion.1
  88.9 1.3 copy_dynamic-update-slice_fusion.own_ref
  91.8 7.3 %attend.5 = (bf16[1024,192]{1,0:T(8,128)(2,1)}, f32[1024,128]{1,0:T(8,128)}) custom-call(bf16[1024,576]{1,0:T(8,128)(2,1)} %copy.56.query_ref, bf16[1024,192]{1,0:T(8,128)(2,1)} %copy.57.keys_ref, bf16[1024,192]{1,0:T(8,128)(2,1)} %convolution_convert_fusion.1.values_ref), custom_call_target="tpu_custom_call" | custom-call | flops 12000000000 | bytes 4000000 | tf_op jit(solution)/shard_map/attend/pallas_call | solution.py:260
  99.2 2.4 copy.66.got_ref
  101.6 10.0 %unpack.3 = (bf16[576,576]{1,0:T(8,128)(2,1)}, bf16[576,1536]{1,0:T(8,128)(2,1)}, bf16[576,1536]{1,0:T(8,128)(2,1)}, bf16[1536,576]{1,0:T(8,128)(2,1)}) custom-call(s32[1]{0:T(128)} %bitcast.15.place_ref, bf16[16,729,128]{2,1,0:T(8,128)(2,1)} %copy-done, bf16[16,729,128]{2,1,0:T(8,128)(2,1)} %copy.66.got_ref), custom_call_target="tpu_custom_call" | custom-call | tf_op jit(solution)/shard_map/unpack/pallas_call | solution.py:159
  111.6 2.4 multiply_reduce_fusion.2
  114.3 2.1 copy-done.34
  116.3 2.7 fusion.47
  119.0 4.7 %fusion.46 = f32[1024,1536]{1,0:T(8,128)} fusion(bf16[1024,576]{0,1:T(8,128)(2,1)S(1)} %multiply_convert_fusion.1, bf16[576,1536]{1,0:T(8,128)(2,1)S(1)} %copy-done.33), kind=kOutput, calls=%fused_computation.127 | convolution fusion | flops 1811939328 | bytes 9240576 | tf_op jit(solution)/shard_map/dot_general | solution.py:577
  123.7 9.5 %fusion.3 = (bf16[1024,1536]{1,0:T(8,128)(2,1)}, bf16[1024,1536]{1,0:T(8,128)(2,1)S(1)}, bf16[1024,1536]{1,0:T(8,128)(2,1)}) fusion(f32[1024,1536]{1,0:T(8,128)} %fusion.46, f32[1024,1536]{1,0:T(8,128)S(1)} %fusion.47, bf16[1536,576]{1,0:T(8,128)(2,1)S(1)} %copy-done.31, bf16[1024,576]{0,1:T(8,128)(2,1)S(1)} %copy-done.11), kind=kOutput, calls=%fused_computation.5 | convolution fusion | flops 1835532288 | bytes 24969216 | tf_op jit(solution)/shard_map/dot_general | solution.py:403
  133.3 4.1 %fusion.51 = f32[1024,576]{0,1:T(8,128)S(1)} fusion(bf16[1024,1536]{1,0:T(8,128)(2,1)} %get-tuple-element.170, bf16[576,1536]{1,0:T(8,128)(2,1)S(1)} %copy-done.34), kind=kOutput, calls=%fused_computation.132 | convolution fusion | flops 1811939328 | bytes 7274496 | tf_op jit(solution)/shard_map/dot_general | solution.py:403
  137.4 3.8 %fusion.49.refs_1_ = f32[576,1536]{1,0:T(8,128)} fusion(bf16[1024,576]{0,1:T(8,128)(2,1)S(1)} %multiply_convert_fusion.1, bf16[1024,1536]{1,0:T(8,128)(2,1)S(1)} %copy-done.38), kind=kOutput, calls=%fused_computation.130 | convolution fusion | flops 1811939328 | bytes 7864320 | tf_op jit(solution)/shard_map/dot_general | solution.py:397
  141.1 3.8 %fusion.48.refs_0_ = f32[576,1536]{1,0:T(8,128)} fusion(bf16[1024,576]{0,1:T(8,128)(2,1)S(1)} %multiply_convert_fusion.1, bf16[1024,1536]{1,0:T(8,128)(2,1)S(1)} %get-tuple-element.171), kind=kOutput, calls=%fused_computation.129 | convolution fusion | flops 1811939328 | bytes 7864320 | tf_op jit(solution)/shard_map/dot_general | solution.py:397
  145.0 2.5 multiply_reduce_fusion
  148.6 2.5 convolution_convert_fusion.back_ref
  151.1 4.6 %fusion.50.refs_2_ = f32[1536,576]{1,0:T(8,128)} fusion(bf16[1024,1536]{1,0:T(8,128)(2,1)S(1)} %copy-done.39, bf16[1024,576]{0,1:T(8,128)(2,1)S(1)} %copy-done.11), kind=kOutput, calls=%fused_computation.131 | convolution fusion | flops 1811939328 | bytes 7864320 | tf_op jit(solution)/shard_map/dot_general | solution.py:397
  155.7 10.1 %pack.2 = (bf16[16,648,128]{2,1,0:T(8,128)(2,1)}, bf16[16,648,128]{2,1,0:T(8,128)(2,1)}) custom-call(s32[1]{0:T(128)} %bitcast.15.place_ref, f32[576,1536]{1,0:T(8,128)} %fusion.48.refs_0_, f32[576,1536]{1,0:T(8,128)} %fusion.49.refs_1_, f32[1536,576]{1,0:T(8,128)} %fusion.50.refs_2_), custom_call_target="tpu_custom_call" | custom-call | tf_op jit(solution)/shard_map/pack/pallas_call | solution.py:195
  166.3 10.8 %attend_back.3 = (f32[1024,192]{1,0:T(8,128)}, f32[1024,128]{1,0:T(8,128)}) custom-call(bf16[1024,576]{1,0:T(8,128)(2,1)} %copy.56.query_ref, bf16[1024,192]{1,0:T(8,128)(2,1)} %copy.57.keys_ref, bf16[1024,192]{1,0:T(8,128)(2,1)} %convolution_convert_fusion.1.values_ref, bf16[1024,576]{1,0:T(8,128)(2,1)} %convolution_convert_fusion.back_ref, ...), custom_call_target="tpu_custom_call" | custom-call | flops 24000000000 | bytes 8000000 | tf_op jit(solution)/shard_map/attend_back/pallas_call | solution.py:338
  177.1 2.7 fusion.15.refs_3_
  179.8 1.8 add_convert_fusion.1
  183.6 1.5 collective-permute-start.17
  185.1 10.9 %attend_back.5 = (f32[1024,192]{1,0:T(8,128)}, f32[1024,128]{1,0:T(8,128)}) custom-call(bf16[1024,576]{1,0:T(8,128)(2,1)} %copy.56.query_ref, bf16[1024,192]{1,0:T(8,128)(2,1)} %copy.57.keys_ref, bf16[1024,192]{1,0:T(8,128)(2,1)} %convolution_convert_fusion.1.values_ref, bf16[1024,576]{1,0:T(8,128)(2,1)} %convolution_convert_fusion.back_ref, ...), custom_call_target="tpu_custom_call" | custom-call | flops 24000000000 | bytes 8000000 | tf_op jit(solution)/shard_map/attend_back/pallas_call | solution.py:338
  196.0 10.7 %attend_back.4 = (f32[1024,192]{1,0:T(8,128)}, f32[1024,128]{1,0:T(8,128)}) custom-call(bf16[1024,576]{1,0:T(8,128)(2,1)} %copy.56.query_ref, bf16[1024,192]{1,0:T(8,128)(2,1)} %copy.57.keys_ref, bf16[1024,192]{1,0:T(8,128)(2,1)} %convolution_convert_fusion.1.values_ref, bf16[1024,576]{1,0:T(8,128)(2,1)} %convolution_convert_fusion.back_ref, ...), custom_call_target="tpu_custom_call" | custom-call | flops 24000000000 | bytes 8000000 | tf_op jit(solution)/shard_map/attend_back/pallas_call | solution.py:338
  206.7 7.1 %collective-permute-done.16 = bf16[4,648,128]{2,1,0:T(8,128)(2,1)S(1)} collective-permute-done((bf16[4,648,128]{2,1,0:T(8,128)(2,1)}, bf16[4,648,128]{2,1,0:T(8,128)(2,1)S(1)}, u32[]{:S(2)}, u32[]{:S(2)}) %collective-permute-start.16) | collective-permute-done | bytes 663584 | tf_op jit(solution)/shard_map/ppermute | solution.py:31
  213.9 1.4 fusion.21
  215.3 2.0 pad_maximum_fusion
  217.2 3.1 %copy.76 = f32[1024,576]{0,1:T(8,128)} copy(f32[1024,576]{1,0:T(8,128)} %pad_maximum_fusion) | data formatting | bytes 4718592 | tf_op jit(solution)/shard_map/concatenate | solution.py:610
  220.4 2.0 subtract_convert_fusion
  222.6 2.3 fusion.39.refs_0_
  224.8 2.4 fusion.52
  229.8 1.3 pad_maximum_fusion.3
  231.1 2.4 copy.77
  233.6 1.3 subtract_convert_fusion.2
  235.0 1.3 fusion.37.refs_1_
  238.4 1.6 fusion.11
  240.0 1.5 fusion.25.refs_2_
  241.6 7.4 %pack.3 = (bf16[16,216,128]{2,1,0:T(8,128)(2,1)}, bf16[16,216,128]{2,1,0:T(8,128)(2,1)}) custom-call(s32[1]{0:T(128)} %bitcast.15.place_ref, f32[576,576]{1,0:T(8,128)} %fusion.39.refs_0_, f32[576,192]{1,0:T(8,128)} %fusion.37.refs_1_, f32[576,192]{1,0:T(8,128)} %fusion.25.refs_2_, f32[576,576]{1,0:T(8,128)} %fusion.15.refs_3_), custom_call_target="tpu_custom_call" | custom-call | tf_op jit(solution)/shard_map/pack/pallas_call | solution.py:195
  250.3 2.9 collective-permute-done.29
  253.9 2.9 %collective-permute-done.30 = f32[2,576]{1,0:T(2,128)S(1)} collective-permute-done((f32[2,576]{1,0:T(2,128)S(1)}, f32[2,576]{1,0:T(2,128)S(1)}, u32[]{:S(2)}, u32[]{:S(2)}) %collective-permute-start.30) | collective-permute-done | bytes 4640 | tf_op jit(solution)/shard_map/ppermute | solution.py:31
  256.9 3.6 %collective-permute-done.31 = f32[2,576]{1,0:T(2,128)S(1)} collective-permute-done((f32[2,576]{1,0:T(2,128)S(1)}, f32[2,576]{1,0:T(2,128)S(1)}, u32[]{:S(2)}, u32[]{:S(2)}) %collective-permute-start.31) | collective-permute-done | bytes 4640 | tf_op jit(solution)/shard_map/ppermute | solution.py:31
  261.6 5.0 %add_convert_fusion = bf16[1024,576]{0,1:T(8,128)(2,1)} fusion(f32[1024,576]{0,1:T(8,128)S(1)} %copy-done.3, bf16[1024,1536]{1,0:T(8,128)(2,1)} %get-tuple-element.172, bf16[1536,576]{1,0:T(8,128)(2,1)S(1)} %copy-done.32), kind=kOutput, calls=%fused_computation.30 | convolution fusion | flops 1813118976 | bytes 8454144 | tf_op jit(solution)/shard_map/dot_general | solution.py:582
  266.6 2.0 collective-permute-start.25
  268.8 2.3 collective-permute-start.27
  274.0 1.4 collective-permute-done.25
  275.3 1.5 collective-permute-start.21
  276.8 3.4 %collective-permute-done.26 = bf16[648,128]{1,0:T(8,128)(2,1)S(1)} collective-permute-done((bf16[648,128]{1,0:T(8,128)(2,1)S(1)}, bf16[648,128]{1,0:T(8,128)(2,1)S(1)}, u32[]{:S(2)}, u32[]{:S(2)}) %collective-permute-start.26) | collective-permute-done | bytes 165920 | tf_op jit(solution)/shard_map/ppermute | solution.py:31
  280.3 1.8 collective-permute-done.21
  283.5 3.2 %collective-permute-start.24 = (bf16[216,128]{1,0:T(8,128)(2,1)S(1)}, bf16[216,128]{1,0:T(8,128)(2,1)S(1)}, u32[]{:S(2)}, u32[]{:S(2)}) collective-permute-start(bf16[216,128]{1,0:T(8,128)(2,1)S(1)} %get-tuple-element.159), channel_id=1, source_target_pairs={{0,24},{1,25},{2,26},{3,27},{4,28},{5,29},{6,30},{7,31},{8,16},{9,... | collective-permute-start | bytes 165896 | tf_op jit(solution)/shard_map/ppermute | solution.py:31
  (188 shorter events, 39.8 us)
Async XLA Ops:
  0.6 24.7 %copy-start.1 = (bf16[1024,576]{0,1:T(8,128)(2,1)S(1)}, bf16[1024,576]{0,1:T(8,128)(2,1)}, u32[]{:S(2)}) copy-start(bf16[1024,576]{0,1:T(8,128)(2,1)} %param.10) | copy-start | bytes 3538948
  1.5 7.0 %collective-permute-start.2 = (bf16[135,128]{1,0:T(8,128)(2,1)S(1)}, bf16[135,128]{1,0:T(8,128)(2,1)S(1)}, u32[]{:S(2)}, u32[]{:S(2)}) collective-permute-start(bf16[135,128]{1,0:T(8,128)(2,1)S(1)} %pad_maximum_fusion.16), channel_id=1, source_target_pairs={{0,24},{1,25},{2,26},{3,27},{4,28},{5,29},{6,30},{7,31},{8,16},{9,... | collective-permute-start | bytes 103688 | tf_op jit(solution)/shard_map/ppermute | solution.py:31
  6.6 4.8 %collective-permute-start.1 = (bf16[135,128]{1,0:T(8,128)(2,1)S(1)}, bf16[135,128]{1,0:T(8,128)(2,1)S(1)}, u32[]{:S(2)}, u32[]{:S(2)}) collective-permute-start(bf16[135,128]{1,0:T(8,128)(2,1)S(1)} %pad_maximum_fusion.16), channel_id=1, source_target_pairs={{0,16},{1,17},{2,18},{3,19},{4,20},{5,21},{6,22},{7,23},{8,24},{9,... | collective-permute-start | bytes 103688 | tf_op jit(solution)/shard_map/ppermute | solution.py:31
  6.6 4.8 %collective-permute-start = (bf16[135,128]{1,0:T(8,128)(2,1)S(1)}, bf16[135,128]{1,0:T(8,128)(2,1)S(1)}, u32[]{:S(2)}, u32[]{:S(2)}) collective-permute-start(bf16[135,128]{1,0:T(8,128)(2,1)S(1)} %pad_maximum_fusion.16), channel_id=1, source_target_pairs={{0,8},{1,9},{2,10},{3,11},{4,12},{5,13},{6,14},{7,15},{8,0},{9,1},... | collective-permute-start | bytes 103688 | tf_op jit(solution)/shard_map/ppermute | solution.py:31
  11.5 7.5 %collective-permute-start.5 = (bf16[4,135,128]{2,1,0:T(8,128)(2,1)S(1)}, bf16[4,135,128]{2,1,0:T(8,128)(2,1)S(1)}, u32[]{:S(2)}, u32[]{:S(2)}) collective-permute-start(bf16[4,135,128]{2,1,0:T(8,128)(2,1)S(1)} %pad_maximum_fusion.11), channel_id=1, source_target_pairs={{0,6},{1,7},{2,4},{3,5},{4,2},{5,3},{6,0},{7,1},{8,14},{9,15},{10,... | collective-permute-start | bytes 414728 | tf_op jit(solution)/shard_map/ppermute | solution.py:31
  14.0 5.8 %collective-permute-start.4 = (bf16[4,135,128]{2,1,0:T(8,128)(2,1)S(1)}, bf16[4,135,128]{2,1,0:T(8,128)(2,1)S(1)}, u32[]{:S(2)}, u32[]{:S(2)}) collective-permute-start(bf16[4,135,128]{2,1,0:T(8,128)(2,1)S(1)} %pad_maximum_fusion.11), channel_id=1, source_target_pairs={{0,4},{1,5},{2,6},{3,7},{4,0},{5,1},{6,2},{7,3},{8,12},{9,13},{10,... | collective-permute-start | bytes 414728 | tf_op jit(solution)/shard_map/ppermute | solution.py:31
  14.5 5.3 %collective-permute-start.3 = (bf16[4,135,128]{2,1,0:T(8,128)(2,1)S(1)}, bf16[4,135,128]{2,1,0:T(8,128)(2,1)S(1)}, u32[]{:S(2)}, u32[]{:S(2)}) collective-permute-start(bf16[4,135,128]{2,1,0:T(8,128)(2,1)S(1)} %pad_maximum_fusion.11), channel_id=1, source_target_pairs={{0,2},{1,3},{2,0},{3,1},{4,6},{5,7},{6,4},{7,5},{8,10},{9,11},{10,... | collective-permute-start | bytes 414728 | tf_op jit(solution)/shard_map/ppermute | solution.py:31
  16.3 40.7 %copy-start.4 = (f32[1024,32]{0,1:T(8,128)}, f32[1024,32]{0,1:T(8,128)S(1)}, u32[]{:S(2)}) copy-start(f32[1024,32]{0,1:T(8,128)S(1)} %get-tuple-element.210) | copy-start | bytes 393220
  19.9 21.7 %copy-start.5 = (bf16[16,135,128]{2,1,0:T(8,128)(2,1)}, bf16[16,135,128]{2,1,0:T(8,128)(2,1)S(1)}, u32[]{:S(2)}) copy-start(bf16[16,135,128]{2,1,0:T(8,128)(2,1)S(1)} %constant_dynamic-update-slice_fusion.own_ref) | copy-start | bytes 1658884
  20.9 19.8 %collective-permute-start.9 = (bf16[16,135,128]{2,0,1:T(8,128)(2,1)}, bf16[16,135,128]{2,0,1:T(8,128)(2,1)S(1)}, u32[]{:S(2)}, u32[]{:S(2)}) collective-permute-start(bf16[16,135,128]{2,0,1:T(8,128)(2,1)} %copy.50), channel_id=1, source_target_pairs={{0,1},{1,0},{2,3},{3,2},{4,5},{5,4},{6,7},{7,6},{8,9},{9,8},{10,11... | collective-permute-start | bytes 1658888 | tf_op jit(solution)/shard_map/ppermute | solution.py:31
  20.9 34.9 %copy-start.28 = (f32[576]{0:T(1024)}, f32[576]{0:T(1024)S(1)}, u32[]{:S(2)}) copy-start(f32[576]{0:T(1024)S(1)} %get-tuple-element.169) | copy-start | bytes 6916
  20.9 9.5 %collective-permute-start.8 = (bf16[729,128]{1,0:T(8,128)(2,1)S(1)}, bf16[729,128]{1,0:T(8,128)(2,1)S(1)}, u32[]{:S(2)}, u32[]{:S(2)}) collective-permute-start(bf16[729,128]{1,0:T(8,128)(2,1)S(1)} %pad_maximum_fusion.10), channel_id=1, source_target_pairs={{0,24},{1,25},{2,26},{3,27},{4,28},{5,29},{6,30},{7,31},{8,16},{9,... | collective-permute-start | bytes 559880 | tf_op jit(solution)/shard_map/ppermute | solution.py:31
  22.6 18.0 %collective-permute-start.7 = (bf16[729,128]{1,0:T(8,128)(2,1)S(1)}, bf16[729,128]{1,0:T(8,128)(2,1)S(1)}, u32[]{:S(2)}, u32[]{:S(2)}) collective-permute-start(bf16[729,128]{1,0:T(8,128)(2,1)S(1)} %pad_maximum_fusion.10), channel_id=1, source_target_pairs={{0,16},{1,17},{2,18},{3,19},{4,20},{5,21},{6,22},{7,23},{8,24},{9,... | collective-permute-start | bytes 559880 | tf_op jit(solution)/shard_map/ppermute | solution.py:31
  23.1 17.4 %collective-permute-start.6 = (bf16[729,128]{1,0:T(8,128)(2,1)S(1)}, bf16[729,128]{1,0:T(8,128)(2,1)S(1)}, u32[]{:S(2)}, u32[]{:S(2)}) collective-permute-start(bf16[729,128]{1,0:T(8,128)(2,1)S(1)} %pad_maximum_fusion.10), channel_id=1, source_target_pairs={{0,8},{1,9},{2,10},{3,11},{4,12},{5,13},{6,14},{7,15},{8,0},{9,1},... | collective-permute-start | bytes 559880 | tf_op jit(solution)/shard_map/ppermute | solution.py:31
  26.3 29.5 %copy-start.26 = (f32[1024]{0:T(1024)}, f32[1024]{0:T(1024)S(1)}, u32[]{:S(2)}) copy-start(f32[1024]{0:T(1024)S(1)} %get-tuple-element.205) | copy-start | bytes 12292
  46.7 7.3 %copy-start.21 = (bf16[576,192]{1,0:T(8,128)(2,1)S(1)}, bf16[576,192]{1,0:T(8,128)(2,1)}, u32[]{:S(2)}) copy-start(bf16[576,192]{1,0:T(8,128)(2,1)} %get-tuple-element.102) | copy-start | bytes 663556
  50.5 23.2 %collective-permute-start.12 = (bf16[4,729,128]{2,0,1:T(4,128)(2,1)}, bf16[4,729,128]{2,0,1:T(4,128)(2,1)}, u32[]{:S(2)}, u32[]{:S(2)}) collective-permute-start(bf16[4,729,128]{2,0,1:T(4,128)(2,1)} %copy.53), channel_id=1, source_target_pairs={{0,6},{1,7},{2,4},{3,5},{4,2},{5,3},{6,0},{7,1},{8,14},{9,15},{10,... | collective-permute-start | bytes 2239496 | tf_op jit(solution)/shard_map/ppermute | solution.py:31
  51.9 34.3 %collective-permute-start.11 = (bf16[4,729,128]{2,0,1:T(4,128)(2,1)}, bf16[4,729,128]{2,0,1:T(4,128)(2,1)}, u32[]{:S(2)}, u32[]{:S(2)}) collective-permute-start(bf16[4,729,128]{2,0,1:T(4,128)(2,1)} %copy.53), channel_id=1, source_target_pairs={{0,4},{1,5},{2,6},{3,7},{4,0},{5,1},{6,2},{7,3},{8,12},{9,13},{10,... | collective-permute-start | bytes 2239496 | tf_op jit(solution)/shard_map/ppermute | solution.py:31
  53.3 33.0 %collective-permute-start.10 = (bf16[4,729,128]{2,0,1:T(4,128)(2,1)}, bf16[4,729,128]{2,0,1:T(4,128)(2,1)}, u32[]{:S(2)}, u32[]{:S(2)}) collective-permute-start(bf16[4,729,128]{2,0,1:T(4,128)(2,1)} %copy.53), channel_id=1, source_target_pairs={{0,2},{1,3},{2,0},{3,1},{4,6},{5,7},{6,4},{7,5},{8,10},{9,11},{10,... | collective-permute-start | bytes 2239496 | tf_op jit(solution)/shard_map/ppermute | solution.py:31
  91.8 7.4 %collective-permute-start.13 = (bf16[16,729,128]{2,0,1:T(8,128)(2,1)S(1)}, bf16[16,729,128]{2,0,1:T(8,128)(2,1)S(1)}, u32[]{:S(2)}, u32[]{:S(2)}) collective-permute-start(bf16[16,729,128]{2,0,1:T(8,128)(2,1)S(1)} %copy.65), channel_id=1, source_target_pairs={{0,1},{1,0},{2,3},{3,2},{4,5},{5,4},{6,7},{7,6},{8,9},{9,8},{10,11... | collective-permute-start | bytes 8957960 | tf_op jit(solution)/shard_map/ppermute | solution.py:31
  101.6 10.0 %copy-start.40 = (bf16[1024,192]{1,0:T(8,128)(2,1)S(1)}, bf16[1024,192]{1,0:T(8,128)(2,1)}, u32[]{:S(2)}) copy-start(bf16[1024,192]{1,0:T(8,128)(2,1)} %get-tuple-element.108.mixed_ref) | copy-start | bytes 1179652
  101.6 10.0 %copy-start.42 = (bf16[1024,192]{1,0:T(8,128)(2,1)S(1)}, bf16[1024,192]{1,0:T(8,128)(2,1)}, u32[]{:S(2)}) copy-start(bf16[1024,192]{1,0:T(8,128)(2,1)} %get-tuple-element.107.mixed_ref) | copy-start | bytes 1179652
  101.6 10.0 %copy-start.44 = (bf16[1024,192]{1,0:T(8,128)(2,1)S(1)}, bf16[1024,192]{1,0:T(8,128)(2,1)}, u32[]{:S(2)}) copy-start(bf16[1024,192]{1,0:T(8,128)(2,1)} %get-tuple-element.110.mixed_ref) | copy-start | bytes 1179652
  114.0 33.5 %copy-start.2 = (f32[1024,576]{0,1:T(8,128)}, f32[1024,576]{0,1:T(8,128)S(1)}, u32[]{:S(2)}) copy-start(f32[1024,576]{0,1:T(8,128)S(1)} %get-tuple-element.212) | copy-start | bytes 7077892
  116.3 2.7 copy-start.33
  119.0 4.7 %copy-start.11 = (bf16[1024,576]{0,1:T(8,128)(2,1)S(1)}, bf16[1024,576]{0,1:T(8,128)(2,1)}, u32[]{:S(2)}) copy-start(bf16[1024,576]{0,1:T(8,128)(2,1)} %param.11) | copy-start | bytes 3538948
  119.0 4.7 %copy-start.31 = (bf16[1536,576]{1,0:T(8,128)(2,1)S(1)}, bf16[1536,576]{1,0:T(8,128)(2,1)}, u32[]{:S(2)}) copy-start(bf16[1536,576]{1,0:T(8,128)(2,1)} %get-tuple-element.118) | copy-start | bytes 5308420
  133.3 4.1 %copy-start.38 = (bf16[1024,1536]{1,0:T(8,128)(2,1)S(1)}, bf16[1024,1536]{1,0:T(8,128)(2,1)}, u32[]{:S(2)}) copy-start(bf16[1024,1536]{1,0:T(8,128)(2,1)} %get-tuple-element.170) | copy-start | bytes 9437188
  165.8 14.0 %collective-permute-start.14 = (bf16[16,648,128]{2,1,0:T(8,128)(2,1)}, bf16[16,648,128]{2,1,0:T(8,128)(2,1)S(1)}, u32[]{:S(2)}, u32[]{:S(2)}) collective-permute-start(bf16[16,648,128]{2,1,0:T(8,128)(2,1)} %get-tuple-element.122), channel_id=1, source_target_pairs={{0,1},{1,0},{2,3},{3,2},{4,5},{5,4},{6,7},{7,6},{8,9},{9,8},{10,11... | collective-permute-start | bytes 7962632 | tf_op jit(solution)/shard_map/ppermute | solution.py:31
  166.3 10.8 %copy-start.41 = (bf16[1024,192]{1,0:T(8,128)(2,1)S(1)}, bf16[1024,192]{1,0:T(8,128)(2,1)}, u32[]{:S(2)}) copy-start(bf16[1024,192]{1,0:T(8,128)(2,1)} %get-tuple-element.108.mixed_ref) | copy-start | bytes 1179652
  166.3 10.8 %copy-start.43 = (bf16[1024,192]{1,0:T(8,128)(2,1)S(1)}, bf16[1024,192]{1,0:T(8,128)(2,1)}, u32[]{:S(2)}) copy-start(bf16[1024,192]{1,0:T(8,128)(2,1)} %get-tuple-element.107.mixed_ref) | copy-start | bytes 1179652
  166.3 10.8 %copy-start.45 = (bf16[1024,192]{1,0:T(8,128)(2,1)S(1)}, bf16[1024,192]{1,0:T(8,128)(2,1)}, u32[]{:S(2)}) copy-start(bf16[1024,192]{1,0:T(8,128)(2,1)} %get-tuple-element.110.mixed_ref) | copy-start | bytes 1179652
  177.1 2.7 copy-start.6
  181.6 25.1 %collective-permute-start.15 = (bf16[4,648,128]{2,1,0:T(8,128)(2,1)}, bf16[4,648,128]{2,1,0:T(8,128)(2,1)S(1)}, u32[]{:S(2)}, u32[]{:S(2)}) collective-permute-start(bf16[4,648,128]{2,1,0:T(8,128)(2,1)} %get-tuple-element.129), channel_id=1, source_target_pairs={{0,2},{1,3},{2,0},{3,1},{4,6},{5,7},{6,4},{7,5},{8,10},{9,11},{10,... | collective-permute-start | bytes 1990664 | tf_op jit(solution)/shard_map/ppermute | solution.py:31
  182.9 31.0 %collective-permute-start.16 = (bf16[4,648,128]{2,1,0:T(8,128)(2,1)}, bf16[4,648,128]{2,1,0:T(8,128)(2,1)S(1)}, u32[]{:S(2)}, u32[]{:S(2)}) collective-permute-start(bf16[4,648,128]{2,1,0:T(8,128)(2,1)} %get-tuple-element.130), channel_id=1, source_target_pairs={{0,4},{1,5},{2,6},{3,7},{4,0},{5,1},{6,2},{7,3},{8,12},{9,13},{10,... | collective-permute-start | bytes 1990664 | tf_op jit(solution)/shard_map/ppermute | solution.py:31
  183.6 30.3 %collective-permute-start.17 = (bf16[4,648,128]{2,1,0:T(8,128)(2,1)}, bf16[4,648,128]{2,1,0:T(8,128)(2,1)S(1)}, u32[]{:S(2)}, u32[]{:S(2)}) collective-permute-start(bf16[4,648,128]{2,1,0:T(8,128)(2,1)} %get-tuple-element.131), channel_id=1, source_target_pairs={{0,6},{1,7},{2,4},{3,5},{4,2},{5,3},{6,0},{7,1},{8,14},{9,15},{10,... | collective-permute-start | bytes 1990664 | tf_op jit(solution)/shard_map/ppermute | solution.py:31
  206.7 8.5 %copy-start.15 = (f32[1024,192]{1,0:T(8,128)S(1)}, f32[1024,192]{1,0:T(8,128)}, u32[]{:S(2)}) copy-start(f32[1024,192]{1,0:T(8,128)} %get-tuple-element.139) | copy-start | bytes 2359300
  206.7 8.5 %copy-start.16 = (f32[1024,192]{1,0:T(8,128)S(1)}, f32[1024,192]{1,0:T(8,128)}, u32[]{:S(2)}) copy-start(f32[1024,192]{1,0:T(8,128)} %get-tuple-element.141) | copy-start | bytes 2359300
  206.7 8.5 %copy-start.17 = (f32[1024,192]{1,0:T(8,128)S(1)}, f32[1024,192]{1,0:T(8,128)}, u32[]{:S(2)}) copy-start(f32[1024,192]{1,0:T(8,128)} %get-tuple-element.140) | copy-start | bytes 2359300
  224.8 3.3 %copy-start.10 = (f32[1024,128]{1,0:T(8,128)S(1)}, f32[1024,128]{1,0:T(8,128)}, u32[]{:S(2)}) copy-start(f32[1024,128]{1,0:T(8,128)} %get-tuple-element.143) | copy-start | bytes 1572868
  224.8 4.2 %copy-start.9 = (f32[1024,128]{1,0:T(8,128)S(1)}, f32[1024,128]{1,0:T(8,128)}, u32[]{:S(2)}) copy-start(f32[1024,128]{1,0:T(8,128)} %get-tuple-element.144) | copy-start | bytes 1572868
  233.6 2.8 copy-start.22
  238.3 11.1 %collective-permute-start.28 = (f32[2,576]{1,0:T(2,128)S(1)}, f32[2,576]{1,0:T(2,128)S(1)}, u32[]{:S(2)}, u32[]{:S(2)}) collective-permute-start(f32[2,576]{1,0:T(2,128)S(1)} %pad_maximum_fusion.17), channel_id=1, source_target_pairs={{0,1},{1,0},{2,3},{3,2},{4,5},{5,4},{6,7},{7,6},{8,9},{9,8},{10,11... | collective-permute-start | bytes 13832 | tf_op jit(solution)/shard_map/ppermute | solution.py:31
  240.0 21.5 %copy-start.32 = (bf16[1536,576]{1,0:T(8,128)(2,1)S(1)}, bf16[1536,576]{1,0:T(8,128)(2,1)}, u32[]{:S(2)}) copy-start(bf16[1536,576]{1,0:T(8,128)(2,1)} %get-tuple-element.118) | copy-start | bytes 5308420
  241.6 20.0 %copy-start.3 = (f32[1024,576]{0,1:T(8,128)S(1)}, f32[1024,576]{0,1:T(8,128)}, u32[]{:S(2)}) copy-start(f32[1024,576]{0,1:T(8,128)} %copy-done.2) | copy-start | bytes 7077892
  249.0 22.7 %collective-permute-start.18 = (bf16[16,216,128]{2,1,0:T(8,128)(2,1)}, bf16[16,216,128]{2,1,0:T(8,128)(2,1)S(1)}, u32[]{:S(2)}, u32[]{:S(2)}) collective-permute-start(bf16[16,216,128]{2,1,0:T(8,128)(2,1)} %get-tuple-element.148), channel_id=1, source_target_pairs={{0,1},{1,0},{2,3},{3,2},{4,5},{5,4},{6,7},{7,6},{8,9},{9,8},{10,11... | collective-permute-start | bytes 2654216 | tf_op jit(solution)/shard_map/ppermute | solution.py:31
  249.5 3.7 %collective-permute-start.29 = (f32[2,576]{1,0:T(2,128)S(1)}, f32[2,576]{1,0:T(2,128)S(1)}, u32[]{:S(2)}, u32[]{:S(2)}) collective-permute-start(f32[2,576]{1,0:T(2,128)S(1)} %fusion.35), channel_id=1, source_target_pairs={{0,2},{1,3},{2,0},{3,1},{4,6},{5,7},{6,4},{7,5},{8,10},{9,11},{10,... | collective-permute-start | bytes 13832 | tf_op jit(solution)/shard_map/ppermute | solution.py:31
  253.2 3.7 %collective-permute-start.30 = (f32[2,576]{1,0:T(2,128)S(1)}, f32[2,576]{1,0:T(2,128)S(1)}, u32[]{:S(2)}, u32[]{:S(2)}) collective-permute-start(f32[2,576]{1,0:T(2,128)S(1)} %fusion.84), channel_id=1, source_target_pairs={{0,4},{1,5},{2,6},{3,7},{4,0},{5,1},{6,2},{7,3},{8,12},{9,13},{10,... | collective-permute-start | bytes 13832 | tf_op jit(solution)/shard_map/ppermute | solution.py:31
  256.9 3.6 %collective-permute-start.31 = (f32[2,576]{1,0:T(2,128)S(1)}, f32[2,576]{1,0:T(2,128)S(1)}, u32[]{:S(2)}, u32[]{:S(2)}) collective-permute-start(f32[2,576]{1,0:T(2,128)S(1)} %add.269), channel_id=1, source_target_pairs={{0,8},{1,9},{2,10},{3,11},{4,12},{5,13},{6,14},{7,15},{8,0},{9,1},... | collective-permute-start | bytes 13832 | tf_op jit(solution)/shard_map/ppermute | solution.py:31
  260.5 6.1 %copy-start.25 = (bf16[648,128]{1,0:T(8,128)(2,1)S(1)}, bf16[648,128]{1,0:T(8,128)(2,1)}, u32[]{:S(2)}) copy-start(bf16[648,128]{1,0:T(8,128)(2,1)} %get-tuple-element.161) | copy-start | bytes 497668
  260.5 8.1 %copy-start.24 = (bf16[648,128]{1,0:T(8,128)(2,1)S(1)}, bf16[648,128]{1,0:T(8,128)(2,1)}, u32[]{:S(2)}) copy-start(bf16[648,128]{1,0:T(8,128)(2,1)} %get-tuple-element.162) | copy-start | bytes 497668
  260.5 8.3 %copy-start.23 = (bf16[648,128]{1,0:T(8,128)(2,1)S(1)}, bf16[648,128]{1,0:T(8,128)(2,1)}, u32[]{:S(2)}) copy-start(bf16[648,128]{1,0:T(8,128)(2,1)} %get-tuple-element.163) | copy-start | bytes 497668
  260.5 11.1 %copy-start.18 = (bf16[16,216,128]{2,1,0:T(8,128)(2,1)S(1)}, bf16[16,216,128]{2,1,0:T(8,128)(2,1)}, u32[]{:S(2)}) copy-start(bf16[16,216,128]{2,1,0:T(8,128)(2,1)} %get-tuple-element.147) | copy-start | bytes 2654212
  260.5 10.5 %collective-permute-start.32 = (f32[2,576]{1,0:T(2,128)S(1)}, f32[2,576]{1,0:T(2,128)S(1)}, u32[]{:S(2)}, u32[]{:S(2)}) collective-permute-start(f32[2,576]{1,0:T(2,128)S(1)} %add.270), channel_id=1, source_target_pairs={{0,16},{1,17},{2,18},{3,19},{4,20},{5,21},{6,22},{7,23},{8,24},{9,... | collective-permute-start | bytes 13832 | tf_op jit(solution)/shard_map/ppermute | solution.py:31
  266.5 13.7 %copy-start.19 = (bf16[648,128]{1,0:T(8,128)(2,1)S(1)}, bf16[648,128]{1,0:T(8,128)(2,1)}, u32[]{:S(2)}) copy-start(bf16[648,128]{1,0:T(8,128)(2,1)} %get-tuple-element.160) | copy-start | bytes 497668
  266.6 8.8 %collective-permute-start.25 = (bf16[648,128]{1,0:T(8,128)(2,1)S(1)}, bf16[648,128]{1,0:T(8,128)(2,1)S(1)}, u32[]{:S(2)}, u32[]{:S(2)}) collective-permute-start(bf16[648,128]{1,0:T(8,128)(2,1)S(1)} %copy-done.25), channel_id=1, source_target_pairs={{0,8},{1,9},{2,10},{3,11},{4,12},{5,13},{6,14},{7,15},{8,0},{9,1},... | collective-permute-start | bytes 497672 | tf_op jit(solution)/shard_map/ppermute | solution.py:31
  268.6 11.6 %collective-permute-start.26 = (bf16[648,128]{1,0:T(8,128)(2,1)S(1)}, bf16[648,128]{1,0:T(8,128)(2,1)S(1)}, u32[]{:S(2)}, u32[]{:S(2)}) collective-permute-start(bf16[648,128]{1,0:T(8,128)(2,1)S(1)} %copy-done.24), channel_id=1, source_target_pairs={{0,16},{1,17},{2,18},{3,19},{4,20},{5,21},{6,22},{7,23},{8,24},{9,... | collective-permute-start | bytes 497672 | tf_op jit(solution)/shard_map/ppermute | solution.py:31
  268.8 11.5 %collective-permute-start.27 = (bf16[648,128]{1,0:T(8,128)(2,1)S(1)}, bf16[648,128]{1,0:T(8,128)(2,1)S(1)}, u32[]{:S(2)}, u32[]{:S(2)}) collective-permute-start(bf16[648,128]{1,0:T(8,128)(2,1)S(1)} %copy-done.23), channel_id=1, source_target_pairs={{0,24},{1,25},{2,26},{3,27},{4,28},{5,29},{6,30},{7,31},{8,16},{9,... | collective-permute-start | bytes 497672 | tf_op jit(solution)/shard_map/ppermute | solution.py:31
  271.9 8.4 %collective-permute-start.19 = (bf16[4,216,128]{2,1,0:T(8,128)(2,1)S(1)}, bf16[4,216,128]{2,1,0:T(8,128)(2,1)S(1)}, u32[]{:S(2)}, u32[]{:S(2)}) collective-permute-start(bf16[4,216,128]{2,1,0:T(8,128)(2,1)S(1)} %get-tuple-element.151), channel_id=1, source_target_pairs={{0,2},{1,3},{2,0},{3,1},{4,6},{5,7},{6,4},{7,5},{8,10},{9,11},{10,... | collective-permute-start | bytes 663560 | tf_op jit(solution)/shard_map/ppermute | solution.py:31
  272.7 7.7 %collective-permute-start.20 = (bf16[4,216,128]{2,1,0:T(8,128)(2,1)S(1)}, bf16[4,216,128]{2,1,0:T(8,128)(2,1)S(1)}, u32[]{:S(2)}, u32[]{:S(2)}) collective-permute-start(bf16[4,216,128]{2,1,0:T(8,128)(2,1)S(1)} %get-tuple-element.152), channel_id=1, source_target_pairs={{0,4},{1,5},{2,6},{3,7},{4,0},{5,1},{6,2},{7,3},{8,12},{9,13},{10,... | collective-permute-start | bytes 663560 | tf_op jit(solution)/shard_map/ppermute | solution.py:31
  275.3 6.8 %collective-permute-start.21 = (bf16[4,216,128]{2,1,0:T(8,128)(2,1)S(1)}, bf16[4,216,128]{2,1,0:T(8,128)(2,1)S(1)}, u32[]{:S(2)}, u32[]{:S(2)}) collective-permute-start(bf16[4,216,128]{2,1,0:T(8,128)(2,1)S(1)} %get-tuple-element.153), channel_id=1, source_target_pairs={{0,6},{1,7},{2,4},{3,5},{4,2},{5,3},{6,0},{7,1},{8,14},{9,15},{10,... | collective-permute-start | bytes 663560 | tf_op jit(solution)/shard_map/ppermute | solution.py:31
  282.3 5.2 %collective-permute-start.22 = (bf16[216,128]{1,0:T(8,128)(2,1)S(1)}, bf16[216,128]{1,0:T(8,128)(2,1)S(1)}, u32[]{:S(2)}, u32[]{:S(2)}) collective-permute-start(bf16[216,128]{1,0:T(8,128)(2,1)S(1)} %get-tuple-element.157), channel_id=1, source_target_pairs={{0,8},{1,9},{2,10},{3,11},{4,12},{5,13},{6,14},{7,15},{8,0},{9,1},... | collective-permute-start | bytes 165896 | tf_op jit(solution)/shard_map/ppermute | solution.py:31
  283.2 5.1 %collective-permute-start.23 = (bf16[216,128]{1,0:T(8,128)(2,1)S(1)}, bf16[216,128]{1,0:T(8,128)(2,1)S(1)}, u32[]{:S(2)}, u32[]{:S(2)}) collective-permute-start(bf16[216,128]{1,0:T(8,128)(2,1)S(1)} %get-tuple-element.158), channel_id=1, source_target_pairs={{0,16},{1,17},{2,18},{3,19},{4,20},{5,21},{6,22},{7,23},{8,24},{9,... | collective-permute-start | bytes 165896 | tf_op jit(solution)/shard_map/ppermute | solution.py:31
  283.5 6.1 %collective-permute-start.24 = (bf16[216,128]{1,0:T(8,128)(2,1)S(1)}, bf16[216,128]{1,0:T(8,128)(2,1)S(1)}, u32[]{:S(2)}, u32[]{:S(2)}) collective-permute-start(bf16[216,128]{1,0:T(8,128)(2,1)S(1)} %get-tuple-element.159), channel_id=1, source_target_pairs={{0,24},{1,25},{2,26},{3,27},{4,28},{5,29},{6,30},{7,31},{8,16},{9,... | collective-permute-start | bytes 165896 | tf_op jit(solution)/shard_map/ppermute | solution.py:31
  (15 other events, 29.5 us)

commit v3 on v2

--- a/solution.py
+++ b/solution.py
@@ -109,6 +109,10 @@
         stage[owner, pl.ds(start + at, pairs, stride=tiles_in), :] = tiles[at]
 
 
+def tiles_of(wide):
+    return -(-wide // LANES)
+
+
 def tile_widths(wide):
     return [min(LANES, wide - at) for at in range(0, wide, LANES)]
 
@@ -135,12 +139,13 @@
         lax.fori_loop(0, devices // 2, store, 0)
 
 
-def unpack_kernel(place_ref, own_ref, got_ref, *refs, devices, shapes):
-    count = len(shapes)
+def unpack_kernel(place_ref, own_ref, got_ref, *refs, devices, shapes, joined):
+    count = 1 if joined else len(shapes)
     outs, stage, wides = refs[:count], refs[count], refs[count + 1 :]
     load_stage(place_ref, own_ref, got_ref, stage, devices)
-    start = 0
-    for (rows, wide), out, target in zip(shapes, outs, wides):
+    start, column = 0, 0
+    for index, ((rows, wide), target) in enumerate(zip(shapes, wides)):
+        out = outs[0 if joined else index]
         each = rows // devices
         each_group(
             devices,
@@ -151,16 +156,27 @@
         )
         start += each * wide // LANES
         for at, width in enumerate(tile_widths(wide)):
-            out[:, at * LANES : at * LANES + width] = target[at][:, :width].astype(jnp.bfloat16)
-
-
-def unpack_pieces(place, pieces, shapes, devices):
+            tile = target[at]
+            if joined and width < LANES:
+                lane = lax.broadcasted_iota(jnp.int32, tile.shape, 1)
+                tile = jnp.where(lane < width, tile, 0.0)
+                width = LANES
+            out[:, column : column + width] = tile[:, :width].astype(jnp.bfloat16)
+            column += width
+        if not joined:
+            column = 0
+
+
+def unpack_pieces(place, pieces, shapes, devices, joined):
     rows_in = pieces[0].shape[1]
+    outs = shapes
+    if joined:
+        outs = [(shapes[0][0], sum(tiles_of(wide) for _, wide in shapes) * LANES)]
     return pl.pallas_call(
-        functools.partial(unpack_kernel, devices=devices, shapes=shapes),
-        out_shape=[jax.ShapeDtypeStruct(shape, jnp.bfloat16) for shape in shapes],
+        functools.partial(unpack_kernel, devices=devices, shapes=shapes, joined=joined),
+        out_shape=[jax.ShapeDtypeStruct(shape, jnp.bfloat16) for shape in outs],
         in_specs=[pl.BlockSpec(memory_space=pltpu.SMEM)] + [pl.BlockSpec(memory_space=pltpu.VMEM)] * 2,
-        out_specs=[pl.BlockSpec(memory_space=pltpu.VMEM)] * len(shapes),
+        out_specs=[pl.BlockSpec(memory_space=pltpu.VMEM)] * len(outs),
         scratch_shapes=[pltpu.VMEM((devices, rows_in, LANES), jnp.float32)]
         + [pltpu.VMEM((-(-wide // LANES), rows, LANES), jnp.float32) for rows, wide in shapes],
         compiler_params=pltpu.CompilerParams(vmem_limit_bytes=VMEM_LIMIT),
@@ -168,41 +184,66 @@
     )(place, *pieces)
 
 
-def pack_kernel(place_ref, *refs, devices, shapes):
-    count = len(shapes)
+def pack_kernel(place_ref, *refs, devices, shapes, tiled_in, extra):
+    count = len(shapes) + (1 if extra else 0)
     sources, kept_ref, sent_ref, stage = refs[:count], refs[count], refs[count + 1], refs[count + 2]
-    wides = refs[count + 3 :]
+    wides = list(refs[count + 3 :])
     place = place_ref[0]
     start = 0
-    for (rows, wide), source, tiled in zip(shapes, sources, wides):
+    for index, (rows, wide) in enumerate(shapes):
         each = rows // devices
-        for at, width in enumerate(tile_widths(wide)):
-            tiled[at, :, :width] = source[:, at * LANES : at * LANES + width]
+        source = sources[index]
+        if not tiled_in[index]:
+            tiled = wides.pop(0)
+            for at, width in enumerate(tile_widths(wide)):
+                tiled[at, :, :width] = source[:, at * LANES : at * LANES + width]
+            source = tiled
         each_group(
             devices,
             each,
-            lambda owner, row, start=start, each=each, wide=wide, tiled=tiled: pack_rows(
-                tiled, row, each, wide, stage, place ^ owner, start
+            lambda owner, row, start=start, each=each, wide=wide, source=source: pack_rows(
+                source, row, each, wide, stage, place ^ owner, start
             ),
         )
         start += each * wide // LANES
+    if extra:
+        row = jnp.concatenate([sources[-1][at : at + 1, :] for at in range(extra[0])], 1)
+        for at in range(extra[0] * extra[1] // LANES):
+            tile = row[:, at * LANES : (at + 1) * LANES].reshape(1, 1, LANES)
+            stage[:, start + at : start + at + 1, :] = jnp.broadcast_to(tile, (devices, 1, LANES))
+        start += extra[0] * extra[1] // LANES
+        spare = stage.shape[1] - start
+        if spare:
+            stage[:, start:, :] = jnp.zeros((devices, spare, LANES), jnp.float32)
     store_stage(kept_ref, sent_ref, stage, devices)
 
 
-def pack_grads(place, grads, shapes, devices):
+def pack_grads(place, grads, shapes, devices, extra):
     rows_out = sum(rows * wide for rows, wide in shapes) // (devices * LANES)
+    sources = list(grads)
+    if extra is not None:
+        rows_out = -(-(rows_out + extra.size // LANES) // 8) * 8
+        sources.append(extra)
+    tiled_in = tuple(grad.ndim == 3 for grad in grads)
     half = jax.ShapeDtypeStruct((devices // 2, rows_out, LANES), jnp.bfloat16)
     return pl.pallas_call(
-        functools.partial(pack_kernel, devices=devices, shapes=shapes),
+        functools.partial(
+            pack_kernel, devices=devices, shapes=shapes, tiled_in=tiled_in,
+            extra=None if extra is None else extra.shape,
+        ),
         out_shape=[half, half],
         in_specs=[pl.BlockSpec(memory_space=pltpu.SMEM)]
-        + [pl.BlockSpec(memory_space=pltpu.VMEM)] * len(shapes),
+        + [pl.BlockSpec(memory_space=pltpu.VMEM)] * len(sources),
         out_specs=[pl.BlockSpec(memory_space=pltpu.VMEM)] * 2,
         scratch_shapes=[pltpu.VMEM((devices, rows_out, LANES), jnp.float32)]
-        + [pltpu.VMEM((-(-wide // LANES), rows, LANES), jnp.float32) for rows, wide in shapes],
+        + [
+            pltpu.VMEM((tiles_of(wide), rows, LANES), jnp.float32)
+            for (rows, wide), tiled in zip(shapes, tiled_in)
+            if not tiled
+        ],
         compiler_params=pltpu.CompilerParams(vmem_limit_bytes=VMEM_LIMIT),
         name="pack",
-    )(place, *grads)
+    )(place, *sources)
 
 
 BLOCK = 256
@@ -224,10 +265,20 @@
     return jnp.dot(left, right, preferred_element_type=jnp.float32)
 
 
-def attend_kernel(query_ref, keys_ref, values_ref, mixed_ref, total_ref, *, head, group):
-    length = query_ref.shape[0]
-    keys = keys_ref[:, head * HEAD_DIM : (head + 1) * HEAD_DIM]
-    values = values_ref[:, head * HEAD_DIM : (head + 1) * HEAD_DIM]
+def key_columns(head):
+    first = tiles_of(HEADS * HEAD_DIM) * LANES + head * HEAD_DIM
+    return slice(first, first + HEAD_DIM)
+
+
+def value_columns(head):
+    first = (tiles_of(HEADS * HEAD_DIM) + tiles_of(KV_HEADS * HEAD_DIM)) * LANES + head * HEAD_DIM
+    return slice(first, first + HEAD_DIM)
+
+
+def attend_kernel(fields_ref, mixed_ref, total_ref, *, head, group):
+    length = fields_ref.shape[0]
+    keys = fields_ref[:, key_columns(head)]
+    values = fields_ref[:, value_columns(head)]
     lower = lax.broadcasted_iota(jnp.int32, (BLOCK, BLOCK), 0) >= lax.broadcasted_iota(
         jnp.int32, (BLOCK, BLOCK), 1
     )
@@ -236,7 +287,7 @@
         mixed, totals_row = [], jnp.zeros((BLOCK, LANES), jnp.float32)
         for member in range(group):
             at = (head * group + member) * HEAD_DIM
-            query = query_ref[start : start + BLOCK, at : at + HEAD_DIM]
+            query = fields_ref[start : start + BLOCK, at : at + HEAD_DIM]
             diagonal = jnp.where(lower, dot_nt(query, keys[start : start + BLOCK]), NEG_BIG)
             maxima = jnp.max(diagonal, 1, keepdims=True)
             if start:
@@ -255,35 +306,35 @@
         total_ref[start : start + BLOCK, :] = totals_row
 
 
-def attend(query, keys, values, head, group):
-    length = query.shape[0]
+def attend(fields, head, group):
+    length = fields.shape[0]
     return pl.pallas_call(
         functools.partial(attend_kernel, head=head, group=group),
         out_shape=[
             jax.ShapeDtypeStruct((length, group * HEAD_DIM), jnp.bfloat16),
             jax.ShapeDtypeStruct((length, LANES), jnp.float32),
         ],
-        in_specs=[pl.BlockSpec(memory_space=pltpu.VMEM)] * 3,
+        in_specs=[pl.BlockSpec(memory_space=pltpu.VMEM)],
         out_specs=[pl.BlockSpec(memory_space=pltpu.VMEM)] * 2,
         compiler_params=pltpu.CompilerParams(vmem_limit_bytes=VMEM_LIMIT),
         cost_estimate=pl.CostEstimate(
             flops=12 * 10**9, bytes_accessed=4 * 10**6, transcendentals=2 * 10**6
         ),
         name="attend",
-    )(query, keys, values)
+    )(fields)
 
 
 def attend_back_kernel(
-    query_ref, keys_ref, values_ref, back_ref, mixed_ref, total_ref,
+    fields_ref, back_ref, mixed_ref, total_ref,
     query_back_ref, key_back_ref, queries, backs, totals, deltas, query_sum, key_sum, value_sum,
     *, head, group,
 ):
-    length = query_ref.shape[0]
+    length = fields_ref.shape[0]
     ones = jnp.ones((8, HEAD_DIM), jnp.float32)
     totals[...] = total_ref[...].T[:8]
     for member in range(group):
         at = (head * group + member) * HEAD_DIM
-        queries[member] = query_ref[:, at : at + HEAD_DIM]
+        queries[member] = fields_ref[:, at : at + HEAD_DIM]
         back = back_ref[:, at : at + HEAD_DIM]
         backs[member] = back
         product = back.astype(jnp.float32) * mixed_ref[
@@ -293,8 +344,8 @@
             ones, product, (((1,), (1,)), ((), ())),
             precision=lax.Precision.HIGHEST, preferred_element_type=jnp.float32,
         )
-    keys_all = keys_ref[:, head * HEAD_DIM : (head + 1) * HEAD_DIM]
-    values_all = values_ref[:, head * HEAD_DIM : (head + 1) * HEAD_DIM]
+    keys_all = fields_ref[:, key_columns(head)]
+    values_all = fields_ref[:, value_columns(head)]
     upper = lax.broadcasted_iota(jnp.int32, (BLOCK, BLOCK), 0) <= lax.broadcasted_iota(
         jnp.int32, (BLOCK, BLOCK), 1
     )
@@ -333,15 +384,15 @@
     key_back_ref[...] = jnp.concatenate([key_sum[...], value_sum[...]], 1)
 
 
-def attend_back(query, keys, values, back, mixed, total, head, group):
-    length = query.shape[0]
+def attend_back(fields, back, mixed, total, head, group):
+    length = fields.shape[0]
     return pl.pallas_call(
         functools.partial(attend_back_kernel, head=head, group=group),
         out_shape=[
             jax.ShapeDtypeStruct((length, group * HEAD_DIM), jnp.float32),
             jax.ShapeDtypeStruct((length, 2 * HEAD_DIM), jnp.float32),
         ],
-        in_specs=[pl.BlockSpec(memory_space=pltpu.VMEM)] * 6,
+        in_specs=[pl.BlockSpec(memory_space=pltpu.VMEM)] * 4,
         out_specs=[pl.BlockSpec(memory_space=pltpu.VMEM)] * 2,
         scratch_shapes=[
             pltpu.VMEM((group, length, HEAD_DIM), jnp.bfloat16),
@@ -357,7 +408,127 @@
             flops=24 * 10**9, bytes_accessed=8 * 10**6, transcendentals=2 * 10**6
         ),
         name="attend_back",
-    )(query, keys, values, back, mixed, total)
+    )(fields, back, mixed, total)
+
+
+def partner_of(tile):
+    lane = lax.broadcasted_iota(jnp.int32, tile.shape, 1)
+    half = HEAD_DIM // 2
+    return jnp.where(
+        lane % HEAD_DIM < half, pltpu.roll(tile, LANES - half, 1), pltpu.roll(tile, half, 1)
+    )
+
+
+def normed_rows(tokens_ref, gains_ref):
+    resid = tokens_ref[...].astype(jnp.float32)
+    inv_rms = lax.rsqrt(jnp.mean(resid * resid, 1, keepdims=True) + EPS)
+    return resid, inv_rms, (resid * inv_rms * gains_ref[0:1, :]).astype(jnp.bfloat16)
+
+
+def project_kernel(tokens_ref, gains_ref, wide_ref, cosine_ref, sine_ref, fields_ref, normed):
+    _, _, normed[...] = normed_rows(tokens_ref, gains_ref)
+    first_key = tiles_of(HEADS * HEAD_DIM)
+    first_value = first_key + tiles_of(KV_HEADS * HEAD_DIM)
+    count = fields_ref.shape[1] // LANES
+    for start in range(0, count, 2):
+        stop = min(start + 2, count)
+        pair = dot_nn(normed[...], wide_ref[:, start * LANES : stop * LANES])
+        for at in range(start, stop):
+            tile = pair[:, (at - start) * LANES : (at - start + 1) * LANES]
+            if at < first_value:
+                tile = tile * cosine_ref[...] - partner_of(tile) * sine_ref[...]
+            tile = tile.astype(jnp.bfloat16)
+            if at < first_key:
+                tile = (tile.astype(jnp.float32) * HEAD_DIM ** (-0.5)).astype(jnp.bfloat16)
+            fields_ref[:, at * LANES : (at + 1) * LANES] = tile
+
+
+def vmem_call(kernel, out_shape, scratch_shapes, name, flops, *args):
+    single = not isinstance(out_shape, list)
+    return pl.pallas_call(
+        kernel,
+        out_shape=out_shape,
+        in_specs=[pl.BlockSpec(memory_space=pltpu.VMEM)] * len(args),
+        out_specs=pl.BlockSpec(memory_space=pltpu.VMEM)
+        if single
+        else [pl.BlockSpec(memory_space=pltpu.VMEM)] * len(out_shape),
+        scratch_shapes=scratch_shapes,
+        compiler_params=pltpu.CompilerParams(vmem_limit_bytes=VMEM_LIMIT),
+        cost_estimate=pl.CostEstimate(flops=flops, bytes_accessed=10**7, transcendentals=0),
+        name=name,
+    )(*args)
+
+
+def project(tokens, gains, wide, cosine, sine):
+    return vmem_call(
+        project_kernel,
+        jax.ShapeDtypeStruct((tokens.shape[0], wide.shape[1]), jnp.bfloat16),
+        [pltpu.VMEM(tokens.shape, jnp.bfloat16)],
+        "project",
+        8 * 10**9,
+        tokens, gains, wide, cosine, sine,
+    )
+
+
+def finish_kernel(
+    tokens_ref, gains_ref, wide_ref, cosine_ref, sine_ref, mid_back_ref, *refs, heads
+):
+    backs = refs[: 2 * heads]
+    input_grad_ref, tiled_ref, gain_ref, fields, normed_t = refs[2 * heads :]
+    half = HEAD_DIM
+    group = HEADS // heads
+    wide_heads = [(backs[2 * (at // group)], at % group * half) for at in range(HEADS)]
+    wide_heads += [None] * (HEADS % 2)
+    for offset in (0, half):
+        wide_heads += [(backs[2 * at + 1], offset) for at in range(heads)] + [None] * (heads % 2)
+    turned = tiles_of(HEADS * HEAD_DIM) + tiles_of(heads * HEAD_DIM)
+    for at in range(len(wide_heads) // 2):
+        cols = []
+        for item in wide_heads[2 * at : 2 * at + 2]:
+            if item is None:
+                cols.append(jnp.zeros((fields.shape[0], half), jnp.float32))
+            else:
+                cols.append(item[0][:, item[1] : item[1] + half])
+        tile = jnp.concatenate(cols, 1)
+        if at < turned:
+            tile = tile * cosine_ref[...] + partner_of(tile) * sine_ref[...]
+        fields[:, at * LANES : (at + 1) * LANES] = tile.astype(jnp.bfloat16)
+    resid, inv_rms, normed = normed_rows(tokens_ref, gains_ref)
+    normed_t[...] = normed.T
+    count = fields.shape[1] // LANES
+    for start in range(0, count, 2):
+        stop = min(start + 2, count)
+        pair = dot_nn(normed_t[...], fields[:, start * LANES : stop * LANES])
+        for at in range(start, stop):
+            tiled_ref[at] = pair[:, (at - start) * LANES : (at - start + 1) * LANES]
+    one_back = dot_nt(fields[...], wide_ref[...])
+    weighted = one_back * gains_ref[0:1, :]
+    cubed = inv_rms * inv_rms * inv_rms
+    scaled = resid * inv_rms
+    gain_ref[...] = jnp.sum(one_back * scaled, 0, keepdims=True)
+    mean = jnp.mean(weighted * resid, 1, keepdims=True)
+    grad = mid_back_ref[...] + inv_rms * weighted - resid * (cubed * mean)
+    input_grad_ref[...] = grad.astype(jnp.bfloat16)
+
+
+def finish(tokens, gains, wide, cosine, sine, mid_back, backs):
+    heads = len(backs)
+    rows, width = tokens.shape
+    return vmem_call(
+        functools.partial(finish_kernel, heads=heads),
+        [
+            jax.ShapeDtypeStruct(tokens.shape, jnp.bfloat16),
+            jax.ShapeDtypeStruct((wide.shape[1] // LANES, width, LANES), jnp.float32),
+            jax.ShapeDtypeStruct((1, width), jnp.float32),
+        ],
+        [
+            pltpu.VMEM((rows, wide.shape[1]), jnp.bfloat16),
+            pltpu.VMEM((width, rows), jnp.bfloat16),
+        ],
+        "finish",
+        12 * 10**9,
+        tokens, gains, wide, cosine, sine, mid_back, *[part for back in backs for part in back],
+    )
 
 
 def rotary_tables(length, head_dim):
@@ -447,21 +618,18 @@
         self.got = swap(self.held, CORE_MASK, self.devices)
         return other
 
-    def result(self):
+    def result(self, joined):
         if not self.stages:
-            return [
+            mats = [
                 lax.all_gather(shard, "dp", axis=0, tiled=True).reshape(shape)
                 for shard, shape in zip(self.shards, self.shapes)
             ]
-        return unpack_pieces(place_of(), (self.held, self.got), self.shapes, self.devices)
-
-
-def sum_all(field, devices):
-    step = 1
-    while step < devices:
-        field = field + swap(field, step, devices)
-        step *= 2
-    return field
+            if not joined:
+                return mats
+            pads = [((0, 0), (0, tiles_of(mat.shape[1]) * LANES - mat.shape[1])) for mat in mats]
+            return [jnp.concatenate([jnp.pad(mat, pad) for mat, pad in zip(mats, pads)], 1)]
+        pieces = (self.held, self.got)
+        return unpack_pieces(place_of(), pieces, self.shapes, self.devices, joined)
 
 
 def tied(first, second):
@@ -469,11 +637,11 @@
 
 
 class GradSum:
-    def __init__(self, grads, shapes, devices):
-        self.grads, self.shapes, self.devices = grads, shapes, devices
+    def __init__(self, grads, shapes, devices, extra=None):
+        self.grads, self.shapes, self.devices, self.extra = grads, shapes, devices, extra
         self.stages = whole_rows(shapes, devices)
         if self.stages:
-            self.kept, self.sent = pack_grads(place_of(), grads, shapes, devices)
+            self.kept, self.sent = pack_grads(place_of(), grads, shapes, devices, extra)
 
     def core_stage(self, other):
         if not self.stages:
@@ -512,16 +680,24 @@
 
     def result(self):
         if not self.stages:
-            return [
+            grads = [
+                grad.swapaxes(0, 1).reshape(rows, -1)[:, :wide] if grad.ndim == 3 else grad
+                for grad, (rows, wide) in zip(self.grads, self.shapes)
+            ]
+            sums = [
                 lax.psum_scatter(grad.reshape(-1), "dp", scatter_dimension=0, tiled=True)
-                for grad in self.grads
+                for grad in grads
             ]
+            return sums if self.extra is None else sums + [lax.psum(self.extra, "dp")]
         pieces = tree_sum([widen(term) for term in [self.parts[0]] + self.arrived])
         sums, start = [], 0
         for rows, wide in self.shapes:
             count = rows * wide // (self.devices * LANES)
             sums.append(pieces[start : start + count].reshape(-1))
             start += count
+        if self.extra is not None:
+            count = self.extra.size // LANES
+            sums.append(pieces[start : start + count].reshape(self.extra.shape))
         return sums
 
 
@@ -543,32 +719,18 @@
     tokens = first.plane_stage(tokens)
     tokens = second.line_stage(tokens)
     tokens = first.core_stage(tokens)
-    wq_mat, wk_mat, wv_mat = first.result()
+    (wide_mat,) = first.result(True)
     resid_in = tokens.astype(jnp.float32)
-    normed_one, rms_one = normalize(resid_in, gain_f[0])
-    normed_one = normed_one.astype(jnp.bfloat16)
-    query_lin = jnp.dot(normed_one, wq_mat, preferred_element_type=jnp.float32)
-    key_lin = jnp.dot(normed_one, wk_mat, preferred_element_type=jnp.float32)
-    value_lin = jnp.dot(normed_one, wv_mat, preferred_element_type=jnp.float32)
     cosine, sine = rotary_tables(LENGTH, HEAD_DIM)
-    tokens_here = seq_count * LENGTH
-    query_rot = rotate_heads(
-        query_lin.reshape(seq_count, LENGTH, HEADS, HEAD_DIM), cosine, sine
-    ).reshape(tokens_here, -1)
-    query_rot = (query_rot.astype(jnp.bfloat16).astype(jnp.float32) * scale_factor).astype(
-        jnp.bfloat16
-    )
-    key_rot = (
-        rotate_heads(key_lin.reshape(seq_count, LENGTH, KV_HEADS, HEAD_DIM), cosine, sine)
-        .reshape(tokens_here, -1)
-        .astype(jnp.bfloat16)
-    )
-    values = value_lin.astype(jnp.bfloat16)
-    values = second.plane_stage(values)
-    attended = [attend(query_rot, key_rot, values, head, group_size) for head in range(2)]
-    values, attended = second.core_stage((values, attended))
-    attended.append(attend(query_rot, key_rot, values, 2, group_size))
-    wo_mat, wg_mat, wu_mat, wd_mat = second.result()
+    pairs = LANES // HEAD_DIM
+    cosine = jnp.tile(cosine, (seq_count, 2 * pairs))
+    sine = jnp.tile(jnp.concatenate([sine, -sine], 1), (seq_count, pairs))
+    fields = project(tokens, gain_f, wide_mat, cosine, sine)
+    fields = second.plane_stage(fields)
+    attended = [attend(fields, head, group_size) for head in range(2)]
+    fields, attended = second.core_stage((fields, attended))
+    attended.append(attend(fields, 2, group_size))
+    wo_mat, wg_mat, wu_mat, wd_mat = second.result(False)
     mixed = jnp.concatenate([part for part, _ in attended], 1)
     attn_out = jnp.dot(mixed, wo_mat, preferred_element_type=jnp.float32)
     middle = resid_in + attn_out
@@ -599,46 +761,26 @@
 
     def back_of(head, field):
         part, total = attended[head]
-        return attend_back(query_rot, key_rot, values, field, part, total, head, group_size)
+        return attend_back(fields, field, part, total, head, group_size)
 
     mixed_back = feed_sum.core_stage(mixed_back)
     backs = [back_of(0, mixed_back)]
     mixed_back, _ = tied(mixed_back, backs[0])
     mixed_back = feed_sum.plane_stage(mixed_back)
     backs += [back_of(head, mixed_back) for head in range(1, KV_HEADS)]
-    backs = feed_sum.line_stage(backs)
-    rot_query_back = jnp.concatenate([back for back, _ in backs], 1).reshape(
-        seq_count, LENGTH, HEADS, HEAD_DIM
-    )
-    key_acc = jnp.concatenate([back[:, :HEAD_DIM] for _, back in backs], 1).reshape(
-        seq_count, LENGTH, KV_HEADS, HEAD_DIM
-    )
-    value_acc = jnp.concatenate([back[:, HEAD_DIM:] for _, back in backs], 1)
-    query_back = (
-        rotate_heads(rot_query_back, cosine, -sine)
-        .reshape(seq_count * LENGTH, model_width)
-        .astype(jnp.bfloat16)
-    )
-    key_back = (
-        rotate_heads(key_acc, cosine, -sine).reshape(seq_count * LENGTH, -1).astype(jnp.bfloat16)
-    )
-    value_back = value_acc.reshape(seq_count * LENGTH, -1).astype(jnp.bfloat16)
-    grad_query = outer_prod(normed_one, query_back)
-    grad_key = outer_prod(normed_one, key_back)
-    grad_value = outer_prod(normed_one, value_back)
-    one_back = (
-        times_transposed(query_back, wq_mat)
-        + times_transposed(key_back, wk_mat)
-        + times_transposed(value_back, wv_mat)
-    )
-    norm_one_back, gain_one = normalize_back(one_back, resid_in, rms_one, gain_f[0])
-    input_grad = (mid_back + norm_one_back).astype(jnp.bfloat16)
-    mix_sum = GradSum((grad_query, grad_key, grad_value, grad_out), shapes[:4], devices)
+    input_grad, tiled, gain_one = finish(tokens, gain_f, wide_mat, cosine, sine, mid_back, backs)
+    input_grad, tiled = feed_sum.line_stage((input_grad, tiled))
+    gains_back = jnp.concatenate([gain_one, gain_two[None]], 0)
+    cuts = [0]
+    for _, wide in shapes[:3]:
+        cuts.append(cuts[-1] + tiles_of(wide))
+    grads = tuple(tiled[start:stop] for start, stop in zip(cuts, cuts[1:])) + (grad_out,)
+    mix_sum = GradSum(grads, shapes[:4], devices, gains_back)
     input_grad = mix_sum.core_stage(input_grad)
     input_grad = mix_sum.plane_stage(input_grad)
     input_grad = mix_sum.line_stage(input_grad)
-    all_parts = mix_sum.result() + feed_sum.result()
-    gain_grad = sum_all(jnp.stack([gain_one, gain_two]), devices)
+    mix_parts = mix_sum.result()
+    all_parts, gain_grad = mix_parts[:4] + feed_sum.result(), mix_parts[4]
     return (output, input_grad) + tuple(all_parts) + (gain_grad,)
 
 

time: 297 us -> 293 us (0.987)
  Pallas kernels: 86.7 us -> 106 us
  matrix products: 61.9 us -> 50 us
  other arithmetic: 19 us -> 10.3 us
    pallas_call x0 -> x2, Pallas kernels: none -> 19.1 us  [vmem_call(): pl.pallas_call(kernel, out_shape=out_shape, in_specs=[pl.BlockSpec(memory...]
    concatenate x2 -> x0, local copies, waits for them, and re-layouts: 5.56 us -> none  [the longest x1 3.14 us: body(): jnp.concatenate([back for back, _ in backs], 1)]
    dot_general x7 -> x4, matrix products: 22.7 us -> 17.6 us  [times_transposed(): lax.dot_general(left, matrix, (((1,), (1,)), ((), ())), preferred_element...]
    dot_general x3 -> x0, matrix products: 4.38 us -> none  [the longest x1 2.6 us: body(): value_lin = jnp.dot(normed_one, wv_mat, preferred_element_type=jnp.float32)]
    another operation x5 -> x0, other arithmetic: 3.88 us -> none
    dot_general x7 -> x4, matrix products: 20 us -> 16.2 us  [outer_prod(): lax.dot_general(left, right, (((0,), (0,)), ((), ())), preferred_element_...]
    another operation x2 -> x4, local copies, waits for them, and re-layouts: 0.01 us -> 2.99 us  [the longest x2 1.94 us: body(): cosine = jnp.tile(cosine, (seq_count, 2 * pairs))]
    unnamed x98 -> x51, local copies, waits for them, and re-layouts: 6.09 us -> 8.11 us
  transfers between devices with their start and end apart: 33 -> 28, of which waited for: 16 -> 14; matrix products, arithmetic and copies ran while one was open for 7% -> 8% of each run, Pallas kernels for 21% -> 16%
where the time goes in v3:
time: 293 us; the launch traced here: 290 us
  Pallas kernels  106 us (36%)
  waiting for transfers between devices  58.7 us (20%)
  matrix products  50 us (17%)
  starting transfers between devices  36.6 us (12%)
  local copies, waits for them, and re-layouts  26.2 us (9%)
  other arithmetic  10.3 us (4%)
    ppermute x28, waiting for transfers between devices, swap(): lax.ppermute(field, 'dp', [(place, place ^ mask) for place in range(devic...  58.7 us
    ppermute x28, starting transfers between devices, swap(): lax.ppermute(field, 'dp', [(place, place ^ mask) for place in range(devic...  36.6 us
    pallas_call x3, Pallas kernels, attend_back(): pl.pallas_call(functools.partial(attend_back_kernel, head=head, group=gro...  32.5 us
    pallas_call x3, Pallas kernels, attend(): pl.pallas_call(functools.partial(attend_kernel, head=head, group=group),...  21.7 us
    pallas_call x2, Pallas kernels, vmem_call(): pl.pallas_call(kernel, out_shape=out_shape, in_specs=[pl.BlockSpec(memory...  19.1 us
    pallas_call x2, Pallas kernels, pack_grads(): pl.pallas_call(functools.partial(pack_kernel, devices=devices, shapes=sha...  17.7 us
    dot_general x4, matrix products, times_transposed(): lax.dot_general(left, matrix, (((1,), (1,)), ((), ())), preferred_element...  17.6 us
    dot_general x4, matrix products, outer_prod(): lax.dot_general(left, right, (((0,), (0,)), ((), ())), preferred_element_...  16.2 us
  transfers between devices with their start and end apart: 28, of which 14 were waited for; matrix products, arithmetic and copies ran while one was open for 8% of the time, Pallas kernels for 16%

profile of v3, /device:TPU:0, one launch (start us, length us, event | category | flops | bytes accessed | tf_op | source)
XLA Modules:
  0.0 289.5 jit_solution(4241167353123761284)
XLA Ops:
  1.4 3.1 %collective-permute-start = (bf16[135,128]{1,0:T(8,128)(2,1)S(1)}, bf16[135,128]{1,0:T(8,128)(2,1)S(1)}, u32[]{:S(2)}, u32[]{:S(2)}) collective-permute-start(bf16[135,128]{1,0:T(8,128)(2,1)S(1)} %pad_maximum_fusion.9), channel_id=1, source_target_pairs={{0,8},{1,9},{2,10},{3,11},{4,12},{5,13},{6,14},{7,15},{8,0},{9,1},... | collective-permute-start | bytes 103688 | tf_op jit(solution)/shard_map/ppermute | solution.py:31
  4.5 2.6 collective-permute-start.1
  7.1 2.9 collective-permute-done.1
  10.0 2.9 collective-permute-done.2
  12.9 1.6 collective-permute-start.3
  14.4 1.5 collective-permute-start.4
  17.3 1.8 collective-permute-done.3
  19.1 1.3 collective-permute-done.4
  20.4 1.5 collective-permute-done.5
  22.3 1.1 collective-permute-start.7
  23.4 3.3 %collective-permute-start.8 = (bf16[729,128]{1,0:T(8,128)(2,1)S(1)}, bf16[729,128]{1,0:T(8,128)(2,1)}, u32[]{:S(2)}, u32[]{:S(2)}) collective-permute-start(bf16[729,128]{1,0:T(8,128)(2,1)S(1)} %pad_maximum_fusion.7), channel_id=1, source_target_pairs={{0,24},{1,25},{2,26},{3,27},{4,28},{5,29},{6,30},{7,31},{8,16},{9,... | collective-permute-start | bytes 559880 | tf_op jit(solution)/shard_map/ppermute | solution.py:31
  26.7 1.2 fusion.13
  30.9 1.3 convert_element_type.303.gains_ref
  32.2 1.4 copy.50.tokens_ref
  33.6 5.4 %collective-permute-done.7 = bf16[729,128]{1,0:T(8,128)(2,1)} collective-permute-done((bf16[729,128]{1,0:T(8,128)(2,1)S(1)}, bf16[729,128]{1,0:T(8,128)(2,1)}, u32[]{:S(2)}, u32[]{:S(2)}) %collective-permute-start.7) | collective-permute-done | bytes 186656 | tf_op jit(solution)/shard_map/ppermute | solution.py:31
  39.0 1.2 pad_maximum_fusion.1
  41.2 5.5 %unpack.2.wide_ref = bf16[576,1152]{1,0:T(8,128)(2,1)} custom-call(s32[1]{0:T(128)} %bitcast.15.place_ref, bf16[16,135,128]{2,1,0:T(8,128)(2,1)} %copy-done.1, bf16[16,135,128]{2,1,0:T(8,128)(2,1)} %copy.52.got_ref), custom_call_target="tpu_custom_call" | custom-call | tf_op jit(solution)/shard_map/unpack/pallas_call | solution.py:175
  46.6 6.2 %project.1.fields_ref = bf16[1024,1152]{1,0:T(8,128)(2,1)} custom-call(bf16[1024,576]{1,0:T(8,128)(2,1)} %copy.50.tokens_ref, f32[2,576]{1,0:T(2,128)} %convert_element_type.303.gains_ref, bf16[576,1152]{1,0:T(8,128)(2,1)} %unpack.2.wide_ref, f32[1024,128]{1,0:T(8,128)} %copy.54.cosine_ref, f32[1024,128]{1,0:T(8,128)} %copy.55.sine_ref), custom_call_target="tpu_custom_call" | custom-call | flops 8000000000 | bytes 10000000 | tf_op jit(solution)/shard_map/project/pallas_call | solution.py:448
  54.4 2.4 collective-permute-start.12
  56.8 7.2 %attend.3 = (bf16[1024,192]{1,0:T(8,128)(2,1)}, f32[1024,128]{1,0:T(8,128)}) custom-call(bf16[1024,1152]{1,0:T(8,128)(2,1)} %project.1.fields_ref), custom_call_target="tpu_custom_call" | custom-call | flops 12000000000 | bytes 4000000 | tf_op jit(solution)/shard_map/attend/pallas_call | solution.py:311
  64.0 7.3 %attend.4 = (bf16[1024,192]{1,0:T(8,128)(2,1)}, f32[1024,128]{1,0:T(8,128)}) custom-call(bf16[1024,1152]{1,0:T(8,128)(2,1)} %project.1.fields_ref), custom_call_target="tpu_custom_call" | custom-call | flops 12000000000 | bytes 4000000 | tf_op jit(solution)/shard_map/attend/pallas_call | solution.py:311
  71.3 1.6 collective-permute-done.10
  73.0 14.4 %collective-permute-done.12 = bf16[4,729,128]{2,0,1:T(4,128)(2,1)S(1)} collective-permute-done((bf16[4,729,128]{2,0,1:T(4,128)(2,1)S(1)}, bf16[4,729,128]{2,0,1:T(4,128)(2,1)S(1)}, u32[]{:S(2)}, u32[]{:S(2)}) %collective-permute-start.12) | collective-permute-done | bytes 746528 | tf_op jit(solution)/shard_map/ppermute | solution.py:31
  88.5 2.8 copy.62
  91.3 1.7 copy.68
  93.1 7.2 %attend.5 = (bf16[1024,192]{1,0:T(8,128)(2,1)}, f32[1024,128]{1,0:T(8,128)}) custom-call(bf16[1024,1152]{1,0:T(8,128)(2,1)} %project.1.fields_ref), custom_call_target="tpu_custom_call" | custom-call | flops 12000000000 | bytes 4000000 | tf_op jit(solution)/shard_map/attend/pallas_call | solution.py:311
  100.3 4.3 %copy.63.got_ref = bf16[16,729,128]{2,1,0:T(8,128)(2,1)} copy(bf16[16,729,128]{2,0,1:T(8,128)(2,1)} %collective-permute-done.13) | data formatting | bytes 5971968 | tf_op jit(solution)/shard_map/ppermute | solution.py:31
  104.5 10.0 %unpack.3 = (bf16[576,576]{1,0:T(8,128)(2,1)}, bf16[576,1536]{1,0:T(8,128)(2,1)}, bf16[576,1536]{1,0:T(8,128)(2,1)}, bf16[1536,576]{1,0:T(8,128)(2,1)}) custom-call(s32[1]{0:T(128)} %bitcast.15.place_ref, bf16[16,729,128]{2,1,0:T(8,128)(2,1)} %copy-done, bf16[16,729,128]{2,1,0:T(8,128)(2,1)} %copy.63.got_ref), custom_call_target="tpu_custom_call" | custom-call | tf_op jit(solution)/shard_map/unpack/pallas_call | solution.py:175
  114.5 2.5 multiply_reduce_fusion.2
  117.4 1.1 copy-done.15
  118.6 4.6 %fusion.24 = f32[1024,1536]{1,0:T(8,128)} fusion(bf16[1024,576]{1,0:T(8,128)(2,1)S(1)} %multiply_convert_fusion.1, bf16[576,1536]{1,0:T(8,128)(2,1)S(1)} %copy-done.15), kind=kOutput, calls=%fused_computation.83 | convolution fusion | flops 1811939328 | bytes 9240576 | tf_op jit(solution)/shard_map/dot_general | solution.py:740
  123.2 4.6 %fusion.23 = f32[1024,1536]{1,0:T(8,128)} fusion(bf16[1024,576]{1,0:T(8,128)(2,1)S(1)} %multiply_convert_fusion.1, bf16[576,1536]{1,0:T(8,128)(2,1)S(1)} %copy-done.14), kind=kOutput, calls=%fused_computation.82 | convolution fusion | flops 1811939328 | bytes 9240576 | tf_op jit(solution)/shard_map/dot_general | solution.py:739
  127.8 9.5 %fusion.3 = (bf16[1024,1536]{1,0:T(8,128)(2,1)S(1)}, bf16[1024,1536]{1,0:T(8,128)(2,1)S(1)}, bf16[1024,1536]{1,0:T(8,128)(2,1)}) fusion(f32[1024,1536]{1,0:T(8,128)} %fusion.23, f32[1024,1536]{1,0:T(8,128)} %fusion.24, bf16[1536,576]{1,0:T(8,128)(2,1)S(1)} %copy-done.12, bf16[1024,576]{0,1:T(8,128)(2,1)S(1)} %copy-done.9), kind=kOutput, calls=%fused_computation.5 | convolution fusion | flops 1835532288 | bytes 24969216 | tf_op jit(solution)/shard_map/dot_general | solution.py:574
  137.3 2.6 fusion.28
  139.9 3.9 %fusion.26.refs_1_ = f32[576,1536]{1,0:T(8,128)} fusion(bf16[1024,576]{1,0:T(8,128)(2,1)S(1)} %multiply_convert_fusion.1, bf16[1024,1536]{1,0:T(8,128)(2,1)S(1)} %get-tuple-element.188), kind=kOutput, calls=%fused_computation.85 | convolution fusion | flops 1811939328 | bytes 7864320 | tf_op jit(solution)/shard_map/dot_general | solution.py:568
  143.7 3.8 %fusion.25.refs_0_ = f32[576,1536]{1,0:T(8,128)} fusion(bf16[1024,576]{1,0:T(8,128)(2,1)S(1)} %multiply_convert_fusion.1, bf16[1024,1536]{1,0:T(8,128)(2,1)S(1)} %get-tuple-element.189), kind=kOutput, calls=%fused_computation.84 | convolution fusion | flops 1811939328 | bytes 7864320 | tf_op jit(solution)/shard_map/dot_general | solution.py:568
  147.6 3.0 %multiply_reduce_fusion = (f32[576]{0:T(1024)S(1)}, f32[1024]{0:T(1024)S(1)}, f32[1024,576]{1,0:T(8,128)S(1)}) fusion(f32[1024,576]{1,0:T(8,128)S(1)} %get-tuple-element.222, f32[1024]{0:T(1024)S(1)} %get-tuple-element.217, f32[576]{0:T(1024)S(1)} %slice_reduce_fusion, f32[1024,576]{1,0:T(8,128)S(1)} %fusion.28, ...), kind=kOutput, calls=%fused_computation.9 | convolution fusion | flops 1816066560 | bytes 12005888 | tf_op jit(solution)/shard_map/dot_general | solution.py:574
  151.5 1.5 copy-done.4
  153.0 2.5 convolution_convert_fusion.back_ref
  155.5 4.6 %fusion.27.refs_2_ = f32[1536,576]{1,0:T(8,128)} fusion(bf16[1024,1536]{1,0:T(8,128)(2,1)S(1)} %copy-done.17, bf16[1024,576]{0,1:T(8,128)(2,1)S(1)} %copy-done.9), kind=kOutput, calls=%fused_computation.86 | convolution fusion | flops 1811939328 | bytes 7864320 | tf_op jit(solution)/shard_map/dot_general | solution.py:568
  160.1 10.4 %pack.2 = (bf16[16,648,128]{2,1,0:T(8,128)(2,1)}, bf16[16,648,128]{2,1,0:T(8,128)(2,1)}) custom-call(s32[1]{0:T(128)} %bitcast.15.place_ref, f32[576,1536]{1,0:T(8,128)} %fusion.25.refs_0_, f32[576,1536]{1,0:T(8,128)} %fusion.26.refs_1_, f32[1536,576]{1,0:T(8,128)} %fusion.27.refs_2_), custom_call_target="tpu_custom_call" | custom-call | tf_op jit(solution)/shard_map/pack/pallas_call | solution.py:229
  171.0 10.9 %attend_back.3 = (f32[1024,192]{1,0:T(8,128)}, f32[1024,128]{1,0:T(8,128)}) custom-call(bf16[1024,1152]{1,0:T(8,128)(2,1)} %project.1.fields_ref, bf16[1024,576]{1,0:T(8,128)(2,1)} %convolution_convert_fusion.back_ref, bf16[1024,192]{1,0:T(8,128)(2,1)} %get-tuple-element.100.mixed_ref, f32[1024,128]{1,0:T(8,128)} %get-tuple-element.117.total_ref), custom_call_target="tpu_custom_call" | custom-call | flops 24000000000 | bytes 8000000 | tf_op jit(solution)/shard_map/attend_back/pallas_call | solution.py:389
  181.9 3.9 %fusion.5.refs_3_ = f32[576,576]{1,0:T(8,128)} fusion(f32[1024,576]{1,0:T(8,128)S(1)} %copy-done.5, bf16[1024,192]{1,0:T(8,128)(2,1)} %get-tuple-element.103.mixed_ref, bf16[1024,192]{1,0:T(8,128)(2,1)} %get-tuple-element.101.mixed_ref, bf16[1024,192]{1,0:T(8,128)(2,1)} %get-tuple-element.100.mixed_ref), kind=kOutput, calls=%fused_computation.27 | convolution fusion | flops 683606016 | bytes 4866048 | tf_op jit(solution)/shard_map/dot_general | solution.py:568
  186.5 10.8 %attend_back.5 = (f32[1024,192]{1,0:T(8,128)}, f32[1024,128]{1,0:T(8,128)}) custom-call(bf16[1024,1152]{1,0:T(8,128)(2,1)} %project.1.fields_ref, bf16[1024,576]{1,0:T(8,128)(2,1)} %convolution_convert_fusion.back_ref, bf16[1024,192]{1,0:T(8,128)(2,1)} %get-tuple-element.103.mixed_ref, f32[1024,128]{1,0:T(8,128)} %get-tuple-element.129.total_ref), custom_call_target="tpu_custom_call" | custom-call | flops 24000000000 | bytes 8000000 | tf_op jit(solution)/shard_map/attend_back/pallas_call | solution.py:389
  197.4 10.8 %attend_back.4 = (f32[1024,192]{1,0:T(8,128)}, f32[1024,128]{1,0:T(8,128)}) custom-call(bf16[1024,1152]{1,0:T(8,128)(2,1)} %project.1.fields_ref, bf16[1024,576]{1,0:T(8,128)(2,1)} %convolution_convert_fusion.back_ref, bf16[1024,192]{1,0:T(8,128)(2,1)} %get-tuple-element.101.mixed_ref, f32[1024,128]{1,0:T(8,128)} %get-tuple-element.126.total_ref), custom_call_target="tpu_custom_call" | custom-call | flops 24000000000 | bytes 8000000 | tf_op jit(solution)/shard_map/attend_back/pallas_call | solution.py:389
  208.1 1.3 collective-permute-start.15
  210.5 1.2 collective-permute-start.17
  211.6 12.9 %finish.1 = (bf16[1024,576]{1,0:T(8,128)(2,1)}, f32[9,576,128]{2,1,0:T(8,128)}, f32[1,576]{1,0:T(1,128)}) custom-call(bf16[1024,576]{1,0:T(8,128)(2,1)} %copy.50.tokens_ref, f32[2,576]{1,0:T(2,128)} %convert_element_type.303.gains_ref, bf16[576,1152]{1,0:T(8,128)(2,1)} %unpack.2.wide_ref, f32[1024,128]{1,0:T(8,128)} %copy.54.cosine_ref, ...), custom_call_target="tpu_custom_call" | custom-call | flops 12000000000 | bytes 10000000 | tf_op jit(solution)/shard_map/finish/pallas_call | solution.py:448
  224.5 1.4 pad_maximum_fusion.10.refs_4_
  225.9 14.2 %collective-permute-done.16 = bf16[4,648,128]{2,1,0:T(8,128)(2,1)S(1)} collective-permute-done((bf16[4,648,128]{2,1,0:T(8,128)(2,1)S(1)}, bf16[4,648,128]{2,1,0:T(8,128)(2,1)S(1)}, u32[]{:S(2)}, u32[]{:S(2)}) %collective-permute-start.16) | collective-permute-done | bytes 663584 | tf_op jit(solution)/shard_map/ppermute | solution.py:31
  241.2 1.2 slice.206.refs_0_
  242.4 1.1 fusion.22
  243.5 7.3 %pack.3 = (bf16[16,232,128]{2,1,0:T(8,128)(2,1)}, bf16[16,232,128]{2,1,0:T(8,128)(2,1)}) custom-call(s32[1]{0:T(128)} %bitcast.15.place_ref, f32[5,576,128]{2,1,0:T(8,128)} %slice.206.refs_0_, f32[2,576,128]{2,1,0:T(8,128)} %get-tuple-element.196.refs_1_, f32[2,576,128]{2,1,0:T(8,128)} %get-tuple-element.195.refs_2_, f32[576,576]{1,0:T(8,128)} %fusion.5.refs_3_, ...), custom_call_target="tpu_custom_call" | custom-call | tf_op jit(solution)/shard_map/pack/pallas_call | solution.py:229
  250.9 4.5 %add_convert_fusion = bf16[1024,576]{1,0:T(8,128)(2,1)S(1)} fusion(f32[1024,576]{1,0:T(8,128)S(1)} %get-tuple-element.222, bf16[1024,1536]{1,0:T(8,128)(2,1)} %get-tuple-element.190, bf16[1536,576]{1,0:T(8,128)(2,1)S(1)} %copy-done.13), kind=kOutput, calls=%fused_computation.12 | convolution fusion | flops 1813118976 | bytes 8454144 | tf_op jit(solution)/shard_map/dot_general | solution.py:744
  255.4 1.4 copy.75
  256.8 4.6 %collective-permute-start.25 = (bf16[648,128]{1,0:T(8,128)(2,1)}, bf16[648,128]{1,0:T(8,128)(2,1)S(1)}, u32[]{:S(2)}, u32[]{:S(2)}) collective-permute-start(bf16[648,128]{1,0:T(8,128)(2,1)} %get-tuple-element.153), channel_id=1, source_target_pairs={{0,8},{1,9},{2,10},{3,11},{4,12},{5,13},{6,14},{7,15},{8,0},{9,1},... | collective-permute-start | bytes 497672 | tf_op jit(solution)/shard_map/ppermute | solution.py:31
  261.4 2.4 collective-permute-start.27
  265.8 3.1 %collective-permute-done.25 = bf16[648,128]{1,0:T(8,128)(2,1)S(1)} collective-permute-done((bf16[648,128]{1,0:T(8,128)(2,1)}, bf16[648,128]{1,0:T(8,128)(2,1)S(1)}, u32[]{:S(2)}, u32[]{:S(2)}) %collective-permute-start.25) | collective-permute-done | bytes 165920 | tf_op jit(solution)/shard_map/ppermute | solution.py:31
  268.9 1.2 collective-permute-start.21
  270.1 6.6 %collective-permute-done.26 = bf16[648,128]{1,0:T(8,128)(2,1)S(1)} collective-permute-done((bf16[648,128]{1,0:T(8,128)(2,1)}, bf16[648,128]{1,0:T(8,128)(2,1)S(1)}, u32[]{:S(2)}, u32[]{:S(2)}) %collective-permute-start.26) | collective-permute-done | bytes 165920 | tf_op jit(solution)/shard_map/ppermute | solution.py:31
  277.6 2.9 %collective-permute-start.22 = (bf16[232,128]{1,0:T(8,128)(2,1)S(1)}, bf16[232,128]{1,0:T(8,128)(2,1)S(1)}, u32[]{:S(2)}, u32[]{:S(2)}) collective-permute-start(bf16[232,128]{1,0:T(8,128)(2,1)S(1)} %get-tuple-element.149), channel_id=1, source_target_pairs={{0,8},{1,9},{2,10},{3,11},{4,12},{5,13},{6,14},{7,15},{8,0},{9,1},... | collective-permute-start | bytes 178184 | tf_op jit(solution)/shard_map/ppermute | solution.py:31
  280.5 2.4 collective-permute-start.24
  283.6 1.4 copy.76
  285.0 2.3 collective-permute-done.23
  (107 shorter events, 19.4 us)
Async XLA Ops:
  1.4 5.7 %collective-permute-start = (bf16[135,128]{1,0:T(8,128)(2,1)S(1)}, bf16[135,128]{1,0:T(8,128)(2,1)S(1)}, u32[]{:S(2)}, u32[]{:S(2)}) collective-permute-start(bf16[135,128]{1,0:T(8,128)(2,1)S(1)} %pad_maximum_fusion.9), channel_id=1, source_target_pairs={{0,8},{1,9},{2,10},{3,11},{4,12},{5,13},{6,14},{7,15},{8,0},{9,1},... | collective-permute-start | bytes 103688 | tf_op jit(solution)/shard_map/ppermute | solution.py:31
  4.5 5.5 %collective-permute-start.1 = (bf16[135,128]{1,0:T(8,128)(2,1)S(1)}, bf16[135,128]{1,0:T(8,128)(2,1)S(1)}, u32[]{:S(2)}, u32[]{:S(2)}) collective-permute-start(bf16[135,128]{1,0:T(8,128)(2,1)S(1)} %pad_maximum_fusion.9), channel_id=1, source_target_pairs={{0,16},{1,17},{2,18},{3,19},{4,20},{5,21},{6,22},{7,23},{8,24},{9,... | collective-permute-start | bytes 103688 | tf_op jit(solution)/shard_map/ppermute | solution.py:31
  7.1 5.7 %collective-permute-start.2 = (bf16[135,128]{1,0:T(8,128)(2,1)S(1)}, bf16[135,128]{1,0:T(8,128)(2,1)S(1)}, u32[]{:S(2)}, u32[]{:S(2)}) collective-permute-start(bf16[135,128]{1,0:T(8,128)(2,1)S(1)} %pad_maximum_fusion.9), channel_id=1, source_target_pairs={{0,24},{1,25},{2,26},{3,27},{4,28},{5,29},{6,30},{7,31},{8,16},{9,... | collective-permute-start | bytes 103688 | tf_op jit(solution)/shard_map/ppermute | solution.py:31
  12.9 6.3 %collective-permute-start.3 = (bf16[4,135,128]{2,1,0:T(8,128)(2,1)S(1)}, bf16[4,135,128]{2,1,0:T(8,128)(2,1)S(1)}, u32[]{:S(2)}, u32[]{:S(2)}) collective-permute-start(bf16[4,135,128]{2,1,0:T(8,128)(2,1)S(1)} %pad_maximum_fusion.8), channel_id=1, source_target_pairs={{0,2},{1,3},{2,0},{3,1},{4,6},{5,7},{6,4},{7,5},{8,10},{9,11},{10,... | collective-permute-start | bytes 414728 | tf_op jit(solution)/shard_map/ppermute | solution.py:31
  14.4 6.0 %collective-permute-start.4 = (bf16[4,135,128]{2,1,0:T(8,128)(2,1)S(1)}, bf16[4,135,128]{2,1,0:T(8,128)(2,1)S(1)}, u32[]{:S(2)}, u32[]{:S(2)}) collective-permute-start(bf16[4,135,128]{2,1,0:T(8,128)(2,1)S(1)} %pad_maximum_fusion.8), channel_id=1, source_target_pairs={{0,4},{1,5},{2,6},{3,7},{4,0},{5,1},{6,2},{7,3},{8,12},{9,13},{10,... | collective-permute-start | bytes 414728 | tf_op jit(solution)/shard_map/ppermute | solution.py:31
  15.9 6.0 %collective-permute-start.5 = (bf16[4,135,128]{2,1,0:T(8,128)(2,1)S(1)}, bf16[4,135,128]{2,1,0:T(8,128)(2,1)S(1)}, u32[]{:S(2)}, u32[]{:S(2)}) collective-permute-start(bf16[4,135,128]{2,1,0:T(8,128)(2,1)S(1)} %pad_maximum_fusion.8), channel_id=1, source_target_pairs={{0,6},{1,7},{2,4},{3,5},{4,2},{5,3},{6,0},{7,1},{8,14},{9,15},{10,... | collective-permute-start | bytes 414728 | tf_op jit(solution)/shard_map/ppermute | solution.py:31
  22.0 8.9 %copy-start.1 = (bf16[16,135,128]{2,1,0:T(8,128)(2,1)}, bf16[16,135,128]{2,1,0:T(8,128)(2,1)S(1)}, u32[]{:S(2)}) copy-start(bf16[16,135,128]{2,1,0:T(8,128)(2,1)S(1)} %constant_dynamic-update-slice_fusion.own_ref) | copy-start | bytes 1658884
  22.0 10.2 %copy-start.8 = (bf16[1024,576]{0,1:T(8,128)(2,1)S(1)}, bf16[1024,576]{0,1:T(8,128)(2,1)}, u32[]{:S(2)}) copy-start(bf16[1024,576]{0,1:T(8,128)(2,1)} %param.10) | copy-start | bytes 3538948
  22.1 18.1 %collective-permute-start.9 = (bf16[16,135,128]{2,0,1:T(8,128)(2,1)S(1)}, bf16[16,135,128]{2,0,1:T(8,128)(2,1)S(1)}, u32[]{:S(2)}, u32[]{:S(2)}) collective-permute-start(bf16[16,135,128]{2,0,1:T(8,128)(2,1)S(1)} %copy.51), channel_id=1, source_target_pairs={{0,1},{1,0},{2,3},{3,2},{4,5},{5,4},{6,7},{7,6},{8,9},{9,8},{10,11... | collective-permute-start | bytes 1658888 | tf_op jit(solution)/shard_map/ppermute | solution.py:31
  22.2 11.4 %collective-permute-start.6 = (bf16[729,128]{1,0:T(8,128)(2,1)S(1)}, bf16[729,128]{1,0:T(8,128)(2,1)}, u32[]{:S(2)}, u32[]{:S(2)}) collective-permute-start(bf16[729,128]{1,0:T(8,128)(2,1)S(1)} %pad_maximum_fusion.7), channel_id=1, source_target_pairs={{0,8},{1,9},{2,10},{3,11},{4,12},{5,13},{6,14},{7,15},{8,0},{9,1},... | collective-permute-start | bytes 559880 | tf_op jit(solution)/shard_map/ppermute | solution.py:31
  22.3 16.7 %collective-permute-start.7 = (bf16[729,128]{1,0:T(8,128)(2,1)S(1)}, bf16[729,128]{1,0:T(8,128)(2,1)}, u32[]{:S(2)}, u32[]{:S(2)}) collective-permute-start(bf16[729,128]{1,0:T(8,128)(2,1)S(1)} %pad_maximum_fusion.7), channel_id=1, source_target_pairs={{0,16},{1,17},{2,18},{3,19},{4,20},{5,21},{6,22},{7,23},{8,24},{9,... | collective-permute-start | bytes 559880 | tf_op jit(solution)/shard_map/ppermute | solution.py:31
  23.4 15.6 %collective-permute-start.8 = (bf16[729,128]{1,0:T(8,128)(2,1)S(1)}, bf16[729,128]{1,0:T(8,128)(2,1)}, u32[]{:S(2)}, u32[]{:S(2)}) collective-permute-start(bf16[729,128]{1,0:T(8,128)(2,1)S(1)} %pad_maximum_fusion.7), channel_id=1, source_target_pairs={{0,24},{1,25},{2,26},{3,27},{4,28},{5,29},{6,30},{7,31},{8,16},{9,... | collective-permute-start | bytes 559880 | tf_op jit(solution)/shard_map/ppermute | solution.py:31
  53.2 19.7 %collective-permute-start.10 = (bf16[4,729,128]{2,0,1:T(4,128)(2,1)S(1)}, bf16[4,729,128]{2,0,1:T(4,128)(2,1)S(1)}, u32[]{:S(2)}, u32[]{:S(2)}) collective-permute-start(bf16[4,729,128]{2,0,1:T(4,128)(2,1)S(1)} %copy.56), channel_id=1, source_target_pairs={{0,2},{1,3},{2,0},{3,1},{4,6},{5,7},{6,4},{7,5},{8,10},{9,11},{10,... | collective-permute-start | bytes 2239496 | tf_op jit(solution)/shard_map/ppermute | solution.py:31
  53.8 19.2 %collective-permute-start.11 = (bf16[4,729,128]{2,0,1:T(4,128)(2,1)S(1)}, bf16[4,729,128]{2,0,1:T(4,128)(2,1)S(1)}, u32[]{:S(2)}, u32[]{:S(2)}) collective-permute-start(bf16[4,729,128]{2,0,1:T(4,128)(2,1)S(1)} %copy.56), channel_id=1, source_target_pairs={{0,4},{1,5},{2,6},{3,7},{4,0},{5,1},{6,2},{7,3},{8,12},{9,13},{10,... | collective-permute-start | bytes 2239496 | tf_op jit(solution)/shard_map/ppermute | solution.py:31
  54.4 33.0 %collective-permute-start.12 = (bf16[4,729,128]{2,0,1:T(4,128)(2,1)S(1)}, bf16[4,729,128]{2,0,1:T(4,128)(2,1)S(1)}, u32[]{:S(2)}, u32[]{:S(2)}) collective-permute-start(bf16[4,729,128]{2,0,1:T(4,128)(2,1)S(1)} %copy.56), channel_id=1, source_target_pairs={{0,6},{1,7},{2,4},{3,5},{4,2},{5,3},{6,0},{7,1},{8,14},{9,15},{10,... | collective-permute-start | bytes 2239496 | tf_op jit(solution)/shard_map/ppermute | solution.py:31
  88.5 2.8 copy-start
  88.5 4.5 %copy-start.11 = (f32[2,576]{1,0:T(2,128)S(1)}, f32[2,576]{1,0:T(2,128)}, u32[]{:S(2)}) copy-start(f32[2,576]{1,0:T(2,128)} %convert_element_type.303.gains_ref) | copy-start | bytes 13828
  91.3 8.9 %collective-permute-start.13 = (bf16[16,729,128]{2,0,1:T(8,128)(2,1)}, bf16[16,729,128]{2,0,1:T(8,128)(2,1)}, u32[]{:S(2)}, u32[]{:S(2)}) collective-permute-start(bf16[16,729,128]{2,0,1:T(8,128)(2,1)} %copy.62), channel_id=1, source_target_pairs={{0,1},{1,0},{2,3},{3,2},{4,5},{5,4},{6,7},{7,6},{8,9},{9,8},{10,11... | collective-permute-start | bytes 8957960 | tf_op jit(solution)/shard_map/ppermute | solution.py:31
  104.5 10.0 %copy-start.6 = (bf16[1024,576]{1,0:T(8,128)(2,1)S(1)}, bf16[1024,576]{1,0:T(8,128)(2,1)}, u32[]{:S(2)}) copy-start(bf16[1024,576]{1,0:T(8,128)(2,1)} %copy.50.tokens_ref) | copy-start | bytes 3538948
  104.5 10.0 %copy-start.18 = (bf16[1024,192]{1,0:T(8,128)(2,1)S(1)}, bf16[1024,192]{1,0:T(8,128)(2,1)}, u32[]{:S(2)}) copy-start(bf16[1024,192]{1,0:T(8,128)(2,1)} %get-tuple-element.101.mixed_ref) | copy-start | bytes 1179652
  104.5 10.0 %copy-start.19 = (bf16[1024,192]{1,0:T(8,128)(2,1)S(1)}, bf16[1024,192]{1,0:T(8,128)(2,1)}, u32[]{:S(2)}) copy-start(bf16[1024,192]{1,0:T(8,128)(2,1)} %get-tuple-element.100.mixed_ref) | copy-start | bytes 1179652
  104.5 10.0 %copy-start.20 = (bf16[1024,192]{1,0:T(8,128)(2,1)S(1)}, bf16[1024,192]{1,0:T(8,128)(2,1)}, u32[]{:S(2)}) copy-start(bf16[1024,192]{1,0:T(8,128)(2,1)} %get-tuple-element.103.mixed_ref) | copy-start | bytes 1179652
  117.1 1.5 copy-start.15
  118.6 4.6 %copy-start.14 = (bf16[576,1536]{1,0:T(8,128)(2,1)S(1)}, bf16[576,1536]{1,0:T(8,128)(2,1)}, u32[]{:S(2)}) copy-start(bf16[576,1536]{1,0:T(8,128)(2,1)} %get-tuple-element.109) | copy-start | bytes 5308420
  123.2 4.6 %copy-start.9 = (bf16[1024,576]{0,1:T(8,128)(2,1)S(1)}, bf16[1024,576]{0,1:T(8,128)(2,1)}, u32[]{:S(2)}) copy-start(bf16[1024,576]{0,1:T(8,128)(2,1)} %param.11) | copy-start | bytes 3538948
  123.2 4.6 %copy-start.12 = (bf16[1536,576]{1,0:T(8,128)(2,1)S(1)}, bf16[1536,576]{1,0:T(8,128)(2,1)}, u32[]{:S(2)}) copy-start(bf16[1536,576]{1,0:T(8,128)(2,1)} %get-tuple-element.111) | copy-start | bytes 5308420
  150.6 2.4 copy-start.16
  151.5 1.5 copy-start.4
  153.0 2.5 copy-start.17
  170.5 11.4 %copy-start.5 = (f32[1024,576]{1,0:T(8,128)S(1)}, f32[1024,576]{1,0:T(8,128)}, u32[]{:S(2)}) copy-start(f32[1024,576]{1,0:T(8,128)} %copy-done.4) | copy-start | bytes 7077892
  170.5 15.4 %collective-permute-start.14 = (bf16[16,648,128]{2,1,0:T(8,128)(2,1)}, bf16[16,648,128]{2,1,0:T(8,128)(2,1)S(1)}, u32[]{:S(2)}, u32[]{:S(2)}) collective-permute-start(bf16[16,648,128]{2,1,0:T(8,128)(2,1)} %get-tuple-element.115), channel_id=1, source_target_pairs={{0,1},{1,0},{2,3},{3,2},{4,5},{5,4},{6,7},{7,6},{8,9},{9,8},{10,11... | collective-permute-start | bytes 7962632 | tf_op jit(solution)/shard_map/ppermute | solution.py:31
  181.9 3.9 %copy-start.3 = (bf16[16,648,128]{2,1,0:T(8,128)(2,1)S(1)}, bf16[16,648,128]{2,1,0:T(8,128)(2,1)}, u32[]{:S(2)}) copy-start(bf16[16,648,128]{2,1,0:T(8,128)(2,1)} %get-tuple-element.114) | copy-start | bytes 7962628
  208.1 17.8 %collective-permute-start.15 = (bf16[4,648,128]{2,1,0:T(8,128)(2,1)S(1)}, bf16[4,648,128]{2,1,0:T(8,128)(2,1)S(1)}, u32[]{:S(2)}, u32[]{:S(2)}) collective-permute-start(bf16[4,648,128]{2,1,0:T(8,128)(2,1)S(1)} %get-tuple-element.122), channel_id=1, source_target_pairs={{0,2},{1,3},{2,0},{3,1},{4,6},{5,7},{6,4},{7,5},{8,10},{9,11},{10,... | collective-permute-start | bytes 1990664 | tf_op jit(solution)/shard_map/ppermute | solution.py:31
  209.5 30.7 %collective-permute-start.16 = (bf16[4,648,128]{2,1,0:T(8,128)(2,1)S(1)}, bf16[4,648,128]{2,1,0:T(8,128)(2,1)S(1)}, u32[]{:S(2)}, u32[]{:S(2)}) collective-permute-start(bf16[4,648,128]{2,1,0:T(8,128)(2,1)S(1)} %get-tuple-element.123), channel_id=1, source_target_pairs={{0,4},{1,5},{2,6},{3,7},{4,0},{5,1},{6,2},{7,3},{8,12},{9,13},{10,... | collective-permute-start | bytes 1990664 | tf_op jit(solution)/shard_map/ppermute | solution.py:31
  210.5 29.7 %collective-permute-start.17 = (bf16[4,648,128]{2,1,0:T(8,128)(2,1)S(1)}, bf16[4,648,128]{2,1,0:T(8,128)(2,1)S(1)}, u32[]{:S(2)}, u32[]{:S(2)}) collective-permute-start(bf16[4,648,128]{2,1,0:T(8,128)(2,1)S(1)} %get-tuple-element.124), channel_id=1, source_target_pairs={{0,6},{1,7},{2,4},{3,5},{4,2},{5,3},{6,0},{7,1},{8,14},{9,15},{10,... | collective-permute-start | bytes 1990664 | tf_op jit(solution)/shard_map/ppermute | solution.py:31
  224.5 16.7 %copy-start.2 = (f32[9,576,128]{2,1,0:T(8,128)S(1)}, f32[9,576,128]{2,1,0:T(8,128)}, u32[]{:S(2)}) copy-start(f32[9,576,128]{2,1,0:T(8,128)} %get-tuple-element.134) | copy-start | bytes 7962628
  243.5 7.3 %copy-start.13 = (bf16[1536,576]{1,0:T(8,128)(2,1)S(1)}, bf16[1536,576]{1,0:T(8,128)(2,1)}, u32[]{:S(2)}) copy-start(bf16[1536,576]{1,0:T(8,128)(2,1)} %get-tuple-element.111) | copy-start | bytes 5308420
  250.9 12.9 %collective-permute-start.18 = (bf16[16,232,128]{2,1,0:T(8,128)(2,1)}, bf16[16,232,128]{2,1,0:T(8,128)(2,1)S(1)}, u32[]{:S(2)}, u32[]{:S(2)}) collective-permute-start(bf16[16,232,128]{2,1,0:T(8,128)(2,1)} %get-tuple-element.140), channel_id=1, source_target_pairs={{0,1},{1,0},{2,3},{3,2},{4,5},{5,4},{6,7},{7,6},{8,9},{9,8},{10,11... | collective-permute-start | bytes 2850824 | tf_op jit(solution)/shard_map/ppermute | solution.py:31
  255.4 8.4 %copy-start.10 = (bf16[16,232,128]{2,1,0:T(8,128)(2,1)S(1)}, bf16[16,232,128]{2,1,0:T(8,128)(2,1)}, u32[]{:S(2)}) copy-start(bf16[16,232,128]{2,1,0:T(8,128)(2,1)} %get-tuple-element.139) | copy-start | bytes 2850820
  256.8 26.8 %copy-start.7 = (bf16[1024,576]{1,0:T(8,128)(2,1)S(1)}, bf16[1024,576]{1,0:T(8,128)(2,1)}, u32[]{:S(2)}) copy-start(bf16[1024,576]{1,0:T(8,128)(2,1)} %get-tuple-element.177) | copy-start | bytes 3538948
  256.8 12.1 %collective-permute-start.25 = (bf16[648,128]{1,0:T(8,128)(2,1)}, bf16[648,128]{1,0:T(8,128)(2,1)S(1)}, u32[]{:S(2)}, u32[]{:S(2)}) collective-permute-start(bf16[648,128]{1,0:T(8,128)(2,1)} %get-tuple-element.153), channel_id=1, source_target_pairs={{0,8},{1,9},{2,10},{3,11},{4,12},{5,13},{6,14},{7,15},{8,0},{9,1},... | collective-permute-start | bytes 497672 | tf_op jit(solution)/shard_map/ppermute | solution.py:31
  261.4 15.3 %collective-permute-start.26 = (bf16[648,128]{1,0:T(8,128)(2,1)}, bf16[648,128]{1,0:T(8,128)(2,1)S(1)}, u32[]{:S(2)}, u32[]{:S(2)}) collective-permute-start(bf16[648,128]{1,0:T(8,128)(2,1)} %get-tuple-element.154), channel_id=1, source_target_pairs={{0,16},{1,17},{2,18},{3,19},{4,20},{5,21},{6,22},{7,23},{8,24},{9,... | collective-permute-start | bytes 497672 | tf_op jit(solution)/shard_map/ppermute | solution.py:31
  261.4 15.3 %collective-permute-start.27 = (bf16[648,128]{1,0:T(8,128)(2,1)S(1)}, bf16[648,128]{1,0:T(8,128)(2,1)S(1)}, u32[]{:S(2)}, u32[]{:S(2)}) collective-permute-start(bf16[648,128]{1,0:T(8,128)(2,1)S(1)} %get-tuple-element.155), channel_id=1, source_target_pairs={{0,24},{1,25},{2,26},{3,27},{4,28},{5,29},{6,30},{7,31},{8,16},{9,... | collective-permute-start | bytes 497672 | tf_op jit(solution)/shard_map/ppermute | solution.py:31
  264.0 12.8 %collective-permute-start.19 = (bf16[4,232,128]{2,1,0:T(8,128)(2,1)S(1)}, bf16[4,232,128]{2,1,0:T(8,128)(2,1)S(1)}, u32[]{:S(2)}, u32[]{:S(2)}) collective-permute-start(bf16[4,232,128]{2,1,0:T(8,128)(2,1)S(1)} %get-tuple-element.143), channel_id=1, source_target_pairs={{0,2},{1,3},{2,0},{3,1},{4,6},{5,7},{6,4},{7,5},{8,10},{9,11},{10,... | collective-permute-start | bytes 712712 | tf_op jit(solution)/shard_map/ppermute | solution.py:31
  264.8 12.0 %collective-permute-start.20 = (bf16[4,232,128]{2,1,0:T(8,128)(2,1)S(1)}, bf16[4,232,128]{2,1,0:T(8,128)(2,1)S(1)}, u32[]{:S(2)}, u32[]{:S(2)}) collective-permute-start(bf16[4,232,128]{2,1,0:T(8,128)(2,1)S(1)} %get-tuple-element.144), channel_id=1, source_target_pairs={{0,4},{1,5},{2,6},{3,7},{4,0},{5,1},{6,2},{7,3},{8,12},{9,13},{10,... | collective-permute-start | bytes 712712 | tf_op jit(solution)/shard_map/ppermute | solution.py:31
  268.9 8.5 %collective-permute-start.21 = (bf16[4,232,128]{2,1,0:T(8,128)(2,1)S(1)}, bf16[4,232,128]{2,1,0:T(8,128)(2,1)S(1)}, u32[]{:S(2)}, u32[]{:S(2)}) collective-permute-start(bf16[4,232,128]{2,1,0:T(8,128)(2,1)S(1)} %get-tuple-element.145), channel_id=1, source_target_pairs={{0,6},{1,7},{2,4},{3,5},{4,2},{5,3},{6,0},{7,1},{8,14},{9,15},{10,... | collective-permute-start | bytes 712712 | tf_op jit(solution)/shard_map/ppermute | solution.py:31
  277.6 7.5 %collective-permute-start.22 = (bf16[232,128]{1,0:T(8,128)(2,1)S(1)}, bf16[232,128]{1,0:T(8,128)(2,1)S(1)}, u32[]{:S(2)}, u32[]{:S(2)}) collective-permute-start(bf16[232,128]{1,0:T(8,128)(2,1)S(1)} %get-tuple-element.149), channel_id=1, source_target_pairs={{0,8},{1,9},{2,10},{3,11},{4,12},{5,13},{6,14},{7,15},{8,0},{9,1},... | collective-permute-start | bytes 178184 | tf_op jit(solution)/shard_map/ppermute | solution.py:31
  280.5 6.9 %collective-permute-start.23 = (bf16[232,128]{1,0:T(8,128)(2,1)S(1)}, bf16[232,128]{1,0:T(8,128)(2,1)S(1)}, u32[]{:S(2)}, u32[]{:S(2)}) collective-permute-start(bf16[232,128]{1,0:T(8,128)(2,1)S(1)} %get-tuple-element.150), channel_id=1, source_target_pairs={{0,16},{1,17},{2,18},{3,19},{4,20},{5,21},{6,22},{7,23},{8,24},{9,... | collective-permute-start | bytes 178184 | tf_op jit(solution)/shard_map/ppermute | solution.py:31
  280.5 6.8 %collective-permute-start.24 = (bf16[232,128]{1,0:T(8,128)(2,1)S(1)}, bf16[232,128]{1,0:T(8,128)(2,1)S(1)}, u32[]{:S(2)}, u32[]{:S(2)}) collective-permute-start(bf16[232,128]{1,0:T(8,128)(2,1)S(1)} %get-tuple-element.151), channel_id=1, source_target_pairs={{0,24},{1,25},{2,26},{3,27},{4,28},{5,29},{6,30},{7,31},{8,16},{9,... | collective-permute-start | bytes 178184 | tf_op jit(solution)/shard_map/ppermute | solution.py:31

commit v4 on v3

--- a/solution.py
+++ b/solution.py
@@ -19,6 +19,7 @@
 LANES = 128
 VMEM_LIMIT = 56 * 1024 * 1024
 CORE_MASK = 1
+LIGHT = pl.CostEstimate(flops=10**8, bytes_accessed=10**6, transcendentals=0)
 
 
 def masks_of(devices):
@@ -46,69 +47,6 @@
     return core * CORE_MASK + 2 * (slot // line) + 8 * (slot % line)
 
 
-def each_group(devices, step, body):
-    group = 4
-
-    def run(at, carry):
-        for inner in range(group):
-            body(at * group + inner, pl.multiple_of(at * group * step, 8) + inner * step)
-        return carry
-
-    lax.fori_loop(0, devices // group, run, 0)
-
-
-def half_tiles(tiles):
-    lane = lax.broadcasted_iota(jnp.int32, tiles[0].shape, 1)
-    rolled = [pltpu.roll(tile, LANES // 2, 1) for tile in tiles]
-    shifted = [
-        jnp.where(lane < LANES // 2, rolled[at], rolled[at + 1]) for at in range(len(tiles) - 1)
-    ]
-    return shifted + [rolled[-1]]
-
-
-def unpack_rows(stage, owner, start, rows, wide, target, row):
-    whole = wide // LANES
-    if wide % LANES == 0:
-        for at in range(whole):
-            target[at, pl.ds(row, rows), :] = stage[
-                owner, pl.ds(start + at, rows, stride=whole), :
-            ]
-        return
-    pairs, tiles_in = rows // 2, 2 * wide // LANES
-    tiles = [stage[owner, pl.ds(start + at, pairs, stride=tiles_in), :] for at in range(tiles_in)]
-    for at in range(whole):
-        target[at, pl.ds(row, pairs, stride=2), :] = tiles[at]
-    target[whole, pl.ds(row, pairs, stride=2), :] = tiles[whole]
-    for at, tile in enumerate(half_tiles(tiles[whole:])):
-        target[at, pl.ds(row + 1, pairs, stride=2), :] = tile
-
-
-def pack_rows(source, row, rows, wide, stage, owner, start):
-    whole = wide // LANES
-    if wide % LANES == 0:
-        for at in range(whole):
-            stage[owner, pl.ds(start + at, rows, stride=whole), :] = source[
-                at, pl.ds(row, rows), :
-            ]
-        return
-    pairs, tiles_in = rows // 2, 2 * wide // LANES
-    even = [
-        source[at, pl.ds(row, pairs, stride=2), :] for at in range(whole + 1)
-    ]
-    odd = [
-        source[at, pl.ds(row + 1, pairs, stride=2), :]
-        for at in range(whole + 1)
-    ]
-    lane = lax.broadcasted_iota(jnp.int32, even[0].shape, 1)
-    rolled = [pltpu.roll(tile, LANES // 2, 1) for tile in odd]
-    tiles = even[:whole]
-    tiles.append(jnp.where(lane < LANES // 2, even[whole], rolled[0]))
-    for at in range(whole):
-        tiles.append(jnp.where(lane < LANES // 2, rolled[at], rolled[at + 1]))
-    for at in range(tiles_in):
-        stage[owner, pl.ds(start + at, pairs, stride=tiles_in), :] = tiles[at]
-
-
 def tiles_of(wide):
     return -(-wide // LANES)
 
@@ -117,54 +55,73 @@
     return [min(LANES, wide - at) for at in range(0, wide, LANES)]
 
 
-def load_stage(place_ref, own_ref, got_ref, stage, devices):
+def flat_starts(shapes, devices):
+    starts = [0]
+    for rows, wide in shapes:
+        starts.append(starts[-1] + rows * wide // (devices * LANES))
+    return starts
+
+
+def tiled_shapes(shapes):
+    return [(tiles_of(wide), rows, LANES) for rows, wide in shapes if wide % LANES]
+
+
+def unpack_kernel(place_ref, *refs, devices, shapes, joined, count):
+    pieces, refs = refs[:count], refs[count:]
+    out_count = 1 if joined else len(shapes)
+    outs, flats, refs = refs[:out_count], refs[out_count : out_count + len(shapes)], refs[out_count + len(shapes) :]
+    stage, tiled_refs = refs[0], list(refs[1:])
     place = place_ref[0]
-    for core, pieces in enumerate((own_ref, got_ref)):
-
-        def load(slot, carry, core=core, pieces=pieces):
-            owner = place ^ slot_mask(core, slot, devices)
-            stage[owner] = pieces[slot].astype(jnp.float32)
+    starts = flat_starts(shapes, devices)
+    block = pieces[0].shape[0]
+    for index, piece_ref in enumerate(pieces):
+        core, plane = index * block * 2 // devices, index % (devices // 2 // block)
+
+        def load(slot, carry, core=core, plane=plane, piece_ref=piece_ref):
+            owner = place ^ slot_mask(core, plane * block + slot, devices)
+            piece = piece_ref[slot].astype(jnp.float32)
+            if any(start % 8 for start in starts[:-1]):
+                stage[slot % 4] = piece
+            for flat, start, stop in zip(flats, starts, starts[1:]):
+                each = stop - start
+                rows = stage[slot % 4, start:stop, :] if start % 8 else piece[start:stop]
+                flat[pl.ds(owner * each, each), :] = rows
             return carry
 
-        lax.fori_loop(0, devices // 2, load, 0)
-
-
-def store_stage(kept_ref, sent_ref, stage, devices):
-    for core, pieces in enumerate((kept_ref, sent_ref)):
-
-        def store(slot, carry, core=core, pieces=pieces):
-            pieces[slot] = stage[slot_mask(core, slot, devices)].astype(jnp.bfloat16)
-            return carry
-
-        lax.fori_loop(0, devices // 2, store, 0)
-
-
-def unpack_kernel(place_ref, own_ref, got_ref, *refs, devices, shapes, joined):
-    count = 1 if joined else len(shapes)
-    outs, stage, wides = refs[:count], refs[count], refs[count + 1 :]
-    load_stage(place_ref, own_ref, got_ref, stage, devices)
-    start, column = 0, 0
-    for index, ((rows, wide), target) in enumerate(zip(shapes, wides)):
+        lax.fori_loop(0, block, load, 0)
+    column = 0
+    for index, ((rows, wide), flat) in enumerate(zip(shapes, flats)):
         out = outs[0 if joined else index]
-        each = rows // devices
-        each_group(
-            devices,
-            each,
-            lambda owner, row, start=start, each=each, wide=wide, target=target: unpack_rows(
-                stage, owner, start, each, wide, target, row
-            ),
-        )
-        start += each * wide // LANES
-        for at, width in enumerate(tile_widths(wide)):
-            tile = target[at]
-            if joined and width < LANES:
-                lane = lax.broadcasted_iota(jnp.int32, tile.shape, 1)
-                tile = jnp.where(lane < width, tile, 0.0)
-                width = LANES
-            out[:, column : column + width] = tile[:, :width].astype(jnp.bfloat16)
-            column += width
-        if not joined:
-            column = 0
+        whole = wide // LANES
+        if wide % LANES == 0:
+            for at in range(whole):
+                tile = flat[pl.ds(at, rows, stride=whole), :]
+                out[:, column + at * LANES : column + (at + 1) * LANES] = tile.astype(jnp.bfloat16)
+        else:
+            target = tiled_refs.pop(0)
+            pairs, tiles_in = rows // 2, 2 * wide // LANES
+            for at in range(whole + 1):
+                target[at, pl.ds(0, pairs, stride=2), :] = flat[pl.ds(at, pairs, stride=tiles_in), :]
+            rolled = None
+            for at in range(whole, tiles_in):
+                after = pltpu.roll(flat[pl.ds(at, pairs, stride=tiles_in), :], LANES // 2, 1)
+                if rolled is not None:
+                    lane = lax.broadcasted_iota(jnp.int32, after.shape, 1)
+                    target[at - whole - 1, pl.ds(1, pairs, stride=2), :] = jnp.where(
+                        lane < LANES // 2, rolled, after
+                    )
+                rolled = after
+            target[whole, pl.ds(1, pairs, stride=2), :] = rolled
+            for at, width in enumerate(tile_widths(wide)):
+                tile = target[at]
+                if joined and width < LANES:
+                    lane = lax.broadcasted_iota(jnp.int32, tile.shape, 1)
+                    tile = jnp.where(lane < width, tile, 0.0)
+                    width = LANES
+                start = column + at * LANES
+                out[:, start : start + width] = tile[:, :width].astype(jnp.bfloat16)
+        if joined:
+            column += tiles_of(wide) * LANES
 
 
 def unpack_pieces(place, pieces, shapes, devices, joined):
@@ -173,13 +130,20 @@
     if joined:
         outs = [(shapes[0][0], sum(tiles_of(wide) for _, wide in shapes) * LANES)]
     return pl.pallas_call(
-        functools.partial(unpack_kernel, devices=devices, shapes=shapes, joined=joined),
+        functools.partial(
+            unpack_kernel, devices=devices, shapes=shapes, joined=joined, count=len(pieces)
+        ),
         out_shape=[jax.ShapeDtypeStruct(shape, jnp.bfloat16) for shape in outs],
-        in_specs=[pl.BlockSpec(memory_space=pltpu.SMEM)] + [pl.BlockSpec(memory_space=pltpu.VMEM)] * 2,
+        in_specs=[pl.BlockSpec(memory_space=pltpu.SMEM)]
+        + [pl.BlockSpec(memory_space=pltpu.VMEM)] * len(pieces),
         out_specs=[pl.BlockSpec(memory_space=pltpu.VMEM)] * len(outs),
-        scratch_shapes=[pltpu.VMEM((devices, rows_in, LANES), jnp.float32)]
-        + [pltpu.VMEM((-(-wide // LANES), rows, LANES), jnp.float32) for rows, wide in shapes],
+        scratch_shapes=[
+            pltpu.VMEM((rows * wide // LANES, LANES), jnp.float32) for rows, wide in shapes
+        ]
+        + [pltpu.VMEM((4, rows_in, LANES), jnp.float32)]
+        + [pltpu.VMEM(shape, jnp.float32) for shape in tiled_shapes(shapes)],
         compiler_params=pltpu.CompilerParams(vmem_limit_bytes=VMEM_LIMIT),
+        cost_estimate=LIGHT,
         name="unpack",
     )(place, *pieces)
 
@@ -187,35 +151,64 @@
 def pack_kernel(place_ref, *refs, devices, shapes, tiled_in, extra):
     count = len(shapes) + (1 if extra else 0)
     sources, kept_ref, sent_ref, stage = refs[:count], refs[count], refs[count + 1], refs[count + 2]
-    wides = list(refs[count + 3 :])
+    flats = refs[count + 3 : count + 3 + len(shapes)]
+    tiled_refs = list(refs[count + 3 + len(shapes) :])
     place = place_ref[0]
-    start = 0
-    for index, (rows, wide) in enumerate(shapes):
-        each = rows // devices
-        source = sources[index]
+    starts = flat_starts(shapes, devices)
+    for index, ((rows, wide), flat) in enumerate(zip(shapes, flats)):
+        source, whole = sources[index], wide // LANES
+        if wide % LANES == 0:
+            for at in range(whole):
+                flat[pl.ds(at, rows, stride=whole), :] = (
+                    source[at] if tiled_in[index] else source[:, at * LANES : (at + 1) * LANES]
+                )
+            continue
         if not tiled_in[index]:
-            tiled = wides.pop(0)
+            tiled = tiled_refs.pop(0)
             for at, width in enumerate(tile_widths(wide)):
                 tiled[at, :, :width] = source[:, at * LANES : at * LANES + width]
             source = tiled
-        each_group(
-            devices,
-            each,
-            lambda owner, row, start=start, each=each, wide=wide, source=source: pack_rows(
-                source, row, each, wide, stage, place ^ owner, start
-            ),
-        )
-        start += each * wide // LANES
+        pairs, tiles_in = rows // 2, 2 * wide // LANES
+        for at in range(whole):
+            flat[pl.ds(at, pairs, stride=tiles_in), :] = source[at, pl.ds(0, pairs, stride=2), :]
+        before = source[whole, pl.ds(0, pairs, stride=2), :]
+        lane = lax.broadcasted_iota(jnp.int32, before.shape, 1)
+        for at in range(whole + 1):
+            rolled = pltpu.roll(source[at, pl.ds(1, pairs, stride=2), :], LANES // 2, 1)
+            flat[pl.ds(whole + at, pairs, stride=tiles_in), :] = jnp.where(
+                lane < LANES // 2, before, rolled
+            )
+            before = rolled
+    row_tiles = []
     if extra:
         row = jnp.concatenate([sources[-1][at : at + 1, :] for at in range(extra[0])], 1)
-        for at in range(extra[0] * extra[1] // LANES):
-            tile = row[:, at * LANES : (at + 1) * LANES].reshape(1, 1, LANES)
-            stage[:, start + at : start + at + 1, :] = jnp.broadcast_to(tile, (devices, 1, LANES))
-        start += extra[0] * extra[1] // LANES
-        spare = stage.shape[1] - start
-        if spare:
-            stage[:, start:, :] = jnp.zeros((devices, spare, LANES), jnp.float32)
-    store_stage(kept_ref, sent_ref, stage, devices)
+        row_tiles = [
+            row[:, at * LANES : (at + 1) * LANES] for at in range(extra[0] * extra[1] // LANES)
+        ]
+    direct = not extra and all(start % 8 == 0 for start in starts)
+    if not direct:
+        for at in range(4):
+            for index, tile in enumerate(row_tiles):
+                stage[at, starts[-1] + index : starts[-1] + index + 1, :] = tile
+            used = starts[-1] + len(row_tiles)
+            if used < stage.shape[1]:
+                stage[at, used:, :] = jnp.zeros((stage.shape[1] - used, LANES), jnp.float32)
+    for core, pieces in enumerate((kept_ref, sent_ref)):
+
+        def store(slot, carry, core=core, pieces=pieces):
+            owner = place ^ slot_mask(core, slot, devices)
+            parts = []
+            for flat, start, stop in zip(flats, starts, starts[1:]):
+                rows = flat[pl.ds(owner * (stop - start), stop - start), :]
+                if direct:
+                    parts.append(rows)
+                else:
+                    stage[slot % 4, start:stop, :] = rows
+            piece = jnp.concatenate(parts, 0) if direct else stage[slot % 4]
+            pieces[slot] = piece.astype(jnp.bfloat16)
+            return carry
+
+        lax.fori_loop(0, devices // 2, store, 0)
 
 
 def pack_grads(place, grads, shapes, devices, extra):
@@ -226,6 +219,7 @@
         sources.append(extra)
     tiled_in = tuple(grad.ndim == 3 for grad in grads)
     half = jax.ShapeDtypeStruct((devices // 2, rows_out, LANES), jnp.bfloat16)
+    untiled = [shape for shape, tiled in zip(shapes, tiled_in) if not tiled]
     return pl.pallas_call(
         functools.partial(
             pack_kernel, devices=devices, shapes=shapes, tiled_in=tiled_in,
@@ -235,13 +229,11 @@
         in_specs=[pl.BlockSpec(memory_space=pltpu.SMEM)]
         + [pl.BlockSpec(memory_space=pltpu.VMEM)] * len(sources),
         out_specs=[pl.BlockSpec(memory_space=pltpu.VMEM)] * 2,
-        scratch_shapes=[pltpu.VMEM((devices, rows_out, LANES), jnp.float32)]
-        + [
-            pltpu.VMEM((tiles_of(wide), rows, LANES), jnp.float32)
-            for (rows, wide), tiled in zip(shapes, tiled_in)
-            if not tiled
-        ],
+        scratch_shapes=[pltpu.VMEM((4, rows_out, LANES), jnp.float32)]
+        + [pltpu.VMEM((rows * wide // LANES, LANES), jnp.float32) for rows, wide in shapes]
+        + [pltpu.VMEM(shape, jnp.float32) for shape in tiled_shapes(untiled)],
         compiler_params=pltpu.CompilerParams(vmem_limit_bytes=VMEM_LIMIT),
+        cost_estimate=LIGHT,
         name="pack",
     )(place, *sources)
 
@@ -317,9 +309,7 @@
         in_specs=[pl.BlockSpec(memory_space=pltpu.VMEM)],
         out_specs=[pl.BlockSpec(memory_space=pltpu.VMEM)] * 2,
         compiler_params=pltpu.CompilerParams(vmem_limit_bytes=VMEM_LIMIT),
-        cost_estimate=pl.CostEstimate(
-            flops=12 * 10**9, bytes_accessed=4 * 10**6, transcendentals=2 * 10**6
-        ),
+        cost_estimate=LIGHT,
         name="attend",
     )(fields)
 
@@ -404,9 +394,7 @@
             pltpu.VMEM((length, HEAD_DIM), jnp.float32),
         ],
         compiler_params=pltpu.CompilerParams(vmem_limit_bytes=VMEM_LIMIT),
-        cost_estimate=pl.CostEstimate(
-            flops=24 * 10**9, bytes_accessed=8 * 10**6, transcendentals=2 * 10**6
-        ),
+        cost_estimate=LIGHT,
         name="attend_back",
     )(fields, back, mixed, total)
 
@@ -443,7 +431,7 @@
             fields_ref[:, at * LANES : (at + 1) * LANES] = tile
 
 
-def vmem_call(kernel, out_shape, scratch_shapes, name, flops, *args):
+def vmem_call(kernel, out_shape, scratch_shapes, name, *args):
     single = not isinstance(out_shape, list)
     return pl.pallas_call(
         kernel,
@@ -454,7 +442,7 @@
         else [pl.BlockSpec(memory_space=pltpu.VMEM)] * len(out_shape),
         scratch_shapes=scratch_shapes,
         compiler_params=pltpu.CompilerParams(vmem_limit_bytes=VMEM_LIMIT),
-        cost_estimate=pl.CostEstimate(flops=flops, bytes_accessed=10**7, transcendentals=0),
+        cost_estimate=LIGHT,
         name=name,
     )(*args)
 
@@ -465,7 +453,6 @@
         jax.ShapeDtypeStruct((tokens.shape[0], wide.shape[1]), jnp.bfloat16),
         [pltpu.VMEM(tokens.shape, jnp.bfloat16)],
         "project",
-        8 * 10**9,
         tokens, gains, wide, cosine, sine,
     )
 
@@ -526,7 +513,6 @@
             pltpu.VMEM((width, rows), jnp.bfloat16),
         ],
         "finish",
-        12 * 10**9,
         tokens, gains, wide, cosine, sine, mid_back, *[part for back in backs for part in back],
     )
 
@@ -614,8 +600,7 @@
         if not self.stages:
             return other
         self.arrived, other = tied(self.arrived, other)
-        self.held = jnp.concatenate(self.arrived)
-        self.got = swap(self.held, CORE_MASK, self.devices)
+        self.got = [swap(field, CORE_MASK, self.devices) for field in self.arrived]
         return other
 
     def result(self, joined):
@@ -628,7 +613,7 @@
                 return mats
             pads = [((0, 0), (0, tiles_of(mat.shape[1]) * LANES - mat.shape[1])) for mat in mats]
             return [jnp.concatenate([jnp.pad(mat, pad) for mat, pad in zip(mats, pads)], 1)]
-        pieces = (self.held, self.got)
+        pieces = self.arrived + self.got
         return unpack_pieces(place_of(), pieces, self.shapes, self.devices, joined)
 
 
@@ -714,7 +699,10 @@
         (shards[6].shape[0] * devices // model_width, model_width)
     ]
     first = WeightGather(shards[:3], shapes[:3], devices)
-    second = WeightGather(shards[3:], shapes[3:], devices)
+    rest = (4, 5, 6, 3)
+    second = WeightGather(
+        [shards[at] for at in rest], [shapes[at] for at in rest], devices
+    )
     tokens = first.line_stage(tokens)
     tokens = first.plane_stage(tokens)
     tokens = second.line_stage(tokens)
@@ -730,7 +718,7 @@
     attended = [attend(fields, head, group_size) for head in range(2)]
     fields, attended = second.core_stage((fields, attended))
     attended.append(attend(fields, 2, group_size))
-    wo_mat, wg_mat, wu_mat, wd_mat = second.result(False)
+    wg_mat, wu_mat, wd_mat, wo_mat = second.result(False)
     mixed = jnp.concatenate([part for part, _ in attended], 1)
     attn_out = jnp.dot(mixed, wo_mat, preferred_element_type=jnp.float32)
     middle = resid_in + attn_out

time: 293 us -> 275 us (0.939)
  waiting for transfers between devices: 58.7 us -> 45.5 us
  Pallas kernels: 106 us -> 98.7 us
  local copies, waits for them, and re-layouts: 26.2 us -> 30.1 us
    ppermute x28 -> x34, waiting for transfers between devices: 58.7 us -> 45.5 us  [swap(): lax.ppermute(field, 'dp', [(place, place ^ mask) for place in range(devic...]
    optimization_barrier x2 -> x6, local copies, waits for them, and re-layouts: 1.79 us -> 8.23 us  [tied(): return lax.optimization_barrier((first, second))]
    pallas_call x2, Pallas kernels: 17.7 us -> 13.6 us  [pack_grads(): pl.pallas_call(functools.partial(pack_kernel, devices=devices, shapes=sha...]
    convert_element_type x2, other arithmetic: 0.93 us -> 4.62 us  [plane_stage(): (widen(self.kept[cut]) + widen(self.got[cut])).astype(jnp.bfloat16)]
    pallas_call x2, Pallas kernels: 15.4 us -> 11.8 us  [unpack_pieces(): pl.pallas_call(functools.partial(unpack_kernel, devices=devices, shapes=s...]
    concatenate x4 -> x0, local copies, waits for them, and re-layouts: 3.1 us -> none  [core_stage(): self.held = jnp.concatenate(self.arrived)]
    ppermute x28 -> x34, starting transfers between devices: 36.6 us -> 34.2 us  [swap(): lax.ppermute(field, 'dp', [(place, place ^ mask) for place in range(devic...]
    ppermute x2 -> x4, local copies, waits for them, and re-layouts: 5.22 us -> 7.29 us  [swap(): lax.ppermute(field, 'dp', [(place, place ^ mask) for place in range(devic...]
  transfers between devices with their start and end apart: 28 -> 34, of which waited for: 14 -> 12; matrix products, arithmetic and copies ran while one was open for 8% -> 12% of each run, Pallas kernels for 16% -> 25%
where the time goes in v4:
time: 275 us; the launch traced here: 272 us
  Pallas kernels  98.7 us (36%)
  matrix products  49 us (18%)
  waiting for transfers between devices  45.5 us (17%)
  starting transfers between devices  34.2 us (12%)
  local copies, waits for them, and re-layouts  30.1 us (11%)
  other arithmetic  12.8 us (5%)
    ppermute x34, waiting for transfers between devices, swap(): lax.ppermute(field, 'dp', [(place, place ^ mask) for place in range(devic...  45.5 us
    ppermute x34, starting transfers between devices, swap(): lax.ppermute(field, 'dp', [(place, place ^ mask) for place in range(devic...  34.2 us
    pallas_call x3, Pallas kernels, attend_back(): pl.pallas_call(functools.partial(attend_back_kernel, head=head, group=gro...  32.2 us
    pallas_call x3, Pallas kernels, attend(): pl.pallas_call(functools.partial(attend_kernel, head=head, group=group),...  22.1 us
    pallas_call x2, Pallas kernels, vmem_call(): pl.pallas_call(kernel, out_shape=out_shape, in_specs=[pl.BlockSpec(memory...  19 us
    dot_general x4, matrix products, times_transposed(): lax.dot_general(left, matrix, (((1,), (1,)), ((), ())), preferred_element...  17.5 us
    dot_general x4, matrix products, outer_prod(): lax.dot_general(left, right, (((0,), (0,)), ((), ())), preferred_element_...  14.7 us
    pallas_call x2, Pallas kernels, pack_grads(): pl.pallas_call(functools.partial(pack_kernel, devices=devices, shapes=sha...  13.6 us
  transfers between devices with their start and end apart: 34, of which 12 were waited for; matrix products, arithmetic and copies ran while one was open for 12% of the time, Pallas kernels for 25%

profile of v4, /device:TPU:0, one launch (start us, length us, event | category | flops | bytes accessed | tf_op | source)
XLA Modules:
  0.0 271.6 jit_solution(7630234578876293208)
XLA Ops:
  1.5 3.1 %collective-permute-start = (bf16[135,128]{1,0:T(8,128)(2,1)S(1)}, bf16[135,128]{1,0:T(8,128)(2,1)S(1)}, u32[]{:S(2)}, u32[]{:S(2)}) collective-permute-start(bf16[135,128]{1,0:T(8,128)(2,1)S(1)} %pad_maximum_fusion.9), channel_id=1, source_target_pairs={{0,8},{1,9},{2,10},{3,11},{4,12},{5,13},{6,14},{7,15},{8,0},{9,1},... | collective-permute-start | bytes 103688 | tf_op jit(solution)/shard_map/ppermute | solution.py:32
  4.6 2.6 collective-permute-start.1
  7.2 2.9 %collective-permute-done.1 = bf16[135,128]{1,0:T(8,128)(2,1)S(1)} collective-permute-done((bf16[135,128]{1,0:T(8,128)(2,1)S(1)}, bf16[135,128]{1,0:T(8,128)(2,1)S(1)}, u32[]{:S(2)}, u32[]{:S(2)}) %collective-permute-start.1) | collective-permute-done | bytes 34592 | tf_op jit(solution)/shard_map/ppermute | solution.py:32
  10.1 2.9 %collective-permute-done.2 = bf16[135,128]{1,0:T(8,128)(2,1)S(1)} collective-permute-done((bf16[135,128]{1,0:T(8,128)(2,1)S(1)}, bf16[135,128]{1,0:T(8,128)(2,1)S(1)}, u32[]{:S(2)}, u32[]{:S(2)}) %collective-permute-start.2) | collective-permute-done | bytes 34592 | tf_op jit(solution)/shard_map/ppermute | solution.py:32
  13.0 1.6 collective-permute-start.3
  15.5 1.6 collective-permute-start.4
  19.0 2.9 %collective-permute-start.8 = (bf16[729,128]{1,0:T(8,128)(2,1)S(1)}, bf16[729,128]{1,0:T(8,128)(2,1)S(1)}, u32[]{:S(2)}, u32[]{:S(2)}) collective-permute-start(bf16[729,128]{1,0:T(8,128)(2,1)S(1)} %pad_maximum_fusion.7), channel_id=1, source_target_pairs={{0,24},{1,25},{2,26},{3,27},{4,28},{5,29},{6,30},{7,31},{8,16},{9,... | collective-permute-start | bytes 559880 | tf_op jit(solution)/shard_map/ppermute | solution.py:32
  24.4 8.2 %collective-permute-done.7 = bf16[729,128]{1,0:T(8,128)(2,1)S(1)} collective-permute-done((bf16[729,128]{1,0:T(8,128)(2,1)S(1)}, bf16[729,128]{1,0:T(8,128)(2,1)S(1)}, u32[]{:S(2)}, u32[]{:S(2)}) %collective-permute-start.7) | collective-permute-done | bytes 186656 | tf_op jit(solution)/shard_map/ppermute | solution.py:32
  35.3 1.4 copy.50.tokens_ref
  37.6 3.9 %unpack.2.wide_ref = bf16[576,1152]{1,0:T(8,128)(2,1)} custom-call(s32[1]{0:T(128)} %bitcast.15.place_ref, bf16[4,135,128]{2,1,0:T(8,128)(2,1)} %copy-done.8, bf16[4,135,128]{2,1,0:T(8,128)(2,1)} %copy-done.15, bf16[4,135,128]{2,1,0:T(8,128)(2,1)} %copy-done.16, bf16[4,135,128]{2,1,0:T(8,128)(2,1)} %copy-done.17, ...), custom_call_target="tpu_custom_call" | custom-call | flops 100000000 | bytes 1000000 | tf_op jit(solution)/shard_map/unpack/pallas_call | solution.py:132
  41.5 6.2 %project.1.fields_ref = bf16[1024,1152]{1,0:T(8,128)(2,1)} custom-call(bf16[1024,576]{1,0:T(8,128)(2,1)} %copy.50.tokens_ref, f32[2,576]{1,0:T(2,128)} %convert_element_type.303.gains_ref, bf16[576,1152]{1,0:T(8,128)(2,1)} %unpack.2.wide_ref, f32[1024,128]{1,0:T(8,128)} %copy.52.cosine_ref, f32[1024,128]{1,0:T(8,128)} %copy.53.sine_ref), custom_call_target="tpu_custom_call" | custom-call | flops 100000000 | bytes 1000000 | tf_op jit(solution)/shard_map/project/pallas_call | solution.py:436
  48.1 1.6 collective-permute-start.13
  49.7 1.5 collective-permute-start.14
  51.7 7.2 %attend.3 = (bf16[1024,192]{1,0:T(8,128)(2,1)}, f32[1024,128]{1,0:T(8,128)}) custom-call(bf16[1024,1152]{1,0:T(8,128)(2,1)} %project.1.fields_ref), custom_call_target="tpu_custom_call" | custom-call | flops 100000000 | bytes 1000000 | tf_op jit(solution)/shard_map/attend/pallas_call | solution.py:303
  58.8 7.8 %attend.4 = (bf16[1024,192]{1,0:T(8,128)(2,1)}, f32[1024,128]{1,0:T(8,128)}) custom-call(bf16[1024,1152]{1,0:T(8,128)(2,1)} %project.1.fields_ref), custom_call_target="tpu_custom_call" | custom-call | flops 100000000 | bytes 1000000 | tf_op jit(solution)/shard_map/attend/pallas_call | solution.py:303
  66.6 1.2 collective-permute-done.13
  67.8 16.8 %collective-permute-done.14 = bf16[4,729,128]{2,0,1:T(4,128)(2,1)} collective-permute-done((bf16[4,729,128]{2,0,1:T(4,128)(2,1)S(1)}, bf16[4,729,128]{2,0,1:T(4,128)(2,1)}, u32[]{:S(2)}, u32[]{:S(2)}) %collective-permute-start.14) | collective-permute-done | bytes 746528 | tf_op jit(solution)/shard_map/ppermute | solution.py:32
  84.6 1.3 copy.57
  86.9 1.7 copy.69
  88.6 2.1 copy.58.refs_1_
  90.7 2.1 copy.59.refs_2_
  93.8 7.2 %attend.5 = (bf16[1024,192]{1,0:T(8,128)(2,1)}, f32[1024,128]{1,0:T(8,128)}) custom-call(bf16[1024,1152]{1,0:T(8,128)(2,1)} %project.1.fields_ref), custom_call_target="tpu_custom_call" | custom-call | flops 100000000 | bytes 1000000 | tf_op jit(solution)/shard_map/attend/pallas_call | solution.py:303
  100.9 2.1 copy.61.refs_4_
  103.0 2.1 copy.62.refs_5_
  105.1 2.1 copy.63.refs_6_
  108.2 7.9 %unpack.3 = (bf16[576,1536]{1,0:T(8,128)(2,1)}, bf16[576,1536]{1,0:T(8,128)(2,1)}, bf16[1536,576]{1,0:T(8,128)(2,1)}, bf16[576,576]{1,0:T(8,128)(2,1)}) custom-call(s32[1]{0:T(128)} %bitcast.15.place_ref, bf16[4,729,128]{2,1,0:T(8,128)(2,1)} %copy-done, bf16[4,729,128]{2,1,0:T(8,128)(2,1)} %copy.58.refs_1_, bf16[4,729,128]{2,1,0:T(8,128)(2,1)} %copy.59.refs_2_, ...), custom_call_target="tpu_custom_call" | custom-call | flops 100000000 | bytes 1000000 | tf_op jit(solution)/shard_map/unpack/pallas_call | solution.py:132
  116.2 2.5 multiply_reduce_fusion.2
  119.0 1.1 copy-done.23
  120.2 4.5 %fusion.24 = f32[1024,1536]{1,0:T(8,128)} fusion(bf16[1024,576]{1,0:T(8,128)(2,1)S(1)} %multiply_convert_fusion.1, bf16[576,1536]{1,0:T(8,128)(2,1)S(1)} %copy-done.23), kind=kOutput, calls=%fused_computation.75 | convolution fusion | flops 1811939328 | bytes 9240576 | tf_op jit(solution)/shard_map/dot_general | solution.py:728
  124.7 4.7 %fusion.23 = f32[1024,1536]{1,0:T(8,128)} fusion(bf16[1024,576]{1,0:T(8,128)(2,1)S(1)} %multiply_convert_fusion.1, bf16[576,1536]{1,0:T(8,128)(2,1)S(1)} %copy-done.22), kind=kOutput, calls=%fused_computation.74 | convolution fusion | flops 1811939328 | bytes 9240576 | tf_op jit(solution)/shard_map/dot_general | solution.py:727
  129.4 9.3 %fusion.3 = (bf16[1024,1536]{1,0:T(8,128)(2,1)S(1)}, bf16[1024,1536]{1,0:T(8,128)(2,1)S(1)}, bf16[1024,1536]{1,0:T(8,128)(2,1)}) fusion(f32[1024,1536]{1,0:T(8,128)} %fusion.23, f32[1024,1536]{1,0:T(8,128)} %fusion.24, bf16[1536,576]{1,0:T(8,128)(2,1)S(1)} %copy-done.21, bf16[1024,576]{0,1:T(8,128)(2,1)S(1)} %copy-done.6), kind=kOutput, calls=%fused_computation.5 | convolution fusion | flops 1835532288 | bytes 24969216 | tf_op jit(solution)/shard_map/dot_general | solution.py:560
  138.8 2.6 fusion.28
  141.4 3.9 %fusion.26.refs_1_ = f32[576,1536]{1,0:T(8,128)} fusion(bf16[1024,576]{1,0:T(8,128)(2,1)S(1)} %multiply_convert_fusion.1, bf16[1024,1536]{1,0:T(8,128)(2,1)S(1)} %get-tuple-element.188), kind=kOutput, calls=%fused_computation.77 | convolution fusion | flops 1811939328 | bytes 7864320 | tf_op jit(solution)/shard_map/dot_general | solution.py:554
  145.3 3.8 %fusion.25.refs_0_ = f32[576,1536]{1,0:T(8,128)} fusion(bf16[1024,576]{1,0:T(8,128)(2,1)S(1)} %multiply_convert_fusion.1, bf16[1024,1536]{1,0:T(8,128)(2,1)S(1)} %get-tuple-element.189), kind=kOutput, calls=%fused_computation.76 | convolution fusion | flops 1811939328 | bytes 7864320 | tf_op jit(solution)/shard_map/dot_general | solution.py:554
  149.1 3.0 %multiply_reduce_fusion = (f32[576]{0:T(1024)S(1)}, f32[1024]{0:T(1024)S(1)}, f32[1024,576]{1,0:T(8,128)S(1)}) fusion(f32[1024,576]{1,0:T(8,128)S(1)} %get-tuple-element.222, f32[1024]{0:T(1024)S(1)} %get-tuple-element.217, f32[576]{0:T(1024)S(1)} %slice_reduce_fusion, f32[1024,576]{1,0:T(8,128)S(1)} %fusion.28, ...), kind=kOutput, calls=%fused_computation.9 | convolution fusion | flops 1816066560 | bytes 12005888 | tf_op jit(solution)/shard_map/dot_general | solution.py:560
  153.3 2.5 convolution_convert_fusion.back_ref
  156.6 4.6 %fusion.27.refs_2_ = f32[1536,576]{1,0:T(8,128)} fusion(bf16[1024,1536]{1,0:T(8,128)(2,1)S(1)} %copy-done.25, bf16[1024,576]{0,1:T(8,128)(2,1)S(1)} %copy-done.6), kind=kOutput, calls=%fused_computation.78 | convolution fusion | flops 1811939328 | bytes 7864320 | tf_op jit(solution)/shard_map/dot_general | solution.py:554
  161.2 8.6 %pack.2 = (bf16[16,648,128]{2,1,0:T(8,128)(2,1)}, bf16[16,648,128]{2,1,0:T(8,128)(2,1)}) custom-call(s32[1]{0:T(128)} %bitcast.15.place_ref, f32[576,1536]{1,0:T(8,128)} %fusion.25.refs_0_, f32[576,1536]{1,0:T(8,128)} %fusion.26.refs_1_, f32[1536,576]{1,0:T(8,128)} %fusion.27.refs_2_), custom_call_target="tpu_custom_call" | custom-call | flops 100000000 | bytes 1000000 | tf_op jit(solution)/shard_map/pack/pallas_call | solution.py:223
  169.8 10.6 %attend_back.3 = (f32[1024,192]{1,0:T(8,128)}, f32[1024,128]{1,0:T(8,128)}) custom-call(bf16[1024,1152]{1,0:T(8,128)(2,1)} %project.1.fields_ref, bf16[1024,576]{1,0:T(8,128)(2,1)} %convolution_convert_fusion.back_ref, bf16[1024,192]{1,0:T(8,128)(2,1)} %get-tuple-element.100.mixed_ref, f32[1024,128]{1,0:T(8,128)} %get-tuple-element.117.total_ref), custom_call_target="tpu_custom_call" | custom-call | flops 100000000 | bytes 1000000 | tf_op jit(solution)/shard_map/attend_back/pallas_call | solution.py:379
  180.5 4.4 %add_convert_fusion.1 = (bf16[4,648,128]{2,1,0:T(8,128)(2,1)}, bf16[4,648,128]{2,1,0:T(8,128)(2,1)}, bf16[4,648,128]{2,1,0:T(8,128)(2,1)}, bf16[4,648,128]{2,1,0:T(8,128)(2,1)S(1)}) fusion(bf16[16,648,128]{2,1,0:T(8,128)(2,1)} %collective-permute-done.20, bf16[16,648,128]{2,1,0:T(8,128)(2,1)} %get-tuple-element.114), kind=kLoop, calls=%fused_computation.18 | loop fusion | flops 5308416 | bytes 7962624 | tf_op jit(solution)/shard_map/convert_element_type | solution.py:644
  184.9 1.1 collective-permute-start.21
  186.9 1.5 collective-permute-start.23
  188.4 2.4 fusion.5.refs_3_
  190.8 10.8 %attend_back.5 = (f32[1024,192]{1,0:T(8,128)}, f32[1024,128]{1,0:T(8,128)}) custom-call(bf16[1024,1152]{1,0:T(8,128)(2,1)} %project.1.fields_ref, bf16[1024,576]{1,0:T(8,128)(2,1)} %convolution_convert_fusion.back_ref, bf16[1024,192]{1,0:T(8,128)(2,1)} %get-tuple-element.103.mixed_ref, f32[1024,128]{1,0:T(8,128)} %get-tuple-element.129.total_ref), custom_call_target="tpu_custom_call" | custom-call | flops 100000000 | bytes 1000000 | tf_op jit(solution)/shard_map/attend_back/pallas_call | solution.py:379
  201.6 10.7 %attend_back.4 = (f32[1024,192]{1,0:T(8,128)}, f32[1024,128]{1,0:T(8,128)}) custom-call(bf16[1024,1152]{1,0:T(8,128)(2,1)} %project.1.fields_ref, bf16[1024,576]{1,0:T(8,128)(2,1)} %convolution_convert_fusion.back_ref, bf16[1024,192]{1,0:T(8,128)(2,1)} %get-tuple-element.101.mixed_ref, f32[1024,128]{1,0:T(8,128)} %get-tuple-element.126.total_ref), custom_call_target="tpu_custom_call" | custom-call | flops 100000000 | bytes 1000000 | tf_op jit(solution)/shard_map/attend_back/pallas_call | solution.py:379
  212.4 12.8 %finish.1 = (bf16[1024,576]{1,0:T(8,128)(2,1)}, f32[9,576,128]{2,1,0:T(8,128)}, f32[1,576]{1,0:T(1,128)}) custom-call(bf16[1024,576]{1,0:T(8,128)(2,1)} %copy.50.tokens_ref, f32[2,576]{1,0:T(2,128)} %convert_element_type.303.gains_ref, bf16[576,1152]{1,0:T(8,128)(2,1)} %unpack.2.wide_ref, f32[1024,128]{1,0:T(8,128)} %copy.52.cosine_ref, ...), custom_call_target="tpu_custom_call" | custom-call | flops 100000000 | bytes 1000000 | tf_op jit(solution)/shard_map/finish/pallas_call | solution.py:436
  225.2 1.4 pad_maximum_fusion.10.refs_4_
  226.6 2.2 fusion.12
  228.8 1.2 slice.206.refs_0_
  231.2 5.0 %pack.3 = (bf16[16,232,128]{2,1,0:T(8,128)(2,1)}, bf16[16,232,128]{2,1,0:T(8,128)(2,1)}) custom-call(s32[1]{0:T(128)} %bitcast.15.place_ref, f32[5,576,128]{2,1,0:T(8,128)} %slice.206.refs_0_, f32[2,576,128]{2,1,0:T(8,128)} %get-tuple-element.196.refs_1_, f32[2,576,128]{2,1,0:T(8,128)} %get-tuple-element.195.refs_2_, f32[576,576]{1,0:T(8,128)} %fusion.5.refs_3_, ...), custom_call_target="tpu_custom_call" | custom-call | flops 100000000 | bytes 1000000 | tf_op jit(solution)/shard_map/pack/pallas_call | solution.py:223
  236.1 5.1 %add_convert_fusion = bf16[1024,576]{1,0:T(8,128)(2,1)S(1)} fusion(f32[1024,576]{1,0:T(8,128)S(1)} %get-tuple-element.222, bf16[1024,1536]{1,0:T(8,128)(2,1)} %get-tuple-element.190, bf16[1536,576]{1,0:T(8,128)(2,1)} %get-tuple-element.111), kind=kOutput, calls=%fused_computation.12 | convolution fusion | flops 1813118976 | bytes 8454144 | tf_op jit(solution)/shard_map/dot_general | solution.py:732
  241.2 1.4 copy.76
  242.7 2.0 collective-permute-start.32
  244.7 2.4 collective-permute-start.33
  247.3 1.2 collective-permute-start.25
  249.4 2.5 collective-permute-done.31
  252.0 1.5 collective-permute-start.27
  253.5 4.5 %collective-permute-done.32 = bf16[648,128]{1,0:T(8,128)(2,1)S(1)} collective-permute-done((bf16[648,128]{1,0:T(8,128)(2,1)}, bf16[648,128]{1,0:T(8,128)(2,1)S(1)}, u32[]{:S(2)}, u32[]{:S(2)}) %collective-permute-start.32) | collective-permute-done | bytes 165920 | tf_op jit(solution)/shard_map/ppermute | solution.py:32
  258.1 2.7 collective-permute-done.27
  260.9 1.1 collective-permute-start.28
  262.0 1.3 collective-permute-start.29
  263.3 2.1 collective-permute-start.30
  266.1 1.4 copy.77
  267.5 1.9 collective-permute-done.29
  (125 shorter events, 22.1 us)
Async XLA Ops:
  0.6 34.7 %copy-start.5 = (bf16[1024,576]{0,1:T(8,128)(2,1)S(1)}, bf16[1024,576]{0,1:T(8,128)(2,1)}, u32[]{:S(2)}) copy-start(bf16[1024,576]{0,1:T(8,128)(2,1)} %param.10) | copy-start | bytes 3538948
  0.7 34.1 %copy-start.20 = (bf16[2,576]{1,0:T(2,128)(2,1)S(1)}, bf16[2,576]{1,0:T(2,128)(2,1)}, u32[]{:S(2)}) copy-start(bf16[2,576]{1,0:T(2,128)(2,1)} %param.19) | copy-start | bytes 6916
  1.5 5.7 %collective-permute-start = (bf16[135,128]{1,0:T(8,128)(2,1)S(1)}, bf16[135,128]{1,0:T(8,128)(2,1)S(1)}, u32[]{:S(2)}, u32[]{:S(2)}) collective-permute-start(bf16[135,128]{1,0:T(8,128)(2,1)S(1)} %pad_maximum_fusion.9), channel_id=1, source_target_pairs={{0,8},{1,9},{2,10},{3,11},{4,12},{5,13},{6,14},{7,15},{8,0},{9,1},... | collective-permute-start | bytes 103688 | tf_op jit(solution)/shard_map/ppermute | solution.py:32
  4.6 5.5 %collective-permute-start.1 = (bf16[135,128]{1,0:T(8,128)(2,1)S(1)}, bf16[135,128]{1,0:T(8,128)(2,1)S(1)}, u32[]{:S(2)}, u32[]{:S(2)}) collective-permute-start(bf16[135,128]{1,0:T(8,128)(2,1)S(1)} %pad_maximum_fusion.9), channel_id=1, source_target_pairs={{0,16},{1,17},{2,18},{3,19},{4,20},{5,21},{6,22},{7,23},{8,24},{9,... | collective-permute-start | bytes 103688 | tf_op jit(solution)/shard_map/ppermute | solution.py:32
  7.2 5.7 %collective-permute-start.2 = (bf16[135,128]{1,0:T(8,128)(2,1)S(1)}, bf16[135,128]{1,0:T(8,128)(2,1)S(1)}, u32[]{:S(2)}, u32[]{:S(2)}) collective-permute-start(bf16[135,128]{1,0:T(8,128)(2,1)S(1)} %pad_maximum_fusion.9), channel_id=1, source_target_pairs={{0,24},{1,25},{2,26},{3,27},{4,28},{5,29},{6,30},{7,31},{8,16},{9,... | collective-permute-start | bytes 103688 | tf_op jit(solution)/shard_map/ppermute | solution.py:32
  13.0 23.8 %copy-start.8 = (bf16[4,135,128]{2,1,0:T(8,128)(2,1)}, bf16[4,135,128]{2,1,0:T(8,128)(2,1)S(1)}, u32[]{:S(2)}) copy-start(bf16[4,135,128]{2,1,0:T(8,128)(2,1)S(1)} %pad_maximum_fusion.8.refs_0_) | copy-start | bytes 414724
  13.0 6.0 %collective-permute-start.3 = (bf16[4,135,128]{2,1,0:T(8,128)(2,1)S(1)}, bf16[4,135,128]{2,1,0:T(8,128)(2,1)S(1)}, u32[]{:S(2)}, u32[]{:S(2)}) collective-permute-start(bf16[4,135,128]{2,1,0:T(8,128)(2,1)S(1)} %pad_maximum_fusion.8.refs_0_), channel_id=1, source_target_pairs={{0,2},{1,3},{2,0},{3,1},{4,6},{5,7},{6,4},{7,5},{8,10},{9,11},{10,... | collective-permute-start | bytes 414728 | tf_op jit(solution)/shard_map/ppermute | solution.py:32
  15.5 7.0 %collective-permute-start.4 = (bf16[4,135,128]{2,1,0:T(8,128)(2,1)S(1)}, bf16[4,135,128]{2,1,0:T(8,128)(2,1)S(1)}, u32[]{:S(2)}, u32[]{:S(2)}) collective-permute-start(bf16[4,135,128]{2,1,0:T(8,128)(2,1)S(1)} %pad_maximum_fusion.8.refs_0_), channel_id=1, source_target_pairs={{0,4},{1,5},{2,6},{3,7},{4,0},{5,1},{6,2},{7,3},{8,12},{9,13},{10,... | collective-permute-start | bytes 414728 | tf_op jit(solution)/shard_map/ppermute | solution.py:32
  17.1 6.1 %collective-permute-start.5 = (bf16[4,135,128]{2,1,0:T(8,128)(2,1)S(1)}, bf16[4,135,128]{2,1,0:T(8,128)(2,1)S(1)}, u32[]{:S(2)}, u32[]{:S(2)}) collective-permute-start(bf16[4,135,128]{2,1,0:T(8,128)(2,1)S(1)} %pad_maximum_fusion.8.refs_0_), channel_id=1, source_target_pairs={{0,6},{1,7},{2,4},{3,5},{4,2},{5,3},{6,0},{7,1},{8,14},{9,15},{10,... | collective-permute-start | bytes 414728 | tf_op jit(solution)/shard_map/ppermute | solution.py:32
  17.5 6.9 %collective-permute-start.6 = (bf16[729,128]{1,0:T(8,128)(2,1)S(1)}, bf16[729,128]{1,0:T(8,128)(2,1)S(1)}, u32[]{:S(2)}, u32[]{:S(2)}) collective-permute-start(bf16[729,128]{1,0:T(8,128)(2,1)S(1)} %pad_maximum_fusion.7), channel_id=1, source_target_pairs={{0,8},{1,9},{2,10},{3,11},{4,12},{5,13},{6,14},{7,15},{8,0},{9,1},... | collective-permute-start | bytes 559880 | tf_op jit(solution)/shard_map/ppermute | solution.py:32
  17.5 15.1 %collective-permute-start.7 = (bf16[729,128]{1,0:T(8,128)(2,1)S(1)}, bf16[729,128]{1,0:T(8,128)(2,1)S(1)}, u32[]{:S(2)}, u32[]{:S(2)}) collective-permute-start(bf16[729,128]{1,0:T(8,128)(2,1)S(1)} %pad_maximum_fusion.7), channel_id=1, source_target_pairs={{0,16},{1,17},{2,18},{3,19},{4,20},{5,21},{6,22},{7,23},{8,24},{9,... | collective-permute-start | bytes 559880 | tf_op jit(solution)/shard_map/ppermute | solution.py:32
  19.0 17.8 %copy-start.15 = (bf16[4,135,128]{2,1,0:T(8,128)(2,1)}, bf16[4,135,128]{2,1,0:T(8,128)(2,1)S(1)}, u32[]{:S(2)}) copy-start(bf16[4,135,128]{2,1,0:T(8,128)(2,1)S(1)} %collective-permute-done.3.refs_1_) | copy-start | bytes 414724
  19.0 17.8 %collective-permute-start.8 = (bf16[729,128]{1,0:T(8,128)(2,1)S(1)}, bf16[729,128]{1,0:T(8,128)(2,1)S(1)}, u32[]{:S(2)}, u32[]{:S(2)}) collective-permute-start(bf16[729,128]{1,0:T(8,128)(2,1)S(1)} %pad_maximum_fusion.7), channel_id=1, source_target_pairs={{0,24},{1,25},{2,26},{3,27},{4,28},{5,29},{6,30},{7,31},{8,16},{9,... | collective-permute-start | bytes 559880 | tf_op jit(solution)/shard_map/ppermute | solution.py:32
  22.5 14.3 %copy-start.16 = (bf16[4,135,128]{2,1,0:T(8,128)(2,1)}, bf16[4,135,128]{2,1,0:T(8,128)(2,1)S(1)}, u32[]{:S(2)}) copy-start(bf16[4,135,128]{2,1,0:T(8,128)(2,1)S(1)} %collective-permute-done.4.refs_2_) | copy-start | bytes 414724
  23.1 13.7 %copy-start.17 = (bf16[4,135,128]{2,1,0:T(8,128)(2,1)}, bf16[4,135,128]{2,1,0:T(8,128)(2,1)S(1)}, u32[]{:S(2)}) copy-start(bf16[4,135,128]{2,1,0:T(8,128)(2,1)S(1)} %collective-permute-done.5.refs_3_) | copy-start | bytes 414724
  23.1 13.8 %collective-permute-start.10 = (bf16[4,135,128]{2,1,0:T(8,128)(2,1)S(1)}, bf16[4,135,128]{2,1,0:T(8,128)(2,1)S(1)}, u32[]{:S(2)}, u32[]{:S(2)}) collective-permute-start(bf16[4,135,128]{2,1,0:T(8,128)(2,1)S(1)} %collective-permute-done.3.refs_1_), channel_id=1, source_target_pairs={{0,1},{1,0},{2,3},{3,2},{4,5},{5,4},{6,7},{7,6},{8,9},{9,8},{10,11... | collective-permute-start | bytes 414728 | tf_op jit(solution)/shard_map/ppermute | solution.py:32
  23.1 13.8 %collective-permute-start.11 = (bf16[4,135,128]{2,1,0:T(8,128)(2,1)S(1)}, bf16[4,135,128]{2,1,0:T(8,128)(2,1)}, u32[]{:S(2)}, u32[]{:S(2)}) collective-permute-start(bf16[4,135,128]{2,1,0:T(8,128)(2,1)S(1)} %collective-permute-done.4.refs_2_), channel_id=1, source_target_pairs={{0,1},{1,0},{2,3},{3,2},{4,5},{5,4},{6,7},{7,6},{8,9},{9,8},{10,11... | collective-permute-start | bytes 414728 | tf_op jit(solution)/shard_map/ppermute | solution.py:32
  24.4 12.5 %collective-permute-start.12 = (bf16[4,135,128]{2,1,0:T(8,128)(2,1)S(1)}, bf16[4,135,128]{2,1,0:T(8,128)(2,1)}, u32[]{:S(2)}, u32[]{:S(2)}) collective-permute-start(bf16[4,135,128]{2,1,0:T(8,128)(2,1)S(1)} %collective-permute-done.5.refs_3_), channel_id=1, source_target_pairs={{0,1},{1,0},{2,3},{3,2},{4,5},{5,4},{6,7},{7,6},{8,9},{9,8},{10,11... | collective-permute-start | bytes 414728 | tf_op jit(solution)/shard_map/ppermute | solution.py:32
  32.6 4.4 %collective-permute-start.9 = (bf16[4,135,128]{2,1,0:T(8,128)(2,1)S(1)}, bf16[4,135,128]{2,1,0:T(8,128)(2,1)}, u32[]{:S(2)}, u32[]{:S(2)}) collective-permute-start(bf16[4,135,128]{2,1,0:T(8,128)(2,1)S(1)} %pad_maximum_fusion.8.refs_0_), channel_id=1, source_target_pairs={{0,1},{1,0},{2,3},{3,2},{4,5},{5,4},{6,7},{7,6},{8,9},{9,8},{10,11... | collective-permute-start | bytes 414728 | tf_op jit(solution)/shard_map/ppermute | solution.py:32
  36.9 47.7 %copy-start = (bf16[4,729,128]{2,1,0:T(8,128)(2,1)}, bf16[4,729,128]{2,1,0:T(8,128)(2,1)S(1)}, u32[]{:S(2)}) copy-start(bf16[4,729,128]{2,1,0:T(8,128)(2,1)S(1)} %pad_maximum_fusion.1.refs_0_) | copy-start | bytes 2239492
  36.9 0.7 copy-start.18
  48.1 19.7 %collective-permute-start.13 = (bf16[4,729,128]{2,0,1:T(4,128)(2,1)S(1)}, bf16[4,729,128]{2,0,1:T(4,128)(2,1)}, u32[]{:S(2)}, u32[]{:S(2)}) collective-permute-start(bf16[4,729,128]{2,0,1:T(4,128)(2,1)S(1)} %copy.54), channel_id=1, source_target_pairs={{0,2},{1,3},{2,0},{3,1},{4,6},{5,7},{6,4},{7,5},{8,10},{9,11},{10,... | collective-permute-start | bytes 2239496 | tf_op jit(solution)/shard_map/ppermute | solution.py:32
  49.7 34.9 %collective-permute-start.14 = (bf16[4,729,128]{2,0,1:T(4,128)(2,1)S(1)}, bf16[4,729,128]{2,0,1:T(4,128)(2,1)}, u32[]{:S(2)}, u32[]{:S(2)}) collective-permute-start(bf16[4,729,128]{2,0,1:T(4,128)(2,1)S(1)} %copy.54), channel_id=1, source_target_pairs={{0,4},{1,5},{2,6},{3,7},{4,0},{5,1},{6,2},{7,3},{8,12},{9,13},{10,... | collective-permute-start | bytes 2239496 | tf_op jit(solution)/shard_map/ppermute | solution.py:32
  51.2 33.4 %collective-permute-start.15 = (bf16[4,729,128]{2,0,1:T(4,128)(2,1)S(1)}, bf16[4,729,128]{2,0,1:T(4,128)(2,1)S(1)}, u32[]{:S(2)}, u32[]{:S(2)}) collective-permute-start(bf16[4,729,128]{2,0,1:T(4,128)(2,1)S(1)} %copy.54), channel_id=1, source_target_pairs={{0,6},{1,7},{2,4},{3,5},{4,2},{5,3},{6,0},{7,1},{8,14},{9,15},{10,... | collective-permute-start | bytes 2239496 | tf_op jit(solution)/shard_map/ppermute | solution.py:32
  58.8 29.7 %copy-start.19 = (f32[2,576]{1,0:T(2,128)S(1)}, f32[2,576]{1,0:T(2,128)}, u32[]{:S(2)}) copy-start(f32[2,576]{1,0:T(2,128)} %convert_element_type.303.gains_ref) | copy-start | bytes 13828
  85.9 15.1 %collective-permute-start.16 = (bf16[4,729,128]{2,0,1:T(4,128)(2,1)}, bf16[4,729,128]{2,0,1:T(4,128)(2,1)}, u32[]{:S(2)}, u32[]{:S(2)}) collective-permute-start(bf16[4,729,128]{2,0,1:T(4,128)(2,1)} %copy.57), channel_id=1, source_target_pairs={{0,1},{1,0},{2,3},{3,2},{4,5},{5,4},{6,7},{7,6},{8,9},{9,8},{10,11... | collective-permute-start | bytes 2239496 | tf_op jit(solution)/shard_map/ppermute | solution.py:32
  85.9 17.2 %collective-permute-start.17 = (bf16[4,729,128]{2,0,1:T(4,128)(2,1)}, bf16[4,729,128]{2,0,1:T(4,128)(2,1)}, u32[]{:S(2)}, u32[]{:S(2)}) collective-permute-start(bf16[4,729,128]{2,0,1:T(4,128)(2,1)} %collective-permute-done.13), channel_id=1, source_target_pairs={{0,1},{1,0},{2,3},{3,2},{4,5},{5,4},{6,7},{7,6},{8,9},{9,8},{10,11... | collective-permute-start | bytes 2239496 | tf_op jit(solution)/shard_map/ppermute | solution.py:32
  86.4 18.8 %collective-permute-start.18 = (bf16[4,729,128]{2,0,1:T(4,128)(2,1)}, bf16[4,729,128]{2,0,1:T(4,128)(2,1)}, u32[]{:S(2)}, u32[]{:S(2)}) collective-permute-start(bf16[4,729,128]{2,0,1:T(4,128)(2,1)} %collective-permute-done.14), channel_id=1, source_target_pairs={{0,1},{1,0},{2,3},{3,2},{4,5},{5,4},{6,7},{7,6},{8,9},{9,8},{10,11... | collective-permute-start | bytes 2239496 | tf_op jit(solution)/shard_map/ppermute | solution.py:32
  86.4 20.9 %collective-permute-start.19 = (bf16[4,729,128]{2,0,1:T(4,128)(2,1)S(1)}, bf16[4,729,128]{2,0,1:T(4,128)(2,1)S(1)}, u32[]{:S(2)}, u32[]{:S(2)}) collective-permute-start(bf16[4,729,128]{2,0,1:T(4,128)(2,1)S(1)} %collective-permute-done.15), channel_id=1, source_target_pairs={{0,1},{1,0},{2,3},{3,2},{4,5},{5,4},{6,7},{7,6},{8,9},{9,8},{10,11... | collective-permute-start | bytes 2239496 | tf_op jit(solution)/shard_map/ppermute | solution.py:32
  108.2 7.9 %copy-start.1 = (bf16[1024,576]{1,0:T(8,128)(2,1)S(1)}, bf16[1024,576]{1,0:T(8,128)(2,1)}, u32[]{:S(2)}) copy-start(bf16[1024,576]{1,0:T(8,128)(2,1)} %copy.50.tokens_ref) | copy-start | bytes 3538948
  108.2 7.9 %copy-start.9 = (bf16[1024,192]{1,0:T(8,128)(2,1)S(1)}, bf16[1024,192]{1,0:T(8,128)(2,1)}, u32[]{:S(2)}) copy-start(bf16[1024,192]{1,0:T(8,128)(2,1)} %get-tuple-element.101.mixed_ref) | copy-start | bytes 1179652
  108.2 7.9 %copy-start.11 = (bf16[1024,192]{1,0:T(8,128)(2,1)S(1)}, bf16[1024,192]{1,0:T(8,128)(2,1)}, u32[]{:S(2)}) copy-start(bf16[1024,192]{1,0:T(8,128)(2,1)} %get-tuple-element.100.mixed_ref) | copy-start | bytes 1179652
  108.2 7.9 %copy-start.13 = (bf16[1024,192]{1,0:T(8,128)(2,1)S(1)}, bf16[1024,192]{1,0:T(8,128)(2,1)}, u32[]{:S(2)}) copy-start(bf16[1024,192]{1,0:T(8,128)(2,1)} %get-tuple-element.103.mixed_ref) | copy-start | bytes 1179652
  118.7 1.5 copy-start.23
  120.2 4.5 %copy-start.22 = (bf16[576,1536]{1,0:T(8,128)(2,1)S(1)}, bf16[576,1536]{1,0:T(8,128)(2,1)}, u32[]{:S(2)}) copy-start(bf16[576,1536]{1,0:T(8,128)(2,1)} %get-tuple-element.109) | copy-start | bytes 5308420
  124.7 4.7 %copy-start.6 = (bf16[1024,576]{0,1:T(8,128)(2,1)S(1)}, bf16[1024,576]{0,1:T(8,128)(2,1)}, u32[]{:S(2)}) copy-start(bf16[1024,576]{0,1:T(8,128)(2,1)} %param.11) | copy-start | bytes 3538948
  124.7 4.7 %copy-start.21 = (bf16[1536,576]{1,0:T(8,128)(2,1)S(1)}, bf16[1536,576]{1,0:T(8,128)(2,1)}, u32[]{:S(2)}) copy-start(bf16[1536,576]{1,0:T(8,128)(2,1)} %get-tuple-element.111) | copy-start | bytes 5308420
  152.1 1.1 copy-start.24
  153.3 35.1 %copy-start.2 = (f32[1024,576]{1,0:T(8,128)}, f32[1024,576]{1,0:T(8,128)S(1)}, u32[]{:S(2)}) copy-start(f32[1024,576]{1,0:T(8,128)S(1)} %subtract_add_fusion.mid_back_ref) | copy-start | bytes 7077892
  153.3 3.3 %copy-start.25 = (bf16[1024,1536]{1,0:T(8,128)(2,1)S(1)}, bf16[1024,1536]{1,0:T(8,128)(2,1)}, u32[]{:S(2)}) copy-start(bf16[1024,1536]{1,0:T(8,128)(2,1)} %get-tuple-element.190) | copy-start | bytes 9437188
  169.8 10.7 %collective-permute-start.20 = (bf16[16,648,128]{2,1,0:T(8,128)(2,1)}, bf16[16,648,128]{2,1,0:T(8,128)(2,1)}, u32[]{:S(2)}, u32[]{:S(2)}) collective-permute-start(bf16[16,648,128]{2,1,0:T(8,128)(2,1)} %get-tuple-element.115), channel_id=1, source_target_pairs={{0,1},{1,0},{2,3},{3,2},{4,5},{5,4},{6,7},{7,6},{8,9},{9,8},{10,11... | collective-permute-start | bytes 7962632 | tf_op jit(solution)/shard_map/ppermute | solution.py:32
  180.5 7.9 %copy-start.10 = (bf16[1024,192]{1,0:T(8,128)(2,1)S(1)}, bf16[1024,192]{1,0:T(8,128)(2,1)}, u32[]{:S(2)}) copy-start(bf16[1024,192]{1,0:T(8,128)(2,1)} %get-tuple-element.101.mixed_ref) | copy-start | bytes 1179652
  180.5 7.9 %copy-start.12 = (bf16[1024,192]{1,0:T(8,128)(2,1)S(1)}, bf16[1024,192]{1,0:T(8,128)(2,1)}, u32[]{:S(2)}) copy-start(bf16[1024,192]{1,0:T(8,128)(2,1)} %get-tuple-element.100.mixed_ref) | copy-start | bytes 1179652
  180.5 7.9 %copy-start.14 = (bf16[1024,192]{1,0:T(8,128)(2,1)S(1)}, bf16[1024,192]{1,0:T(8,128)(2,1)}, u32[]{:S(2)}) copy-start(bf16[1024,192]{1,0:T(8,128)(2,1)} %get-tuple-element.103.mixed_ref) | copy-start | bytes 1179652
  184.9 41.7 %collective-permute-start.21 = (bf16[4,648,128]{2,1,0:T(8,128)(2,1)}, bf16[4,648,128]{2,1,0:T(8,128)(2,1)S(1)}, u32[]{:S(2)}, u32[]{:S(2)}) collective-permute-start(bf16[4,648,128]{2,1,0:T(8,128)(2,1)} %get-tuple-element.122), channel_id=1, source_target_pairs={{0,2},{1,3},{2,0},{3,1},{4,6},{5,7},{6,4},{7,5},{8,10},{9,11},{10,... | collective-permute-start | bytes 1990664 | tf_op jit(solution)/shard_map/ppermute | solution.py:32
  186.0 40.6 %collective-permute-start.22 = (bf16[4,648,128]{2,1,0:T(8,128)(2,1)}, bf16[4,648,128]{2,1,0:T(8,128)(2,1)S(1)}, u32[]{:S(2)}, u32[]{:S(2)}) collective-permute-start(bf16[4,648,128]{2,1,0:T(8,128)(2,1)} %get-tuple-element.123), channel_id=1, source_target_pairs={{0,4},{1,5},{2,6},{3,7},{4,0},{5,1},{6,2},{7,3},{8,12},{9,13},{10,... | collective-permute-start | bytes 1990664 | tf_op jit(solution)/shard_map/ppermute | solution.py:32
  186.9 39.7 %collective-permute-start.23 = (bf16[4,648,128]{2,1,0:T(8,128)(2,1)}, bf16[4,648,128]{2,1,0:T(8,128)(2,1)}, u32[]{:S(2)}, u32[]{:S(2)}) collective-permute-start(bf16[4,648,128]{2,1,0:T(8,128)(2,1)} %get-tuple-element.124), channel_id=1, source_target_pairs={{0,6},{1,7},{2,4},{3,5},{4,2},{5,3},{6,0},{7,1},{8,14},{9,15},{10,... | collective-permute-start | bytes 1990664 | tf_op jit(solution)/shard_map/ppermute | solution.py:32
  225.1 3.7 %copy-start.3 = (f32[9,576,128]{2,1,0:T(8,128)S(1)}, f32[9,576,128]{2,1,0:T(8,128)}, u32[]{:S(2)}) copy-start(f32[9,576,128]{2,1,0:T(8,128)} %get-tuple-element.134) | copy-start | bytes 7962628
  236.1 10.9 %collective-permute-start.24 = (bf16[16,232,128]{2,1,0:T(8,128)(2,1)}, bf16[16,232,128]{2,1,0:T(8,128)(2,1)S(1)}, u32[]{:S(2)}, u32[]{:S(2)}) collective-permute-start(bf16[16,232,128]{2,1,0:T(8,128)(2,1)} %get-tuple-element.140), channel_id=1, source_target_pairs={{0,1},{1,0},{2,3},{3,2},{4,5},{5,4},{6,7},{7,6},{8,9},{9,8},{10,11... | collective-permute-start | bytes 2850824 | tf_op jit(solution)/shard_map/ppermute | solution.py:32
  241.2 5.8 %copy-start.7 = (bf16[16,232,128]{2,1,0:T(8,128)(2,1)S(1)}, bf16[16,232,128]{2,1,0:T(8,128)(2,1)}, u32[]{:S(2)}) copy-start(bf16[16,232,128]{2,1,0:T(8,128)(2,1)} %get-tuple-element.139) | copy-start | bytes 2850820
  242.7 23.4 %copy-start.4 = (bf16[1024,576]{1,0:T(8,128)(2,1)S(1)}, bf16[1024,576]{1,0:T(8,128)(2,1)}, u32[]{:S(2)}) copy-start(bf16[1024,576]{1,0:T(8,128)(2,1)} %get-tuple-element.177) | copy-start | bytes 3538948
  242.7 9.3 %collective-permute-start.31 = (bf16[648,128]{1,0:T(8,128)(2,1)}, bf16[648,128]{1,0:T(8,128)(2,1)S(1)}, u32[]{:S(2)}, u32[]{:S(2)}) collective-permute-start(bf16[648,128]{1,0:T(8,128)(2,1)} %get-tuple-element.153), channel_id=1, source_target_pairs={{0,8},{1,9},{2,10},{3,11},{4,12},{5,13},{6,14},{7,15},{8,0},{9,1},... | collective-permute-start | bytes 497672 | tf_op jit(solution)/shard_map/ppermute | solution.py:32
  242.7 15.3 %collective-permute-start.32 = (bf16[648,128]{1,0:T(8,128)(2,1)}, bf16[648,128]{1,0:T(8,128)(2,1)S(1)}, u32[]{:S(2)}, u32[]{:S(2)}) collective-permute-start(bf16[648,128]{1,0:T(8,128)(2,1)} %get-tuple-element.154), channel_id=1, source_target_pairs={{0,16},{1,17},{2,18},{3,19},{4,20},{5,21},{6,22},{7,23},{8,24},{9,... | collective-permute-start | bytes 497672 | tf_op jit(solution)/shard_map/ppermute | solution.py:32
  244.7 13.3 %collective-permute-start.33 = (bf16[648,128]{1,0:T(8,128)(2,1)S(1)}, bf16[648,128]{1,0:T(8,128)(2,1)S(1)}, u32[]{:S(2)}, u32[]{:S(2)}) collective-permute-start(bf16[648,128]{1,0:T(8,128)(2,1)S(1)} %get-tuple-element.155), channel_id=1, source_target_pairs={{0,24},{1,25},{2,26},{3,27},{4,28},{5,29},{6,30},{7,31},{8,16},{9,... | collective-permute-start | bytes 497672 | tf_op jit(solution)/shard_map/ppermute | solution.py:32
  247.3 10.7 %collective-permute-start.25 = (bf16[4,232,128]{2,1,0:T(8,128)(2,1)S(1)}, bf16[4,232,128]{2,1,0:T(8,128)(2,1)S(1)}, u32[]{:S(2)}, u32[]{:S(2)}) collective-permute-start(bf16[4,232,128]{2,1,0:T(8,128)(2,1)S(1)} %get-tuple-element.143), channel_id=1, source_target_pairs={{0,2},{1,3},{2,0},{3,1},{4,6},{5,7},{6,4},{7,5},{8,10},{9,11},{10,... | collective-permute-start | bytes 712712 | tf_op jit(solution)/shard_map/ppermute | solution.py:32
  248.5 9.6 %collective-permute-start.26 = (bf16[4,232,128]{2,1,0:T(8,128)(2,1)S(1)}, bf16[4,232,128]{2,1,0:T(8,128)(2,1)S(1)}, u32[]{:S(2)}, u32[]{:S(2)}) collective-permute-start(bf16[4,232,128]{2,1,0:T(8,128)(2,1)S(1)} %get-tuple-element.144), channel_id=1, source_target_pairs={{0,4},{1,5},{2,6},{3,7},{4,0},{5,1},{6,2},{7,3},{8,12},{9,13},{10,... | collective-permute-start | bytes 712712 | tf_op jit(solution)/shard_map/ppermute | solution.py:32
  252.0 8.8 %collective-permute-start.27 = (bf16[4,232,128]{2,1,0:T(8,128)(2,1)S(1)}, bf16[4,232,128]{2,1,0:T(8,128)(2,1)S(1)}, u32[]{:S(2)}, u32[]{:S(2)}) collective-permute-start(bf16[4,232,128]{2,1,0:T(8,128)(2,1)S(1)} %get-tuple-element.145), channel_id=1, source_target_pairs={{0,6},{1,7},{2,4},{3,5},{4,2},{5,3},{6,0},{7,1},{8,14},{9,15},{10,... | collective-permute-start | bytes 712712 | tf_op jit(solution)/shard_map/ppermute | solution.py:32
  260.9 6.6 %collective-permute-start.28 = (bf16[232,128]{1,0:T(8,128)(2,1)S(1)}, bf16[232,128]{1,0:T(8,128)(2,1)S(1)}, u32[]{:S(2)}, u32[]{:S(2)}) collective-permute-start(bf16[232,128]{1,0:T(8,128)(2,1)S(1)} %get-tuple-element.149), channel_id=1, source_target_pairs={{0,8},{1,9},{2,10},{3,11},{4,12},{5,13},{6,14},{7,15},{8,0},{9,1},... | collective-permute-start | bytes 178184 | tf_op jit(solution)/shard_map/ppermute | solution.py:32
  262.0 7.4 %collective-permute-start.29 = (bf16[232,128]{1,0:T(8,128)(2,1)S(1)}, bf16[232,128]{1,0:T(8,128)(2,1)S(1)}, u32[]{:S(2)}, u32[]{:S(2)}) collective-permute-start(bf16[232,128]{1,0:T(8,128)(2,1)S(1)} %get-tuple-element.150), channel_id=1, source_target_pairs={{0,16},{1,17},{2,18},{3,19},{4,20},{5,21},{6,22},{7,23},{8,24},{9,... | collective-permute-start | bytes 178184 | tf_op jit(solution)/shard_map/ppermute | solution.py:32
  263.3 6.1 %collective-permute-start.30 = (bf16[232,128]{1,0:T(8,128)(2,1)S(1)}, bf16[232,128]{1,0:T(8,128)(2,1)S(1)}, u32[]{:S(2)}, u32[]{:S(2)}) collective-permute-start(bf16[232,128]{1,0:T(8,128)(2,1)S(1)} %get-tuple-element.151), channel_id=1, source_target_pairs={{0,24},{1,25},{2,26},{3,27},{4,28},{5,29},{6,30},{7,31},{8,16},{9,... | collective-permute-start | bytes 178184 | tf_op jit(solution)/shard_map/ppermute | solution.py:32
